TPU v7x, 32 devices: a whole 2x2x4 slice. The times are simulated.
32 devices in a mesh: seq: 8 (over y, x, core), ep: 4 (over z).
Axes of the slice: x: 2, y: 2, z: 4, core: 2. Of those that a mesh axis runs over, the one named last changes fastest.
Arguments:
- tokens: bfloat16 [16384, 768], P('seq'), may hold values from -6 to 6
- input_proj: bfloat16 [768, 3, 768], P(None, None, 'ep'), may hold values from -0.21875 to 0.21875
- output_proj: bfloat16 [768, 768], P('ep'), may hold values from -0.21875 to 0.21875
- expert_index: int32 [16384, 1], P(('seq', 'ep')), may hold values from 0 to 31; in each aligned block of 512 rows (0 to 511, 512 to 1023, ...) at most 32 rows name the same one
- expert_in: bfloat16 [64, 768, 1536], P(('seq', 'ep')), may hold values from -0.21875 to 0.21875
- expert_out: bfloat16 [64, 1536, 768], P(('seq', 'ep')), may hold values from -0.109375 to 0.109375
Outputs:
- mixed_out: bfloat16 [16384, 768], P(('seq', 'ep'))
Inputs may be any that keep to these rules, and one draw needn't show every extreme that they name: `expert_index`: among the rows of one device (aligned blocks of 512 rows) no expert is named more than 32 times, a bound that some block reaches.
All inputs are finite; a program needn't handle non-finite values.
Results may differ from a plain program's by a relative error of at most 0.015.
Values may be sent and summed in bfloat16 or wider, within the bound.
No kernel may reach another device: no remote copies, remote signals or barrier semaphores. Data moves between devices by JAX's collectives and lax.ppermute only.
A program may use at most 64 MiB of HBM per device.

v0:
```python
import jax
import jax.numpy as jnp
from jax import lax
from jax.sharding import PartitionSpec as P

HD = 64
EXP_DEV = 2
BLOCK = 512


epsilon = 1e-05


def prefix(x, axis, combine, identity):
    peers, place = (lax.axis_size(axis), lax.axis_index(axis))
    everything = lax.all_gather(x.astype(jnp.bfloat16), axis)
    start = jnp.broadcast_to(jnp.asarray(identity, x.dtype), x.shape)

    def step(k, before):
        reached = k < place
        new = combine(before, everything[k].astype(x.dtype))
        return jnp.where(reached, new, before)

    return lax.fori_loop(0, peers, step, start)


def rms_rows(values):
    return values * lax.rsqrt(jnp.mean(values * values, axis=-1, keepdims=True) + epsilon)


def add_states(earlier, later):
    return earlier + later


def per_device(tokens, input_proj, output_proj, expert_index, expert_in, expert_out):
    seq_rows, model_width = tokens.shape
    local_heads = output_proj.shape[0] // HD
    seq_devices = lax.axis_size("seq")
    ep_devices = lax.axis_size("ep")
    blocks = seq_rows // BLOCK
    normed = rms_rows(tokens.astype(jnp.float32)).astype(jnp.bfloat16)
    flat_proj = input_proj.reshape(model_width, 3 * input_proj.shape[2])
    projected = jnp.dot(normed, flat_proj, preferred_element_type=jnp.float32).astype(jnp.bfloat16)
    projected = projected.reshape(blocks, BLOCK, 3, local_heads, HD)
    queries = projected[:, :, 0]
    key_rows = projected[:, :, 1]
    value_rows = projected[:, :, 2]
    scores = jnp.einsum("bqhd,bkhd->bhqk", queries, key_rows, preferred_element_type=jnp.float32)
    causal = jnp.arange(BLOCK)[:, None] >= jnp.arange(BLOCK)[None, :]
    weights = jnp.where(causal[None, None], scores, 0.0).astype(jnp.bfloat16)
    within = jnp.einsum("bhqk,bkhd->bqhd", weights, value_rows, preferred_element_type=jnp.float32)
    block_states = jnp.einsum(
        "bkhd,bkhe->bhde", key_rows, value_rows, preferred_element_type=jnp.float32
    )
    local_sum = jnp.sum(block_states, axis=0)
    earlier_blocks = jnp.cumsum(block_states, axis=0) - block_states
    device_prefix = prefix(local_sum, "seq", add_states, jnp.zeros_like(local_sum))
    before = device_prefix[None] + earlier_blocks
    across = jnp.einsum(
        "bqhd,bhde->bqhe", queries.astype(jnp.float32), before, precision=lax.Precision.HIGHEST
    )
    heads_out = rms_rows(across + within).astype(jnp.bfloat16).reshape(seq_rows, local_heads * HD)
    row_count = seq_rows // ep_devices
    attn_out = lax.psum_scatter(
        jnp.dot(heads_out, output_proj, preferred_element_type=jnp.float32).astype(jnp.bfloat16),
        "ep",
        scatter_dimension=0,
        tiled=True,
    ).astype(jnp.float32)
    own_rows = lax.dynamic_slice_in_dim(tokens, lax.axis_index("ep") * row_count, row_count, 0)
    stream = (own_rows.astype(jnp.float32) + attn_out).astype(jnp.bfloat16)
    moe_in = rms_rows(stream.astype(jnp.float32)).astype(jnp.bfloat16)
    experts = EXP_DEV * seq_devices * ep_devices // 2
    capacity = max(2, 2 * row_count // experts)
    pair_count = experts // EXP_DEV
    group_slots = EXP_DEV * capacity
    chosen = expert_index[:, 0]
    one_hot = (chosen[:, None] == jnp.arange(experts, dtype=jnp.int32)[None, :]).astype(
        jnp.bfloat16
    )
    strict_lower = (jnp.arange(row_count)[:, None] > jnp.arange(row_count)[None, :]).astype(
        jnp.bfloat16
    )
    preceding = jnp.dot(strict_lower, one_hot, preferred_element_type=jnp.float32)
    slot_rank = jnp.sum(preceding * one_hot.astype(jnp.float32), axis=1).astype(jnp.int32)
    slots = chosen * capacity + slot_rank
    outgoing = jnp.zeros((experts * capacity, model_width), jnp.bfloat16).at[slots].set(moe_in)
    doubled = jnp.repeat(outgoing.reshape(pair_count, group_slots, model_width), 2, axis=0).reshape(
        -1, model_width
    )
    received = lax.all_to_all(doubled, ("seq", "ep"), split_axis=0, concat_axis=0, tiled=True)
    inputs = received.reshape(-1, EXP_DEV, capacity, model_width)
    active = jnp.maximum(
        jnp.einsum("sjcd,jdf->sjcf", inputs, expert_in, preferred_element_type=jnp.float32), 0.0
    ).astype(jnp.bfloat16)
    expert_part = jnp.einsum(
        "sjcf,jfd->sjcd", active, expert_out, preferred_element_type=jnp.float32
    ).astype(jnp.bfloat16)
    expert_part = expert_part.reshape(-1, model_width)
    returned = lax.all_to_all(expert_part, ("seq", "ep"), split_axis=0, concat_axis=0, tiled=True)
    halves = returned.reshape(pair_count, 2, group_slots, model_width)
    moe_part = (
        jnp.sum(halves.astype(jnp.float32), axis=1).astype(jnp.bfloat16).reshape(-1, model_width)
    )
    combined = moe_part[slots]
    return (stream.astype(jnp.float32) + combined.astype(jnp.float32)).astype(jnp.bfloat16)


def solution(mesh):
    return jax.shard_map(
        per_device,
        mesh=mesh,
        in_specs=(
            P("seq", None),
            P(None, None, "ep"),
            P("ep", None),
            P(("seq", "ep"), None),
            P(("seq", "ep"), None, None),
            P(("seq", "ep"), None, None),
        ),
        out_specs=P(("seq", "ep"), None),
        check_vma=False,
    )
```

profile of v0, /device:TPU:0, one launch (start us, length us, event | category | flops | bytes accessed | tf_op | source)
XLA Modules:
  0.0 292.9 jit_solution(1389261581845386023)
XLA Ops:
  6.5 0.8 iota_compare_fusion.1
  7.3 3.1 %fusion = f32[2048]{0:T(1024)S(1)} fusion(bf16[2048,768]{1,0:T(8,128)(2,1)} %param.8), kind=kLoop, calls=%fused_computation.7 | loop fusion | flops 4716544 | bytes 3153920 | tf_op jit(solution)/shard_map/reduce_sum | solution.py:28
  10.4 3.5 %fusion.15 = bf16[2048,576]{0,1:T(8,128)(2,1)} fusion(bf16[768,576]{0,1:T(8,128)(2,1)S(1)} %bitcast.79, bf16[2048,768]{1,0:T(8,128)(2,1)S(1)} %copy-done.1, f32[2048]{0:T(1024)S(1)} %add_rsqrt_fusion.1), kind=kOutput, calls=%fused_computation.23 | convolution fusion | flops 1817837568 | bytes 6397952 | tf_op jit(solution)/shard_map/dot_general | solution.py:43
  14.0 5.1 %reshape.86 = bf16[4,512,3,3,64]{1,0,4,3,2:T(4,128)(2,1)S(1)} reshape(bf16[2048,576]{0,1:T(8,128)(2,1)} %fusion.15) | data formatting | bytes 4718592 | tf_op jit(solution)/shard_map/reshape | solution.py:44
  19.0 1.7 fusion.46
  20.7 0.5 fusion.47
  21.3 0.4 copy-done.3
  21.6 0.3 copy-done.4
  21.9 11.2 %all-gather = bf16[24,64,64]{2,1,0:T(8,128)(2,1)S(1)} all-gather(bf16[3,64,64]{2,1,0:T(8,128)(2,1)S(1)} %get-tuple-element.113), channel_id=2, replica_groups=mesh['seq'=8,'ep'=4] {'seq'}, dimensions={0}, use_global_device_ids=true | all-gather | bytes 221184 | tf_op jit(solution)/shard_map/all_gather | solution.py:16
  33.1 0.4 while.14
  33.5 0.8 fusion.27
  34.3 5.1 %fusion.2 = f32[4,3,64,512]{3,2,1,0:T(8,128)S(1)} fusion(pred[512,512]{1,0:T(8,128)(4,1)} %iota_compare_fusion.1, bf16[4,512,1,3,64]{1,0,4,3,2:T(4,128)(2,1)} %copy-done.4, bf16[4,512,1,3,64]{1,0,4,3,2:T(4,128)(2,1)} %copy-done.3, bf16[4,512,1,3,64]{1,0,4,3,2:T(4,128)(2,1)S(1)} %copy-done.2), kind=kOutput, calls=%fused_computation.9 | convolution fusion | flops 811597824 | bytes 4194304 | tf_op jit(solution)/shard_map/bhqk,bkhd->bqhd/dot_general | solution.py:51
  39.4 2.0 fusion.25
  41.5 0.2 fusion.26
  41.7 0.6 copy.27
  42.3 0.2 copy.36
  42.5 2.7 convolution_convert_fusion
  45.2 0.0 reduce-scatter.2.cloned.1.call-update
  45.2 0.7 copy-done.6
  45.9 0.3 fusion.28
  46.2 59.8 %reduce-scatter.2.cloned.1.call-done = bf16[512,768]{1,0:T(8,128)(2,1)} async-done(((bf16[2048,768]{1,0:T(8,128)(2,1)}), bf16[512,768]{1,0:T(8,128)(2,1)}) %reduce-scatter.2.cloned.1.call-update) | async-done | bytes 786448 | tf_op jit(solution)/shard_map/reduce_scatter | solution.py:64
  106.0 1.7 fusion.22
  107.7 3.1 %scatter_custom_fusion = bf16[1024,768]{1,0:T(8,128)(2,1)S(1)} fusion(s32[512]{0:T(512)S(1)} %bitcast.88, bf16[512,768]{1,0:T(8,128)(2,1)S(1)} %get-tuple-element.109, f32[512]{0:T(512)S(1)} %add_rsqrt_fusion.2, bf16[]{:T(256)} %constant.61.clone.1), kind=kCustom, calls=%fused_computation.42 | custom fusion | flops 1179648 | bytes 2361346 | tf_op jit(solution)/shard_map/scatter | solution.py:87
  110.8 0.4 broadcast_in_dim.22
  111.3 74.5 %all_to_all.18 = bf16[32,64,768]{2,1,0:T(8,128)(2,1)} all-to-all(bf16[32,64,768]{2,1,0:T(8,128)(2,1)S(1)} %bitcast.82), channel_id=1, replica_groups=mesh['seq'=8,'ep'=4] {'seq','ep'}, dimensions={0} | all-to-all | bytes 6291456 | tf_op jit(solution)/shard_map/all_to_all | solution.py:91
  185.8 14.4 %convert_bitcast_fusion = bf16[32,2,32,768]{3,2,0,1:T(8,128)(2,1)} fusion(bf16[2,1536,768]{2,1,0:T(8,128)(2,1)} %param.13, bf16[2,768,1536]{2,1,0:T(8,128)(2,1)} %param.12, bf16[32,2,32,768]{3,2,1,0:T(8,128)(2,1)} %bitcast.85), kind=kOutput, calls=%fused_computation.21 | convolution fusion | flops 9671540736 | bytes 15728640 | tf_op jit(solution)/shard_map/sjcf,jfd->sjcd/dot_general | solution.py:96
  200.1 3.9 %copy.29 = bf16[32,2,32,768]{3,2,1,0:T(8,128)(2,1)} copy(bf16[32,2,32,768]{3,2,0,1:T(8,128)(2,1)} %convert_bitcast_fusion) | data formatting | bytes 6291456 | tf_op jit(solution)/shard_map/convert_element_type | solution.py:98
  204.0 4.6 %all-to-all-start.1 = ((bf16[32,64,768]{2,1,0:T(8,128)(2,1)}), bf16[32,64,768]{2,1,0:T(8,128)(2,1)}, u32[]{:S(2)}, u32[]{:S(2)}) async-start(bf16[32,64,768]{2,1,0:T(8,128)(2,1)} %bitcast.81), calls=%async_computation.2 | async-start | bytes 6291456 | tf_op jit(solution)/shard_map/all_to_all | solution.py:100
  208.6 70.1 %all-to-all-done.1 = bf16[32,64,768]{2,1,0:T(8,128)(2,1)} async-done(((bf16[32,64,768]{2,1,0:T(8,128)(2,1)}), bf16[32,64,768]{2,1,0:T(8,128)(2,1)}, u32[]{:S(2)}, u32[]{:S(2)}) %all-to-all-start.1) | async-done | bytes 3145760 | tf_op jit(solution)/shard_map/all_to_all | solution.py:100
  278.7 2.4 bitcast_reduce_fusion
  281.1 2.7 gather_fusion
  283.8 2.2 fusion.24
  (27 shorter events, 0.3 us)
Async XLA Ops:
  6.5 3.9 %copy-start = (bf16[768,3,192]{0,2,1:T(8,128)(2,1)S(1)}, bf16[768,3,192]{0,2,1:T(8,128)(2,1)}, u32[]{:S(2)}) copy-start(bf16[768,3,192]{0,2,1:T(8,128)(2,1)} %param.9) | copy-start | bytes 2654212
  6.5 99.4 %reduce-scatter.2.cloned.1.call-start = ((), (), s32[]{:S(2)}) async-start(), calls=%async_computation.3 | async-start | bytes 3932160 | tf_op jit(solution)/shard_map/reduce_scatter | solution.py:64
  6.5 3.9 %copy-start.1 = (bf16[2048,768]{1,0:T(8,128)(2,1)S(1)}, bf16[2048,768]{1,0:T(8,128)(2,1)}, u32[]{:S(2)}) copy-start(bf16[2048,768]{1,0:T(8,128)(2,1)} %param.8) | copy-start | bytes 9437188
  20.7 0.9 copy-start.3
  20.7 1.2 copy-start.4
  20.7 13.6 %copy-start.2 = (bf16[4,512,1,3,64]{1,0,4,3,2:T(4,128)(2,1)S(1)}, bf16[4,512,1,3,64]{1,0,4,3,2:T(4,128)(2,1)}, u32[]{:S(2)}) copy-start(bf16[4,512,1,3,64]{1,0,4,3,2:T(4,128)(2,1)} %get-tuple-element.110) | copy-start | bytes 2359300
  41.4 1.1 copy-start.5
  45.2 0.7 copy-start.6
  204.0 74.7 %all-to-all-start.1 = ((bf16[32,64,768]{2,1,0:T(8,128)(2,1)}), bf16[32,64,768]{2,1,0:T(8,128)(2,1)}, u32[]{:S(2)}, u32[]{:S(2)}) async-start(bf16[32,64,768]{2,1,0:T(8,128)(2,1)} %bitcast.81), calls=%async_computation.2 | async-start | bytes 6291456 | tf_op jit(solution)/shard_map/all_to_all | solution.py:100
Sparse Core Ops, SparseCore 0:
  45.4 60.5 reduce-scatter.1
where the time goes:
time: 294 us; the launch traced here: 293 us
  waiting for transfers between devices  130 us (44%)
  blocking collectives  85.7 us (29%)
  matrix products  28.5 us (10%)
  local copies, waits for them, and re-layouts  15.8 us (5%)
  other arithmetic  14.5 us (5%)
  between operations  13.6 us (5%)
  starting transfers between devices  4.57 us (2%)
    all_to_all x1, blocking collectives, per_device(): lax.all_to_all(doubled, ('seq', 'ep'), split_axis=0, concat_axis=0, tiled...  74.5 us
    all_to_all x1, waiting for transfers between devices, per_device(): lax.all_to_all(expert_part, ('seq', 'ep'), split_axis=0, concat_axis=0, t...  70.1 us
    reduce_scatter x1, waiting for transfers between devices, per_device(): lax.psum_scatter(jnp.dot(heads_out, output_proj, preferred_element_type=j...  59.8 us
    dot_general x1, matrix products, per_device(): jnp.einsum('sjcf,jfd->sjcd', active, expert_out, preferred_element_type=j...  14.4 us
    all_gather x1, blocking collectives, prefix(): everything = lax.all_gather(x.astype(jnp.bfloat16), axis)  11.2 us
  transfers between devices with their start and end apart: 2, of which 2 were waited for; matrix products, arithmetic and copies ran while one was open for 0% of the time, Pallas kernels for 0%

commit v1 on v0

v1 whole, which is shorter than its diff:
```python
import jax
import jax.numpy as jnp
from jax import lax
from jax.experimental import pallas as pl
from jax.experimental.pallas import tpu as pltpu
from jax.sharding import PartitionSpec as P

HD = 64
EXP_DEV = 2
BLOCK = 512
CHUNK = 256
SPLIT = 8
EPS = 1e-05
VMEM_BYTES = 48 * 1024 * 1024

F32 = jnp.float32
BF16 = jnp.bfloat16


def xor_pairs(count, bits):
    return [(place, place ^ bits) for place in range(count)]


def dot_nt(a, b):
    return lax.dot_general(a, b, (((1,), (1,)), ((), ())), preferred_element_type=F32)


def dot_tn(a, b):
    return lax.dot_general(a, b, (((0,), (0,)), ((), ())), preferred_element_type=F32)


def dot_nn(a, b):
    return jnp.dot(a, b, preferred_element_type=F32)


def two_terms(x):
    high = x.astype(BF16)
    return high, (x - high.astype(F32)).astype(BF16)


def rms(values):
    return values * lax.rsqrt(jnp.mean(values * values, axis=-1, keepdims=True) + EPS)


def same_head(width):
    rows = lax.broadcasted_iota(jnp.int32, (width, width), 0) // HD
    cols = lax.broadcasted_iota(jnp.int32, (width, width), 1) // HD
    return rows == cols


def params(semantics=1):
    return pltpu.CompilerParams(vmem_limit_bytes=VMEM_BYTES)


def cost(flops, nbytes):
    return pl.CostEstimate(flops=flops, bytes_accessed=nbytes, transcendentals=0)


def norm_states(tokens, stacked, width):
    rows, model = tokens.shape

    def kernel(tok_ref, w_ref, normed_ref, sum_ref, state):
        step = pl.program_id(0)

        @pl.when(step == 0)
        def _():
            state[...] = jnp.zeros_like(state)

        normed = rms(tok_ref[...].astype(F32)).astype(BF16)
        normed_ref[...] = normed
        keys = dot_nt(normed, w_ref[width : 2 * width, :]).astype(BF16)
        values = dot_nt(normed, w_ref[2 * width : 3 * width, :]).astype(BF16)
        state[...] += dot_tn(keys, values)

        @pl.when(step == pl.num_programs(0) - 1)
        def _():
            kept = jnp.where(same_head(width), state[...], 0.0)
            total = kept[:HD]
            for head in range(1, width // HD):
                total = total + kept[head * HD : (head + 1) * HD]
            sum_ref[...] = total.astype(BF16)

    return pl.pallas_call(
        kernel,
        grid=(rows // BLOCK,),
        in_specs=[
            pl.BlockSpec((BLOCK, model), lambda i: (i, 0)),
            pl.BlockSpec(stacked.shape, lambda i: (0, 0)),
        ],
        out_specs=[
            pl.BlockSpec((BLOCK, model), lambda i: (i, 0)),
            pl.BlockSpec((HD, width), lambda i: (0, 0)),
        ],
        out_shape=[
            jax.ShapeDtypeStruct((rows, model), BF16),
            jax.ShapeDtypeStruct((HD, width), BF16),
        ],
        scratch_shapes=[pltpu.VMEM((width, width), F32)],
        compiler_params=params(),
        cost_estimate=cost(2 * rows * model * 2 * width, 8 << 20),
    )(tokens, stacked)


def attend(meta, normed, pieces, prior, width):
    rows, model = normed.shape
    whole = len(pieces) == 1

    def kernel(meta_ref, normed_ref, *refs):
        piece_refs, prior_ref, out_ref = refs[: len(pieces)], refs[len(pieces)], refs[len(pieces) + 1]
        if whole:
            w_ref, state = piece_refs[0], refs[-1]
        else:
            proj_ref, w_ref, state = refs[-3:]
        step = pl.program_id(0)

        @pl.when(step == 0)
        def _():
            spread = jnp.concatenate([prior_ref[...].astype(F32)] * (width // HD), axis=0)
            state[...] = jnp.where(same_head(width), spread, 0.0)
            if not whole:
                part = pieces[0].shape[1]
                for parity in range(2):
                    for i in range(pieces[0].shape[0]):
                        place = (meta_ref[0] % SPLIT) ^ (2 * i + parity)
                        at = pl.ds(pl.multiple_of(place * part, part), part)
                        w_ref[at, :] = piece_refs[parity][i]
                proj_ref[...] = w_ref[3 * width : 4 * width, :]

        normed = normed_ref[...]
        queries = dot_nt(normed, w_ref[0:width, :]).astype(BF16)
        keys = dot_nt(normed, w_ref[width : 2 * width, :]).astype(BF16)
        values = dot_nt(normed, w_ref[2 * width : 3 * width, :]).astype(BF16)
        head_of = lax.broadcasted_iota(jnp.int32, (CHUNK, width), 1) // HD
        causal = lax.broadcasted_iota(jnp.int32, (CHUNK, CHUNK), 0) >= lax.broadcasted_iota(
            jnp.int32, (CHUNK, CHUNK), 1
        )
        heads_same = same_head(width)
        averaging = jnp.where(heads_same, 1.0 / HD, 0.0).astype(BF16)
        zero = jnp.zeros((), BF16)
        for c in range(BLOCK // CHUNK):
            q = queries[c * CHUNK : (c + 1) * CHUNK]
            k = keys[c * CHUNK : (c + 1) * CHUNK]
            v = values[c * CHUNK : (c + 1) * CHUNK]
            high, low = two_terms(state[...])
            attended = dot_nn(q, high) + dot_nn(q, low)
            for h in range(width // HD):
                scores = dot_nt(jnp.where(head_of == h, q, zero), k)
                weights = jnp.where(causal, scores, 0.0).astype(BF16)
                attended = attended + dot_nn(weights, jnp.where(head_of == h, v, zero))
            state[...] += jnp.where(heads_same, dot_tn(k, v), 0.0)
            high, low = two_terms(attended * attended)
            mean = dot_nn(high, averaging) + dot_nn(low, averaging)
            out_ref[c * CHUNK : (c + 1) * CHUNK, :] = (attended * lax.rsqrt(mean + EPS)).astype(BF16)

    def fixed(shape):
        return pl.BlockSpec(shape, lambda i, m: (0,) * len(shape))

    out_specs = [pl.BlockSpec((BLOCK, width), lambda i, m: (i, 0))]
    out_shape = [jax.ShapeDtypeStruct((rows, width), BF16)]
    scratch = [pltpu.VMEM((width, width), F32)]
    if not whole:
        out_specs.append(fixed((width, model)))
        out_shape.append(jax.ShapeDtypeStruct((width, model), BF16))
        scratch.insert(0, pltpu.VMEM((4 * width, model), BF16))
    return pl.pallas_call(
        kernel,
        grid_spec=pltpu.PrefetchScalarGridSpec(
            num_scalar_prefetch=1,
            grid=(rows // BLOCK,),
            in_specs=[pl.BlockSpec((BLOCK, model), lambda i, m: (i, 0))]
            + [fixed(p.shape) for p in pieces]
            + [fixed((HD, width))],
            out_specs=out_specs,
            scratch_shapes=scratch,
        ),
        out_shape=out_shape,
        compiler_params=params(),
        cost_estimate=cost(6 * rows * model * width, 6 << 20),
    )(meta, normed, *pieces, prior)


def slot_rows(chosen, experts, capacity):
    rows = chosen.shape[1]
    hot = chosen == lax.broadcasted_iota(jnp.int32, (experts, rows), 0)
    before = lax.broadcasted_iota(jnp.int32, (rows, rows), 0) < lax.broadcasted_iota(
        jnp.int32, (rows, rows), 1
    )
    preceding = dot_nn(hot.astype(BF16), before.astype(BF16))
    rank = jnp.sum(jnp.where(hot, preceding, 0.0), axis=0, keepdims=True)
    return chosen * capacity + rank.astype(jnp.int32)


def slot_cols(chosen, experts, capacity):
    rows = chosen.shape[0]
    hot = chosen == lax.broadcasted_iota(jnp.int32, (rows, experts), 1)
    before = lax.broadcasted_iota(jnp.int32, (rows, rows), 0) > lax.broadcasted_iota(
        jnp.int32, (rows, rows), 1
    )
    preceding = dot_nn(before.astype(BF16), hot.astype(BF16))
    rank = jnp.sum(jnp.where(hot, preceding, 0.0), axis=1, keepdims=True)
    return chosen * capacity + rank.astype(jnp.int32)


def pick(slots_row, moe_in, seq, ep, local, n_seq, n_ep, capacity):
    wanted = n_seq * capacity
    row = lax.broadcasted_iota(jnp.int32, (wanted, 1), 0)
    pair = ((row // capacity) ^ seq) * (n_ep // 2) + ep // 2
    key = (pair * EXP_DEV + local) * capacity + row % capacity
    hot = (key == slots_row).astype(BF16)
    return dot_nn(hot, moe_in).astype(BF16)


def route_first(meta, tokens, heads, projections, chosen, n_seq, n_ep, capacity, experts):
    rows, model = tokens.shape
    width = heads[0].shape[1]
    blocks = rows // BLOCK

    def kernel(meta_ref, tok_ref, idx_ref, *refs):
        head_refs, proj_refs = refs[:n_ep], refs[n_ep : 2 * n_ep]
        stream_ref, moe_ref, key_ref = refs[2 * n_ep : 2 * n_ep + 3]
        out_refs = refs[2 * n_ep + 3 :]
        total = tok_ref[...].astype(F32)
        for h_ref, p_ref in zip(head_refs, proj_refs):
            total = total + dot_nn(h_ref[...], p_ref[...])
        stream = total.astype(BF16)
        moe_in = rms(stream.astype(F32)).astype(BF16)
        moe_ref[0] = moe_in
        keys = slot_rows(idx_ref[0], experts, capacity)
        key_ref[0] = keys

        @pl.when(pl.program_id(0) == 0)
        def _():
            stream_ref[...] = stream

        picked = pick(keys, moe_in, meta_ref[0], meta_ref[1], 0, n_seq, n_ep, capacity)
        for k, out_ref in enumerate(out_refs):
            out_ref[0] = picked[k * capacity : (k + 1) * capacity]

    def fixed(shape):
        return pl.BlockSpec(shape, lambda i, m: (0,) * len(shape))

    at_block = lambda i, m: (i ^ m[1], 0)
    return pl.pallas_call(
        kernel,
        grid_spec=pltpu.PrefetchScalarGridSpec(
            num_scalar_prefetch=1,
            grid=(blocks,),
            in_specs=[
                pl.BlockSpec((BLOCK, model), at_block),
                pl.BlockSpec((1, 1, BLOCK), lambda i, m: (i ^ m[1], 0, 0)),
            ]
            + [pl.BlockSpec((BLOCK, width), at_block) for _ in heads]
            + [fixed(p.shape) for p in projections],
            out_specs=[
                fixed((BLOCK, model)),
                pl.BlockSpec((1, BLOCK, model), lambda i, m: (i, 0, 0)),
                pl.BlockSpec((1, 1, BLOCK), lambda i, m: (i, 0, 0)),
            ]
            + [pl.BlockSpec((1, capacity, model), lambda i, m: (i, 0, 0)) for _ in range(n_seq)],
        ),
        out_shape=[
            jax.ShapeDtypeStruct((BLOCK, model), BF16),
            jax.ShapeDtypeStruct((blocks, BLOCK, model), BF16),
            jax.ShapeDtypeStruct((blocks, 1, BLOCK), jnp.int32),
        ]
        + [jax.ShapeDtypeStruct((blocks, capacity, model), BF16) for _ in range(n_seq)],
        compiler_params=params(),
        cost_estimate=cost(2 * rows * model * model, 12 << 20),
    )(meta, tokens, chosen, *heads, *projections)


def route_next(meta, moe_in, keys, local, n_seq, n_ep, capacity):
    blocks, rows, model = moe_in.shape

    def kernel(meta_ref, moe_ref, key_ref, *out_refs):
        picked = pick(key_ref[0], moe_ref[0], meta_ref[0], meta_ref[1], local, n_seq, n_ep, capacity)
        for k, out_ref in enumerate(out_refs):
            out_ref[0] = picked[k * capacity : (k + 1) * capacity]

    return pl.pallas_call(
        kernel,
        grid_spec=pltpu.PrefetchScalarGridSpec(
            num_scalar_prefetch=1,
            grid=(blocks,),
            in_specs=[
                pl.BlockSpec((1, rows, model), lambda i, m: (i, 0, 0)),
                pl.BlockSpec((1, 1, rows), lambda i, m: (i, 0, 0)),
            ],
            out_specs=[pl.BlockSpec((1, capacity, model), lambda i, m: (i, 0, 0)) for _ in range(n_seq)],
        ),
        out_shape=[jax.ShapeDtypeStruct((blocks, capacity, model), BF16) for _ in range(n_seq)],
        compiler_params=params(),
        cost_estimate=cost(blocks * n_seq * capacity * rows * model * 2, 5 << 20),
    )(meta, moe_in, keys)


def expert(arrived, expert_in, expert_out, local):
    blocks, capacity, model = arrived[0].shape
    count = len(arrived)
    rows = blocks * count * capacity
    hidden = expert_in.shape[2]
    tile = 512
    steps = hidden // tile

    def kernel(*refs):
        in_refs, (w1, w2), out_refs, (held, total) = (
            refs[:count],
            refs[count : count + 2],
            refs[count + 2 : count + 2 + blocks],
            refs[count + 2 + blocks :],
        )
        step = pl.program_id(0)

        @pl.when(step == 0)
        def _():
            for k, ref in enumerate(in_refs):
                for m in range(blocks):
                    at = (m * count + k) * capacity
                    held[at : at + capacity, :] = ref[m]

        active = jnp.maximum(dot_nn(held[...], w1[0]), 0.0).astype(BF16)
        term = dot_nn(active, w2[0])

        @pl.when(step == 0)
        def _():
            total[...] = term

        @pl.when(step > 0)
        def _():
            total[...] += term

        @pl.when(step == steps - 1)
        def _():
            span = count * capacity
            for m, ref in enumerate(out_refs):
                ref[...] = total[m * span : (m + 1) * span, :].astype(BF16)

    return pl.pallas_call(
        kernel,
        grid=(steps,),
        in_specs=[pl.BlockSpec(a.shape, lambda f: (0, 0, 0)) for a in arrived]
        + [
            pl.BlockSpec((1, model, tile), lambda f: (local, 0, f)),
            pl.BlockSpec((1, tile, model), lambda f: (local, f, 0)),
        ],
        out_specs=[pl.BlockSpec((count * capacity, model), lambda f: (0, 0)) for _ in range(blocks)],
        out_shape=[jax.ShapeDtypeStruct((count * capacity, model), BF16) for _ in range(blocks)],
        scratch_shapes=[pltpu.VMEM((rows, model), BF16), pltpu.VMEM((rows, model), F32)],
        compiler_params=params(),
        cost_estimate=cost(4 * rows * model * hidden, 9 << 20),
    )(*arrived, expert_in, expert_out)


def add_halves(parts, n_seq, capacity):
    model = parts[0].shape[1]
    pairs = len(parts) // 2

    def kernel(*refs):
        in_refs, out_refs = refs[: len(parts)], refs[len(parts) :]
        for i in range(pairs):
            both = in_refs[2 * i][...].astype(F32) + in_refs[2 * i + 1][...].astype(F32)
            both = both.astype(BF16)
            for k in range(n_seq):
                out_refs[k][i * capacity : (i + 1) * capacity, :] = both[k * capacity : (k + 1) * capacity]

    return pl.pallas_call(
        kernel,
        out_shape=[jax.ShapeDtypeStruct((pairs * capacity, model), BF16) for _ in range(n_seq)],
        compiler_params=params(),
        cost_estimate=cost(1 << 20, 3 << 20),
    )(*parts)


def combine(meta, stream, chosen, returned, n_seq, n_ep, capacity, experts):
    rows, model = stream.shape
    pairs = n_ep // 2

    def kernel(meta_ref, stream_ref, idx_ref, *refs):
        out_ref = refs[-1]
        keys = slot_cols(idx_ref[...], experts, capacity)
        total = stream_ref[...].astype(F32)
        span = pairs * capacity
        col = lax.broadcasted_iota(jnp.int32, (1, n_seq * span), 1)
        seq = (col // span) ^ meta_ref[0]
        pair = seq * pairs + (((col // capacity) % pairs) ^ (meta_ref[1] // 2))
        for local in range(EXP_DEV):
            key = (pair * EXP_DEV + local) * capacity + col % capacity
            hot = (keys == key).astype(BF16)
            block = jnp.concatenate([r[...] for r in refs[local * n_seq : (local + 1) * n_seq]], axis=0)
            total = total + dot_nn(hot, block)
        out_ref[...] = total.astype(BF16)

    flat = [r for group in returned for r in group]
    return pl.pallas_call(
        kernel,
        in_specs=[pl.BlockSpec(memory_space=pltpu.SMEM)]
        + [pl.BlockSpec(memory_space=pltpu.VMEM)] * (2 + len(flat)),
        out_shape=jax.ShapeDtypeStruct((rows, model), BF16),
        compiler_params=params(),
        cost_estimate=cost(4 * rows * rows * model, 4 << 20),
    )(meta, stream, chosen, *flat)


def per_device(tokens, input_proj, output_proj, expert_index, expert_in, expert_out):
    rows, model = tokens.shape
    width = output_proj.shape[0]
    n_seq, n_ep = lax.axis_size("seq"), lax.axis_size("ep")
    seq, ep = lax.axis_index("seq"), lax.axis_index("ep")
    meta = jnp.stack([seq, ep]).astype(jnp.int32)
    own_rows = rows // n_ep
    experts = EXP_DEV * n_seq * n_ep // 2
    capacity = max(2, 2 * own_rows // experts)

    stacked = jnp.concatenate(
        [jnp.transpose(input_proj, (1, 2, 0)).reshape(3 * width, model), output_proj], axis=0
    )
    part = stacked.shape[0] // SPLIT
    piece = lax.dynamic_slice_in_dim(stacked, (seq % SPLIT) * part, part, 0)
    along = [None] + [lax.ppermute(piece, "ep", xor_pairs(n_ep, m)) for m in range(1, n_ep)]
    chosen_all = lax.all_gather(expert_index, "ep").reshape(n_ep, 1, own_rows)

    normed, own_sum = norm_states(tokens, stacked, width)
    sums = lax.all_gather(own_sum, "seq").astype(F32)
    earlier = (jnp.arange(n_seq) < seq).astype(F32)
    prior = jnp.sum(sums * earlier[:, None, None], axis=0).astype(BF16)
    priors = [prior] + [lax.ppermute(prior, "ep", xor_pairs(n_ep, m)) for m in range(1, n_ep)]

    heads, projections = [], []
    for m in range(n_ep):
        if m == 0:
            (out,) = attend(meta, normed, [stacked], priors[0], width)
            projections.append(output_proj)
        else:
            same = [along[m]] + [
                lax.ppermute(along[m], "seq", xor_pairs(n_seq, bits)) for bits in range(2, SPLIT, 2)
            ]
            same = jnp.stack(same)
            other = lax.ppermute(same, "seq", xor_pairs(n_seq, 1))
            out, proj = attend(meta, normed, [same, other], priors[m], width)
            projections.append(proj)
        heads.append(out)

    stream, moe_in, keys, *first = route_first(
        meta, tokens, heads, projections, chosen_all, n_seq, n_ep, capacity, experts
    )
    returned = []
    for local in range(EXP_DEV):
        outgoing = first if local == 0 else route_next(meta, moe_in, keys, local, n_seq, n_ep, capacity)
        arrived = [outgoing[0]] + [
            lax.ppermute(outgoing[k], "seq", xor_pairs(n_seq, k)) for k in range(1, n_seq)
        ]
        made = expert(arrived, expert_in, expert_out, local)
        parts = [made[0]] + [lax.ppermute(made[m], "ep", xor_pairs(n_ep, m)) for m in range(1, n_ep)]
        summed = add_halves(parts, n_seq, capacity)
        returned.append(
            [summed[0]] + [lax.ppermute(summed[k], "seq", xor_pairs(n_seq, k)) for k in range(1, n_seq)]
        )
    return combine(meta, stream, expert_index, returned, n_seq, n_ep, capacity, experts)


def solution(mesh):
    return jax.shard_map(
        per_device,
        mesh=mesh,
        in_specs=(
            P("seq", None),
            P(None, None, "ep"),
            P("ep", None),
            P(("seq", "ep"), None),
            P(("seq", "ep"), None, None),
            P(("seq", "ep"), None, None),
        ),
        out_specs=P(("seq", "ep"), None),
        check_vma=False,
    )
```

time: 294 us -> 249 us (0.85)
  Pallas kernels: 0 us -> 74.7 us
  blocking collectives: 85.7 us -> 24.3 us
  starting transfers between devices: 4.57 us -> 59.8 us
  waiting for transfers between devices: 130 us -> 78.1 us
  matrix products: 28.5 us -> 0 us
  between operations: 13.6 us -> 0.26 us
  other arithmetic: 14.5 us -> 3.67 us
  local copies, waits for them, and re-layouts: 15.8 us -> 7.51 us
    ppermute x0 -> x52, waiting for transfers between devices: none -> 78.1 us  [the longest x6 45 us: per_device(): lax.ppermute(made[m], 'ep', xor_pairs(n_ep, m))]
    pallas_call x0 -> x12, Pallas kernels: none -> 74.7 us  [the longest x4 36.6 us: attend(): pl.pallas_call(kernel, grid_spec=pltpu.PrefetchScalarGridSpec(num_scalar_...]
    all_to_all x1 -> x0, blocking collectives: 74.5 us -> none  [per_device(): lax.all_to_all(doubled, ('seq', 'ep'), split_axis=0, concat_axis=0, tiled...]
    all_to_all x1 -> x0, waiting for transfers between devices: 70.1 us -> none  [per_device(): lax.all_to_all(expert_part, ('seq', 'ep'), split_axis=0, concat_axis=0, t...]
    reduce_scatter x1 -> x0, waiting for transfers between devices: 59.8 us -> none  [per_device(): lax.psum_scatter(jnp.dot(heads_out, output_proj, preferred_element_type=j...]
    ppermute x0 -> x52, starting transfers between devices: none -> 59.8 us  [the longest x14 13.2 us: per_device(): lax.ppermute(summed[k], 'seq', xor_pairs(n_seq, k))]
    dot_general x7 -> x0, matrix products: 28.5 us -> none  [the longest x1 14.4 us: per_device(): jnp.einsum('sjcf,jfd->sjcd', active, expert_out, preferred_element_type=j...]
    all_gather x1 -> x2, blocking collectives: 11.2 us -> 24.3 us  [the longest x1 12.3 us: per_device(): sums = lax.all_gather(own_sum, 'seq').astype(F32)]
  transfers between devices with their start and end apart: 2 -> 52, of which waited for: 2 -> 14; matrix products, arithmetic and copies ran while one was open for 0% -> 1% of each run, Pallas kernels for 0% -> 20%
where the time goes in v1:
time: 249 us; the launch traced here: 248 us
  waiting for transfers between devices  78.1 us (31%)
  Pallas kernels  74.7 us (30%)
  starting transfers between devices  59.8 us (24%)
  blocking collectives  24.3 us (10%)
  local copies, waits for them, and re-layouts  7.51 us (3%)
  other arithmetic  3.67 us (1%)
    ppermute x6, waiting for transfers between devices, per_device(): lax.ppermute(made[m], 'ep', xor_pairs(n_ep, m))  45 us
    pallas_call x4, Pallas kernels, attend(): pl.pallas_call(kernel, grid_spec=pltpu.PrefetchScalarGridSpec(num_scalar_...  36.6 us
    ppermute x14, waiting for transfers between devices, per_device(): lax.ppermute(outgoing[k], 'seq', xor_pairs(n_seq, k))  17.8 us
    pallas_call x2, Pallas kernels, expert(): pl.pallas_call(kernel, grid=(steps,), in_specs=[pl.BlockSpec(a.shape, lam...  16.8 us
    ppermute x14, starting transfers between devices, per_device(): lax.ppermute(summed[k], 'seq', xor_pairs(n_seq, k))  13.2 us
    ppermute x14, starting transfers between devices, per_device(): lax.ppermute(outgoing[k], 'seq', xor_pairs(n_seq, k))  13 us
    all_gather x1, blocking collectives, per_device(): sums = lax.all_gather(own_sum, 'seq').astype(F32)  12.3 us
    all_gather x1, blocking collectives, per_device(): chosen_all = lax.all_gather(expert_index, 'ep').reshape(n_ep, 1, own_rows)  12.1 us
  transfers between devices with their start and end apart: 52, of which 14 were waited for; matrix products, arithmetic and copies ran while one was open for 1% of the time, Pallas kernels for 20%

profile of v1, /device:TPU:0, one launch (start us, length us, event | category | flops | bytes accessed | tf_op | source)
XLA Modules:
  0.0 248.3 jit_solution(13067805272501533188)
XLA Ops:
  1.0 5.1 %collective-permute-start.12 = (bf16[96,768]{1,0:T(8,128)(2,1)S(1)}, bf16[96,768]{1,0:T(8,128)(2,1)S(1)}, u32[]{:S(2)}, u32[]{:S(2)}) collective-permute-start(bf16[96,768]{1,0:T(8,128)(2,1)S(1)} %fusion.1), channel_id=1, source_target_pairs={{0,3},{1,2},{2,1},{3,0},{4,7},{5,6},{6,5},{7,4},{8,11},{9,10},{10,... | collective-permute-start | bytes 442376 | tf_op jit(solution)/shard_map/ppermute | solution.py:419
  8.1 2.8 %collective-permute-done.12 = bf16[96,768]{1,0:T(8,128)(2,1)S(1)} collective-permute-done((bf16[96,768]{1,0:T(8,128)(2,1)S(1)}, bf16[96,768]{1,0:T(8,128)(2,1)S(1)}, u32[]{:S(2)}, u32[]{:S(2)}) %collective-permute-start.12) | collective-permute-done | bytes 147488 | tf_op jit(solution)/shard_map/ppermute | solution.py:419
  12.6 5.1 %shard_map.64 = (bf16[2048,768]{1,0:T(8,128)(2,1)S(1)}, bf16[64,192]{1,0:T(8,128)(2,1)S(1)}) custom-call(bf16[2048,768]{1,0:T(8,128)(2,1)} %tok_ref.3, bf16[768,768]{1,0:T(8,128)(2,1)S(1)} %pad_maximum_fusion.w_ref.refs_0_), custom_call_target="tpu_custom_call" | custom-call | flops 1207959552 | bytes 8388608 | tf_op jit(solution)/shard_map/pallas_call | solution.py:83
  24.6 12.3 %all-gather.1 = bf16[512,192]{1,0:T(8,128)(2,1)S(1)} all-gather(bf16[64,192]{1,0:T(8,128)(2,1)S(1)} %get-tuple-element.57), channel_id=3, replica_groups=mesh['seq'=8,'ep'=4] {'seq'}, dimensions={0}, use_global_device_ids=true | all-gather | bytes 221184 | tf_op jit(solution)/shard_map/all_gather | solution.py:423
  41.3 2.2 collective-permute-done.1
  43.5 3.5 %collective-permute-start.17 = (bf16[64,192]{1,0:T(8,128)(2,1)S(1)}, bf16[64,192]{1,0:T(8,128)(2,1)S(1)}, u32[]{:S(2)}, u32[]{:S(2)}) collective-permute-start(bf16[64,192]{1,0:T(8,128)(2,1)S(1)} %fusion.refs_1_), channel_id=1, source_target_pairs={{0,3},{1,2},{2,1},{3,0},{4,7},{5,6},{6,5},{7,4},{8,11},{9,10},{10,... | collective-permute-start | bytes 73736 | tf_op jit(solution)/shard_map/ppermute | solution.py:426
  47.0 4.8 %collective-permute-start.11 = (bf16[64,192]{1,0:T(8,128)(2,1)S(1)}, bf16[64,192]{1,0:T(8,128)(2,1)S(1)}, u32[]{:S(2)}, u32[]{:S(2)}) collective-permute-start(bf16[64,192]{1,0:T(8,128)(2,1)S(1)} %fusion.refs_1_), channel_id=1, source_target_pairs={{0,2},{1,3},{2,0},{3,1},{4,6},{5,7},{6,4},{7,5},{8,10},{9,11},{10,... | collective-permute-start | bytes 73736 | tf_op jit(solution)/shard_map/ppermute | solution.py:426
  53.0 1.9 copy-done.3
  54.9 8.8 %shard_map.65.refs_0_ = bf16[2048,192]{1,0:T(8,128)(2,1)S(1)} custom-call(s32[2]{0:T(128)S(1)} %pad_add_fusion.meta_ref, bf16[2048,768]{1,0:T(8,128)(2,1)S(1)} %copy-done.3, bf16[768,768]{1,0:T(8,128)(2,1)S(1)} %pad_maximum_fusion.w_ref.refs_0_, bf16[64,192]{1,0:T(8,128)(2,1)S(1)} %fusion.refs_1_), custom_call_target="tpu_custom_call" | custom-call | flops 1811939328 | bytes 6291456 | tf_op jit(solution)/shard_map/pallas_call | solution.py:165
  63.7 12.1 %all-gather = s32[2048,1]{0,1:T(1,128)S(1)} all-gather(s32[512,1]{0,1:T(1,128)S(1)} %copy-done.6), channel_id=2, replica_groups=mesh['seq'=8,'ep'=4] {'ep'}, dimensions={0}, use_global_device_ids=true | all-gather | bytes 10240 | tf_op jit(solution)/shard_map/all_gather | solution.py:420
  75.7 1.8 collective-permute-start.5
  77.5 8.9 %shard_map.68 = (bf16[2048,192]{1,0:T(8,128)(2,1)S(1)}, bf16[192,768]{1,0:T(8,128)(2,1)S(1)}) custom-call(s32[2]{0:T(128)S(1)} %pad_add_fusion.meta_ref, bf16[2048,768]{1,0:T(8,128)(2,1)S(1)} %copy-done.3, bf16[4,96,768]{2,1,0:T(8,128)(2,1)S(1)} %pad_maximum_fusion.3.refs_0_, bf16[4,96,768]{2,1,0:T(8,128)(2,1)S(1)} %collective-permute-done.16.refs_1_, ...), custom_call_target="tpu_custom_call" | custom-call | flops 1811939328 | bytes 6291456 | tf_op jit(solution)/shard_map/pallas_call | solution.py:165
  87.4 10.0 %shard_map.67 = (bf16[2048,192]{1,0:T(8,128)(2,1)S(1)}, bf16[192,768]{1,0:T(8,128)(2,1)S(1)}) custom-call(s32[2]{0:T(128)S(1)} %pad_add_fusion.meta_ref, bf16[2048,768]{1,0:T(8,128)(2,1)S(1)} %copy-done.3, bf16[4,96,768]{2,1,0:T(8,128)(2,1)S(1)} %pad_maximum_fusion.2.refs_0_, bf16[4,96,768]{2,1,0:T(8,128)(2,1)} %collective-permute-done.10.refs_1_, ...), custom_call_target="tpu_custom_call" | custom-call | flops 1811939328 | bytes 6291456 | tf_op jit(solution)/shard_map/pallas_call | solution.py:165
  98.4 8.9 %shard_map.66 = (bf16[2048,192]{1,0:T(8,128)(2,1)S(1)}, bf16[192,768]{1,0:T(8,128)(2,1)S(1)}) custom-call(s32[2]{0:T(128)S(1)} %pad_add_fusion.meta_ref, bf16[2048,768]{1,0:T(8,128)(2,1)S(1)} %copy-done.3, bf16[4,96,768]{2,1,0:T(8,128)(2,1)S(1)} %pad_maximum_fusion.1.refs_0_, bf16[4,96,768]{2,1,0:T(8,128)(2,1)S(1)} %collective-permute-done.4.refs_1_, ...), custom_call_target="tpu_custom_call" | custom-call | flops 1811939328 | bytes 6291456 | tf_op jit(solution)/shard_map/pallas_call | solution.py:165
  107.3 10.5 %shard_map.69 = (bf16[512,768]{1,0:T(8,128)(2,1)S(1)}, bf16[4,512,768]{2,1,0:T(8,128)(2,1)}, s32[4,1,512]{2,1,0:T(1,128)S(1)}, bf16[4,32,768]{2,1,0:T(8,128)(2,1...) custom-call(s32[2]{0:T(128)S(1)} %pad_add_fusion.meta_ref, ...), custom_call_target="tpu_custom_call" | custom-call | flops 2415919104 | bytes 12582912 | tf_op jit(solution)/shard_map/pallas_call | solution.py:243
  117.9 1.9 copy-done
  119.8 2.1 shard_map.72
  127.0 2.7 %collective-permute-done.36.refs_2_ = bf16[4,32,768]{2,1,0:T(8,128)(2,1)S(1)} collective-permute-done((bf16[4,32,768]{2,1,0:T(8,128)(2,1)S(1)}, bf16[4,32,768]{2,1,0:T(8,128)(2,1)S(1)}, u32[]{:S(2)}, u32[]{:S(2)}) %collective-permute-start.36) | collective-permute-done | bytes 196640 | tf_op jit(solution)/shard_map/ppermute | solution.py:450
  130.0 3.0 %collective-permute-done.37.refs_3_ = bf16[4,32,768]{2,1,0:T(8,128)(2,1)S(1)} collective-permute-done((bf16[4,32,768]{2,1,0:T(8,128)(2,1)S(1)}, bf16[4,32,768]{2,1,0:T(8,128)(2,1)S(1)}, u32[]{:S(2)}, u32[]{:S(2)}) %collective-permute-start.37) | collective-permute-done | bytes 196640 | tf_op jit(solution)/shard_map/ppermute | solution.py:450
  135.0 8.0 %collective-permute-done.39.refs_5_ = bf16[4,32,768]{2,1,0:T(8,128)(2,1)S(1)} collective-permute-done((bf16[4,32,768]{2,1,0:T(8,128)(2,1)S(1)}, bf16[4,32,768]{2,1,0:T(8,128)(2,1)S(1)}, u32[]{:S(2)}, u32[]{:S(2)}) %collective-permute-start.39) | collective-permute-done | bytes 196640 | tf_op jit(solution)/shard_map/ppermute | solution.py:450
  148.7 8.3 %shard_map.73 = (bf16[256,768]{1,0:T(8,128)(2,1)S(1)}, bf16[256,768]{1,0:T(8,128)(2,1)S(1)}, bf16[256,768]{1,0:T(8,128)(2,1)S(1)}, bf16[256,768]{1,0:T(8,128)(2,1)S(1)}) custom-call(bf16[4,32,768]{2,1,0:T(8,128)(2,1)S(1)} %get-tuple-element.87.refs_0_, bf16[4,32,768]{2,1,0:T(8,128)(2,1)S(1)} %collective-permute-done.35.refs_1_, ...), custom_call_target="tpu_custom_call" | custom-call | flops 4831838208 | bytes 9437184 | tf_op jit(solution)/shard_map/pallas_call | solution.py:338
  157.3 3.3 %collective-permute-done.21.refs_4_ = bf16[4,32,768]{2,1,0:T(8,128)(2,1)S(1)} collective-permute-done((bf16[4,32,768]{2,1,0:T(8,128)(2,1)S(1)}, bf16[4,32,768]{2,1,0:T(8,128)(2,1)S(1)}, u32[]{:S(2)}, u32[]{:S(2)}) %collective-permute-start.21) | collective-permute-done | bytes 196640 | tf_op jit(solution)/shard_map/ppermute | solution.py:450
  163.1 8.5 %shard_map.70 = (bf16[256,768]{1,0:T(8,128)(2,1)S(1)}, bf16[256,768]{1,0:T(8,128)(2,1)S(1)}, bf16[256,768]{1,0:T(8,128)(2,1)S(1)}, bf16[256,768]{1,0:T(8,128)(2,1)S(1)}) custom-call(bf16[4,32,768]{2,1,0:T(8,128)(2,1)S(1)} %get-tuple-element.65.refs_0_, bf16[4,32,768]{2,1,0:T(8,128)(2,1)S(1)} %collective-permute-done.18.refs_1_, ...), custom_call_target="tpu_custom_call" | custom-call | flops 4831838208 | bytes 9437184 | tf_op jit(solution)/shard_map/pallas_call | solution.py:338
  172.7 2.7 %collective-permute-start.26 = (bf16[256,768]{1,0:T(8,128)(2,1)S(1)}, bf16[256,768]{1,0:T(8,128)(2,1)S(1)}, u32[]{:S(2)}, u32[]{:S(2)}) collective-permute-start(bf16[256,768]{1,0:T(8,128)(2,1)S(1)} %get-tuple-element.75), channel_id=1, source_target_pairs={{0,2},{1,3},{2,0},{3,1},{4,6},{5,7},{6,4},{7,5},{8,10},{9,11},{10,... | collective-permute-start | bytes 1179656 | tf_op jit(solution)/shard_map/ppermute | solution.py:453
  176.1 13.3 %collective-permute-done.43.refs_2_ = bf16[256,768]{1,0:T(8,128)(2,1)S(1)} collective-permute-done((bf16[256,768]{1,0:T(8,128)(2,1)S(1)}, bf16[256,768]{1,0:T(8,128)(2,1)S(1)}, u32[]{:S(2)}, u32[]{:S(2)}) %collective-permute-start.43) | collective-permute-done | bytes 393248 | tf_op jit(solution)/shard_map/ppermute | solution.py:453
  190.7 4.6 %collective-permute-done.25.refs_1_ = bf16[256,768]{1,0:T(8,128)(2,1)S(1)} collective-permute-done((bf16[256,768]{1,0:T(8,128)(2,1)S(1)}, bf16[256,768]{1,0:T(8,128)(2,1)S(1)}, u32[]{:S(2)}, u32[]{:S(2)}) %collective-permute-start.25) | collective-permute-done | bytes 393248 | tf_op jit(solution)/shard_map/ppermute | solution.py:453
  196.0 27.1 %collective-permute-done.26.refs_2_ = bf16[256,768]{1,0:T(8,128)(2,1)S(1)} collective-permute-done((bf16[256,768]{1,0:T(8,128)(2,1)S(1)}, bf16[256,768]{1,0:T(8,128)(2,1)S(1)}, u32[]{:S(2)}, u32[]{:S(2)}) %collective-permute-start.26) | collective-permute-done | bytes 393248 | tf_op jit(solution)/shard_map/ppermute | solution.py:453
  225.8 1.9 collective-permute-start.51
  229.4 3.9 %collective-permute-done.49.refs_13_ = bf16[64,768]{1,0:T(8,128)(2,1)S(1)} collective-permute-done((bf16[64,768]{1,0:T(8,128)(2,1)S(1)}, bf16[64,768]{1,0:T(8,128)(2,1)S(1)}, u32[]{:S(2)}, u32[]{:S(2)}) %collective-permute-start.49) | collective-permute-done | bytes 98336 | tf_op jit(solution)/shard_map/ppermute | solution.py:456
  237.3 1.9 collective-permute-start.34
  240.1 4.9 %collective-permute-done.32.refs_5_ = bf16[64,768]{1,0:T(8,128)(2,1)S(1)} collective-permute-done((bf16[64,768]{1,0:T(8,128)(2,1)S(1)}, bf16[64,768]{1,0:T(8,128)(2,1)S(1)}, u32[]{:S(2)}, u32[]{:S(2)}) %collective-permute-start.32) | collective-permute-done | bytes 98336 | tf_op jit(solution)/shard_map/ppermute | solution.py:456
  245.0 3.3 %shard_map.75 = bf16[512,768]{1,0:T(8,128)(2,1)} custom-call(s32[2]{0:T(128)S(1)} %pad_add_fusion.meta_ref, bf16[512,768]{1,0:T(8,128)(2,1)S(1)} %get-tuple-element.64.stream_ref, s32[512,1]{1,0:T(8,128)S(1)} %copy.7.idx_ref, bf16[64,768]{1,0:T(8,128)(2,1)S(1)} %get-tuple-element.77.refs_0_, bf16[64,768]{1,0:T(8,128)(2,1)S(1)} %collective-permute-done.28.refs_1_, ...), custom_call_target="tpu_custom_call" | custom-call | flops 805306368 | bytes 4194304 | tf_op jit(solution)/shard_map/pallas_call | solution.py:394
  (109 shorter events, 48.1 us)
Async XLA Ops:
  6.1 15.0 %collective-permute-start.6 = (bf16[96,768]{1,0:T(8,128)(2,1)S(1)}, bf16[96,768]{1,0:T(8,128)(2,1)S(1)}, u32[]{:S(2)}, u32[]{:S(2)}) collective-permute-start(bf16[96,768]{1,0:T(8,128)(2,1)S(1)} %fusion.1), channel_id=1, source_target_pairs={{0,2},{1,3},{2,0},{3,1},{4,6},{5,7},{6,4},{7,5},{8,10},{9,11},{10,... | collective-permute-start | bytes 442376 | tf_op jit(solution)/shard_map/ppermute | solution.py:419
  6.1 16.7 %collective-permute-start = (bf16[96,768]{1,0:T(8,128)(2,1)S(1)}, bf16[96,768]{1,0:T(8,128)(2,1)S(1)}, u32[]{:S(2)}, u32[]{:S(2)}) collective-permute-start(bf16[96,768]{1,0:T(8,128)(2,1)S(1)} %fusion.1), channel_id=1, source_target_pairs={{0,1},{1,0},{2,3},{3,2},{4,5},{5,4},{6,7},{7,6},{8,9},{9,8},{10,11... | collective-permute-start | bytes 442376 | tf_op jit(solution)/shard_map/ppermute | solution.py:419
  10.9 13.5 %collective-permute-start.13 = (bf16[96,768]{1,0:T(8,128)(2,1)S(1)}, bf16[96,768]{1,0:T(8,128)(2,1)S(1)}, u32[]{:S(2)}, u32[]{:S(2)}) collective-permute-start(bf16[96,768]{1,0:T(8,128)(2,1)S(1)} %collective-permute-done.12), channel_id=1, source_target_pairs={{0,8},{4,12},{8,0},{12,4},{16,24},{20,28},{24,16},{28,20},{1,9},{5... | collective-permute-start | bytes 442376 | tf_op jit(solution)/shard_map/ppermute | solution.py:435
  19.3 17.6 %collective-permute-start.14 = (bf16[96,768]{1,0:T(8,128)(2,1)S(1)}, bf16[96,768]{1,0:T(8,128)(2,1)S(1)}, u32[]{:S(2)}, u32[]{:S(2)}) collective-permute-start(bf16[96,768]{1,0:T(8,128)(2,1)S(1)} %collective-permute-done.12), channel_id=1, source_target_pairs={{0,16},{4,20},{8,24},{12,28},{16,0},{20,4},{24,8},{28,12},{1,17},{... | collective-permute-start | bytes 442376 | tf_op jit(solution)/shard_map/ppermute | solution.py:435
  20.8 17.1 %collective-permute-start.15 = (bf16[96,768]{1,0:T(8,128)(2,1)S(1)}, bf16[96,768]{1,0:T(8,128)(2,1)S(1)}, u32[]{:S(2)}, u32[]{:S(2)}) collective-permute-start(bf16[96,768]{1,0:T(8,128)(2,1)S(1)} %collective-permute-done.12), channel_id=1, source_target_pairs={{0,24},{4,28},{8,16},{12,20},{16,8},{20,12},{24,0},{28,4},{1,25},{... | collective-permute-start | bytes 442376 | tf_op jit(solution)/shard_map/ppermute | solution.py:435
  21.1 17.9 %collective-permute-start.7 = (bf16[96,768]{1,0:T(8,128)(2,1)S(1)}, bf16[96,768]{1,0:T(8,128)(2,1)S(1)}, u32[]{:S(2)}, u32[]{:S(2)}) collective-permute-start(bf16[96,768]{1,0:T(8,128)(2,1)S(1)} %collective-permute-done.6), channel_id=1, source_target_pairs={{0,8},{4,12},{8,0},{12,4},{16,24},{20,28},{24,16},{28,20},{1,9},{5... | collective-permute-start | bytes 442376 | tf_op jit(solution)/shard_map/ppermute | solution.py:435
  22.8 17.7 %collective-permute-start.8 = (bf16[96,768]{1,0:T(8,128)(2,1)S(1)}, bf16[96,768]{1,0:T(8,128)(2,1)S(1)}, u32[]{:S(2)}, u32[]{:S(2)}) collective-permute-start(bf16[96,768]{1,0:T(8,128)(2,1)S(1)} %collective-permute-done.6), channel_id=1, source_target_pairs={{0,16},{4,20},{8,24},{12,28},{16,0},{20,4},{24,8},{28,12},{1,17},{... | collective-permute-start | bytes 442376 | tf_op jit(solution)/shard_map/ppermute | solution.py:435
  24.3 16.2 %collective-permute-start.9 = (bf16[96,768]{1,0:T(8,128)(2,1)S(1)}, bf16[96,768]{1,0:T(8,128)(2,1)S(1)}, u32[]{:S(2)}, u32[]{:S(2)}) collective-permute-start(bf16[96,768]{1,0:T(8,128)(2,1)S(1)} %collective-permute-done.6), channel_id=1, source_target_pairs={{0,24},{4,28},{8,16},{12,20},{16,8},{20,12},{24,0},{28,4},{1,25},{... | collective-permute-start | bytes 442376 | tf_op jit(solution)/shard_map/ppermute | solution.py:435
  40.5 37.0 %collective-permute-start.16 = (bf16[4,96,768]{2,1,0:T(8,128)(2,1)S(1)}, bf16[4,96,768]{2,1,0:T(8,128)(2,1)S(1)}, u32[]{:S(2)}, u32[]{:S(2)}) collective-permute-start(bf16[4,96,768]{2,1,0:T(8,128)(2,1)S(1)} %pad_maximum_fusion.3.refs_0_), channel_id=1, source_target_pairs={{0,4},{4,0},{8,12},{12,8},{16,20},{20,16},{24,28},{28,24},{1,5},{5... | collective-permute-start | bytes 1769480 | tf_op jit(solution)/shard_map/ppermute | solution.py:438
  40.6 46.8 %collective-permute-start.10 = (bf16[4,96,768]{2,1,0:T(8,128)(2,1)S(1)}, bf16[4,96,768]{2,1,0:T(8,128)(2,1)}, u32[]{:S(2)}, u32[]{:S(2)}) collective-permute-start(bf16[4,96,768]{2,1,0:T(8,128)(2,1)S(1)} %pad_maximum_fusion.2.refs_0_), channel_id=1, source_target_pairs={{0,4},{4,0},{8,12},{12,8},{16,20},{20,16},{24,28},{28,24},{1,5},{5... | collective-permute-start | bytes 1769480 | tf_op jit(solution)/shard_map/ppermute | solution.py:438
  43.5 32.2 %collective-permute-start.17 = (bf16[64,192]{1,0:T(8,128)(2,1)S(1)}, bf16[64,192]{1,0:T(8,128)(2,1)S(1)}, u32[]{:S(2)}, u32[]{:S(2)}) collective-permute-start(bf16[64,192]{1,0:T(8,128)(2,1)S(1)} %fusion.refs_1_), channel_id=1, source_target_pairs={{0,3},{1,2},{2,1},{3,0},{4,7},{5,6},{6,5},{7,4},{8,11},{9,10},{10,... | collective-permute-start | bytes 73736 | tf_op jit(solution)/shard_map/ppermute | solution.py:426
  47.0 40.4 %collective-permute-start.11 = (bf16[64,192]{1,0:T(8,128)(2,1)S(1)}, bf16[64,192]{1,0:T(8,128)(2,1)S(1)}, u32[]{:S(2)}, u32[]{:S(2)}) collective-permute-start(bf16[64,192]{1,0:T(8,128)(2,1)S(1)} %fusion.refs_1_), channel_id=1, source_target_pairs={{0,2},{1,3},{2,0},{3,1},{4,6},{5,7},{6,4},{7,5},{8,10},{9,11},{10,... | collective-permute-start | bytes 73736 | tf_op jit(solution)/shard_map/ppermute | solution.py:426
  52.8 45.6 %collective-permute-start.4 = (bf16[4,96,768]{2,1,0:T(8,128)(2,1)S(1)}, bf16[4,96,768]{2,1,0:T(8,128)(2,1)S(1)}, u32[]{:S(2)}, u32[]{:S(2)}) collective-permute-start(bf16[4,96,768]{2,1,0:T(8,128)(2,1)S(1)} %pad_maximum_fusion.1.refs_0_), channel_id=1, source_target_pairs={{0,4},{4,0},{8,12},{12,8},{16,20},{20,16},{24,28},{28,24},{1,5},{5... | collective-permute-start | bytes 1769480 | tf_op jit(solution)/shard_map/ppermute | solution.py:438
  75.7 22.7 %collective-permute-start.5 = (bf16[64,192]{1,0:T(8,128)(2,1)S(1)}, bf16[64,192]{1,0:T(8,128)(2,1)S(1)}, u32[]{:S(2)}, u32[]{:S(2)}) collective-permute-start(bf16[64,192]{1,0:T(8,128)(2,1)S(1)} %fusion.refs_1_), channel_id=1, source_target_pairs={{0,1},{1,0},{2,3},{3,2},{4,5},{5,4},{6,7},{7,6},{8,9},{9,8},{10,11... | collective-permute-start | bytes 73736 | tf_op jit(solution)/shard_map/ppermute | solution.py:426
  124.8 18.2 %collective-permute-start.39 = (bf16[4,32,768]{2,1,0:T(8,128)(2,1)S(1)}, bf16[4,32,768]{2,1,0:T(8,128)(2,1)S(1)}, u32[]{:S(2)}, u32[]{:S(2)}) collective-permute-start(bf16[4,32,768]{2,1,0:T(8,128)(2,1)S(1)} %get-tuple-element.92), channel_id=1, source_target_pairs={{0,20},{4,16},{8,28},{12,24},{16,4},{20,0},{24,12},{28,8},{1,21},{... | collective-permute-start | bytes 589832 | tf_op jit(solution)/shard_map/ppermute | solution.py:450
  125.5 18.8 %collective-permute-start.40 = (bf16[4,32,768]{2,1,0:T(8,128)(2,1)S(1)}, bf16[4,32,768]{2,1,0:T(8,128)(2,1)S(1)}, u32[]{:S(2)}, u32[]{:S(2)}) collective-permute-start(bf16[4,32,768]{2,1,0:T(8,128)(2,1)S(1)} %get-tuple-element.93), channel_id=1, source_target_pairs={{0,24},{4,28},{8,16},{12,20},{16,8},{20,12},{24,0},{28,4},{1,25},{... | collective-permute-start | bytes 589832 | tf_op jit(solution)/shard_map/ppermute | solution.py:450
  129.7 15.7 %collective-permute-start.41 = (bf16[4,32,768]{2,1,0:T(8,128)(2,1)S(1)}, bf16[4,32,768]{2,1,0:T(8,128)(2,1)S(1)}, u32[]{:S(2)}, u32[]{:S(2)}) collective-permute-start(bf16[4,32,768]{2,1,0:T(8,128)(2,1)S(1)} %get-tuple-element.94), channel_id=1, source_target_pairs={{0,28},{4,24},{8,20},{12,16},{16,12},{20,8},{24,4},{28,0},{1,29},{... | collective-permute-start | bytes 589832 | tf_op jit(solution)/shard_map/ppermute | solution.py:450
  134.1 12.9 %collective-permute-start.19 = (bf16[4,32,768]{2,1,0:T(8,128)(2,1)S(1)}, bf16[4,32,768]{2,1,0:T(8,128)(2,1)S(1)}, u32[]{:S(2)}, u32[]{:S(2)}) collective-permute-start(bf16[4,32,768]{2,1,0:T(8,128)(2,1)S(1)} %get-tuple-element.67), channel_id=1, source_target_pairs={{0,8},{4,12},{8,0},{12,4},{16,24},{20,28},{24,16},{28,20},{1,9},{5... | collective-permute-start | bytes 589832 | tf_op jit(solution)/shard_map/ppermute | solution.py:450
  143.0 14.0 %collective-permute-start.20 = (bf16[4,32,768]{2,1,0:T(8,128)(2,1)S(1)}, bf16[4,32,768]{2,1,0:T(8,128)(2,1)S(1)}, u32[]{:S(2)}, u32[]{:S(2)}) collective-permute-start(bf16[4,32,768]{2,1,0:T(8,128)(2,1)S(1)} %get-tuple-element.68), channel_id=1, source_target_pairs={{0,12},{4,8},{8,4},{12,0},{16,28},{20,24},{24,20},{28,16},{1,13},{... | collective-permute-start | bytes 589832 | tf_op jit(solution)/shard_map/ppermute | solution.py:450
  144.3 16.2 %collective-permute-start.21 = (bf16[4,32,768]{2,1,0:T(8,128)(2,1)S(1)}, bf16[4,32,768]{2,1,0:T(8,128)(2,1)S(1)}, u32[]{:S(2)}, u32[]{:S(2)}) collective-permute-start(bf16[4,32,768]{2,1,0:T(8,128)(2,1)S(1)} %get-tuple-element.69), channel_id=1, source_target_pairs={{0,16},{4,20},{8,24},{12,28},{16,0},{20,4},{24,8},{28,12},{1,17},{... | collective-permute-start | bytes 589832 | tf_op jit(solution)/shard_map/ppermute | solution.py:450
  145.4 17.0 %collective-permute-start.22 = (bf16[4,32,768]{2,1,0:T(8,128)(2,1)S(1)}, bf16[4,32,768]{2,1,0:T(8,128)(2,1)S(1)}, u32[]{:S(2)}, u32[]{:S(2)}) collective-permute-start(bf16[4,32,768]{2,1,0:T(8,128)(2,1)S(1)} %get-tuple-element.70), channel_id=1, source_target_pairs={{0,20},{4,16},{8,28},{12,24},{16,4},{20,0},{24,12},{28,8},{1,21},{... | collective-permute-start | bytes 589832 | tf_op jit(solution)/shard_map/ppermute | solution.py:450
  145.5 17.6 %collective-permute-start.23 = (bf16[4,32,768]{2,1,0:T(8,128)(2,1)S(1)}, bf16[4,32,768]{2,1,0:T(8,128)(2,1)S(1)}, u32[]{:S(2)}, u32[]{:S(2)}) collective-permute-start(bf16[4,32,768]{2,1,0:T(8,128)(2,1)S(1)} %get-tuple-element.71), channel_id=1, source_target_pairs={{0,24},{4,28},{8,16},{12,20},{16,8},{20,12},{24,0},{28,4},{1,25},{... | collective-permute-start | bytes 589832 | tf_op jit(solution)/shard_map/ppermute | solution.py:450
  147.0 16.1 %collective-permute-start.24 = (bf16[4,32,768]{2,1,0:T(8,128)(2,1)S(1)}, bf16[4,32,768]{2,1,0:T(8,128)(2,1)S(1)}, u32[]{:S(2)}, u32[]{:S(2)}) collective-permute-start(bf16[4,32,768]{2,1,0:T(8,128)(2,1)S(1)} %get-tuple-element.72), channel_id=1, source_target_pairs={{0,28},{4,24},{8,20},{12,16},{16,12},{20,8},{24,4},{28,0},{1,29},{... | collective-permute-start | bytes 589832 | tf_op jit(solution)/shard_map/ppermute | solution.py:450
  157.0 18.4 %collective-permute-start.42 = (bf16[256,768]{1,0:T(8,128)(2,1)S(1)}, bf16[256,768]{1,0:T(8,128)(2,1)S(1)}, u32[]{:S(2)}, u32[]{:S(2)}) collective-permute-start(bf16[256,768]{1,0:T(8,128)(2,1)S(1)} %get-tuple-element.96), channel_id=1, source_target_pairs={{0,1},{1,0},{2,3},{3,2},{4,5},{5,4},{6,7},{7,6},{8,9},{9,8},{10,11... | collective-permute-start | bytes 1179656 | tf_op jit(solution)/shard_map/ppermute | solution.py:453
  160.5 28.9 %collective-permute-start.43 = (bf16[256,768]{1,0:T(8,128)(2,1)S(1)}, bf16[256,768]{1,0:T(8,128)(2,1)S(1)}, u32[]{:S(2)}, u32[]{:S(2)}) collective-permute-start(bf16[256,768]{1,0:T(8,128)(2,1)S(1)} %get-tuple-element.97), channel_id=1, source_target_pairs={{0,2},{1,3},{2,0},{3,1},{4,6},{5,7},{6,4},{7,5},{8,10},{9,11},{10,... | collective-permute-start | bytes 1179656 | tf_op jit(solution)/shard_map/ppermute | solution.py:453
  162.4 27.0 %collective-permute-start.44 = (bf16[256,768]{1,0:T(8,128)(2,1)S(1)}, bf16[256,768]{1,0:T(8,128)(2,1)S(1)}, u32[]{:S(2)}, u32[]{:S(2)}) collective-permute-start(bf16[256,768]{1,0:T(8,128)(2,1)S(1)} %get-tuple-element.98), channel_id=1, source_target_pairs={{0,3},{1,2},{2,1},{3,0},{4,7},{5,6},{6,5},{7,4},{8,11},{9,10},{10,... | collective-permute-start | bytes 1179656 | tf_op jit(solution)/shard_map/ppermute | solution.py:453
  171.6 23.8 %collective-permute-start.25 = (bf16[256,768]{1,0:T(8,128)(2,1)S(1)}, bf16[256,768]{1,0:T(8,128)(2,1)S(1)}, u32[]{:S(2)}, u32[]{:S(2)}) collective-permute-start(bf16[256,768]{1,0:T(8,128)(2,1)S(1)} %get-tuple-element.74), channel_id=1, source_target_pairs={{0,1},{1,0},{2,3},{3,2},{4,5},{5,4},{6,7},{7,6},{8,9},{9,8},{10,11... | collective-permute-start | bytes 1179656 | tf_op jit(solution)/shard_map/ppermute | solution.py:453
  172.7 50.4 %collective-permute-start.26 = (bf16[256,768]{1,0:T(8,128)(2,1)S(1)}, bf16[256,768]{1,0:T(8,128)(2,1)S(1)}, u32[]{:S(2)}, u32[]{:S(2)}) collective-permute-start(bf16[256,768]{1,0:T(8,128)(2,1)S(1)} %get-tuple-element.75), channel_id=1, source_target_pairs={{0,2},{1,3},{2,0},{3,1},{4,6},{5,7},{6,4},{7,5},{8,10},{9,11},{10,... | collective-permute-start | bytes 1179656 | tf_op jit(solution)/shard_map/ppermute | solution.py:453
  175.4 48.8 %collective-permute-start.27 = (bf16[256,768]{1,0:T(8,128)(2,1)S(1)}, bf16[256,768]{1,0:T(8,128)(2,1)S(1)}, u32[]{:S(2)}, u32[]{:S(2)}) collective-permute-start(bf16[256,768]{1,0:T(8,128)(2,1)S(1)} %get-tuple-element.76), channel_id=1, source_target_pairs={{0,3},{1,2},{2,1},{3,0},{4,7},{5,6},{6,5},{7,4},{8,11},{9,10},{10,... | collective-permute-start | bytes 1179656 | tf_op jit(solution)/shard_map/ppermute | solution.py:453
  189.6 34.8 %collective-permute-start.45 = (bf16[64,768]{1,0:T(8,128)(2,1)S(1)}, bf16[64,768]{1,0:T(8,128)(2,1)S(1)}, u32[]{:S(2)}, u32[]{:S(2)}) collective-permute-start(bf16[64,768]{1,0:T(8,128)(2,1)S(1)} %get-tuple-element.100), channel_id=1, source_target_pairs={{0,4},{4,0},{8,12},{12,8},{16,20},{20,16},{24,28},{28,24},{1,5},{5... | collective-permute-start | bytes 294920 | tf_op jit(solution)/shard_map/ppermute | solution.py:456
  189.7 36.2 %collective-permute-start.46 = (bf16[64,768]{1,0:T(8,128)(2,1)S(1)}, bf16[64,768]{1,0:T(8,128)(2,1)S(1)}, u32[]{:S(2)}, u32[]{:S(2)}) collective-permute-start(bf16[64,768]{1,0:T(8,128)(2,1)S(1)} %get-tuple-element.101), channel_id=1, source_target_pairs={{0,8},{4,12},{8,0},{12,4},{16,24},{20,28},{24,16},{28,20},{1,9},{5... | collective-permute-start | bytes 294920 | tf_op jit(solution)/shard_map/ppermute | solution.py:456
  195.4 32.4 %collective-permute-start.47 = (bf16[64,768]{1,0:T(8,128)(2,1)S(1)}, bf16[64,768]{1,0:T(8,128)(2,1)S(1)}, u32[]{:S(2)}, u32[]{:S(2)}) collective-permute-start(bf16[64,768]{1,0:T(8,128)(2,1)S(1)} %get-tuple-element.102), channel_id=1, source_target_pairs={{0,12},{4,8},{8,4},{12,0},{16,28},{20,24},{24,20},{28,16},{1,13},{... | collective-permute-start | bytes 294920 | tf_op jit(solution)/shard_map/ppermute | solution.py:456
  (27 other events, 197.0 us)

commit v2 on v0

v2 whole, which is shorter than its diff:
```python
import jax
import jax.numpy as jnp
from jax import lax
from jax.experimental import pallas as pl
from jax.experimental.pallas import tpu as pltpu
from jax.sharding import PartitionSpec as P

HD = 64
EXP_DEV = 2
BLOCK = 512
CHUNK = 256
SPLIT = 8
EPS = 1e-05
VMEM_BYTES = 40 * 1024 * 1024
EXPERT_VMEM_BYTES = 16 * 1024 * 1024
LANES = 128
FLOPS = 1.15e9
CELL = 256
CELLS = 26
NORMED, TOKENS, HEADS = 0, 3, 6

F32 = jnp.float32
BF16 = jnp.bfloat16


def xor_pairs(count, bits):
    return [(place, place ^ bits) for place in range(count)]


def dot_nt(a, b):
    return lax.dot_general(a, b, (((1,), (1,)), ((), ())), preferred_element_type=F32)


def dot_tn(a, b):
    return lax.dot_general(a, b, (((0,), (0,)), ((), ())), preferred_element_type=F32)


def dot_nn(a, b):
    return jnp.dot(a, b, preferred_element_type=F32)


def two_terms(x):
    high = x.astype(BF16)
    return high, (x - high.astype(F32)).astype(BF16)


def rms(values):
    return values * lax.rsqrt(jnp.mean(values * values, axis=-1, keepdims=True) + EPS)


def same_head(width):
    rows = lax.broadcasted_iota(jnp.int32, (width, width), 0) // HD
    cols = lax.broadcasted_iota(jnp.int32, (width, width), 1) // HD
    return rows == cols


def rows_of(i):
    return pl.ds(pl.multiple_of(i * BLOCK, BLOCK), BLOCK)


def call(kernel, out_shape, args, micros, scratch=(), space=None, reads=(), writes=(), steps=0, block=None, moving=None):
    given = [] if space is None else [space]
    rows = steps * BLOCK
    made = [] if not writes else [jax.ShapeDtypeStruct((CELLS, rows, CELL), BF16)]
    buffers = [pltpu.VMEM((rows, count * CELL), BF16) for _, count in (*reads, *writes)]
    sems = [pltpu.SemaphoreType.DMA((len(buffers), steps))] if buffers else []

    def body(*refs):
        ins, refs = refs[: len(args)], refs[len(args) :]
        given_ref, refs = refs[: len(given)], refs[len(given) :]
        outs, refs = refs[: len(out_shape)], refs[len(out_shape) :]
        made_ref, refs = refs[: len(made)], refs[len(made) :]
        own, held, sem = refs[: len(scratch)], refs[len(scratch) : len(scratch) + len(buffers)], refs[-1:]

        def copies(n, i):
            first, count = (*reads, *writes)[n]
            at = i if block is None or n >= moving else block(ins[0], i)
            there, here = rows_of(at), rows_of(i)
            for cell in range(count):
                near = held[n].at[here, pl.ds(cell * CELL, CELL)]
                if n < len(reads):
                    yield pltpu.make_async_copy(given_ref[0].at[first + cell, there], near, sem[0].at[n, i])
                else:
                    yield pltpu.make_async_copy(near, made_ref[0].at[first + cell, there], sem[0].at[n, i])

        def arrive(i, fixed=False):
            split = len(reads) if moving is None else moving
            for n in range(split, len(reads)) if fixed else range(split):
                for copy in copies(n, i):
                    copy.wait()

        def leave(i):
            for n in range(len(reads), len(buffers)):
                for copy in copies(n, i):
                    copy.start()

        if reads:

            @pl.loop(0, steps)
            def _(i):
                for n in range(len(reads)):
                    for copy in copies(n, i):
                        copy.start()

        kernel(ins, outs, own, arrive, leave, held[: len(reads)], held[len(reads) :])
        if writes:

            @pl.loop(0, steps)
            def _(i):
                for n in range(len(reads), len(buffers)):
                    for copy in copies(n, i):
                        copy.wait()

    return pl.pallas_call(
        body,
        in_specs=[pl.BlockSpec(memory_space=pltpu.SMEM)]
        + [pl.BlockSpec(memory_space=pltpu.VMEM)] * (len(args) - 1)
        + [pl.BlockSpec(memory_space=pl.ANY)] * len(given),
        out_specs=[pl.BlockSpec(memory_space=pltpu.VMEM)] * len(out_shape)
        + [pl.BlockSpec(memory_space=pl.ANY)] * len(made),
        out_shape=[jax.ShapeDtypeStruct(shape, dtype) for shape, dtype in out_shape] + made,
        scratch_shapes=[*scratch, *buffers, *sems],
        input_output_aliases={len(args): len(out_shape)} if given and made else {},
        compiler_params=pltpu.CompilerParams(vmem_limit_bytes=VMEM_BYTES),
        cost_estimate=pl.CostEstimate(flops=int(micros * FLOPS), bytes_accessed=1 << 20, transcendentals=0),
    )(*args, *given)


def attend_rows(normed, w_ref, width, state):
    q_all = dot_nt(normed, w_ref[0:width, :]).astype(BF16)
    k_all = dot_nt(normed, w_ref[width : 2 * width, :]).astype(BF16)
    v_all = dot_nt(normed, w_ref[2 * width : 3 * width, :]).astype(BF16)
    heads = width // HD
    head_of = lax.broadcasted_iota(jnp.int32, (CHUNK, width), 1) // HD
    causal = lax.broadcasted_iota(jnp.int32, (CHUNK, CHUNK), 0) >= lax.broadcasted_iota(
        jnp.int32, (CHUNK, CHUNK), 1
    )
    same = same_head(width)
    zero = jnp.zeros((), BF16)
    out = []
    for c in range(normed.shape[0] // CHUNK):
        q, k, v = (a[c * CHUNK : (c + 1) * CHUNK] for a in (q_all, k_all, v_all))
        attended = dot_nn(q, state.astype(BF16))
        stacked_q = jnp.concatenate([jnp.where(head_of == h, q, zero) for h in range(heads)], axis=0)
        scores = dot_nt(stacked_q, k)
        weights = jnp.concatenate(
            [jnp.where(causal, scores[h * CHUNK : (h + 1) * CHUNK], 0.0).astype(BF16) for h in range(heads)],
            axis=1,
        )
        stacked_v = jnp.concatenate([jnp.where(head_of == h, v, zero) for h in range(heads)], axis=0)
        out.append(attended + dot_nn(weights, stacked_v))
        state = state + jnp.where(same, dot_tn(k, v), 0.0)
    return q_all, jnp.concatenate(out, axis=0), state


def spread_heads(prior, width):
    spread = jnp.concatenate([prior] * (width // HD), axis=0)
    return jnp.where(same_head(width), spread, jnp.zeros((), prior.dtype))


def attend_own(meta, tokens, stacked, chosen, width, experts, capacity):
    rows, model = tokens.shape
    steps = rows // BLOCK

    def kernel(ins, outs, scratch, arrive, leave, reads, writes):
        _, w_ref, idx_ref, tok_ref = ins
        sum_ref, slot_ref = outs
        normed_ref, kept_ref, q_ref, att_ref = writes
        slot_ref[...] = slot_cols(idx_ref[...], experts, capacity)
        state = jnp.zeros((width, width), F32)
        for i in range(steps):
            at = slice(i * BLOCK, (i + 1) * BLOCK)
            kept_ref[at, :] = tok_ref[at, :]
            normed = rms(tok_ref[at, :].astype(F32)).astype(BF16)
            normed_ref[at, :] = normed
            q_ref[at, 0:width], attended, state = attend_rows(normed, w_ref, width, state)
            att_ref[at, 0:width] = attended.astype(BF16)
            leave(i)
        total = state[:HD]
        for head in range(1, width // HD):
            total = total + state[head * HD : (head + 1) * HD]
        sum_ref[...] = total.astype(BF16)

    cells = model // CELL
    return call(
        kernel,
        [((HD, width), BF16), (chosen.shape, jnp.int32)],
        [meta, stacked, chosen, tokens],
        7,
        writes=[(NORMED, cells), (TOKENS, cells), (HEADS, 1), (HEADS + 1, 1)],
        steps=steps,
    )


def place_slices(meta_ref, same_ref, other_ref, shard, w_ref):
    part = w_ref.shape[0] // SPLIT
    for parity, ref in enumerate((same_ref, other_ref)):
        for i in range(same_ref.shape[0]):
            place = (meta_ref[0] % SPLIT) ^ (2 * i + parity)
            at = pl.ds(pl.multiple_of(place * part, part), part)
            w_ref[at, :] = ref[i, shard * part : (shard + 1) * part]


def attend_other(meta, space, same, other, at_slice, shard, width, rows, model):
    steps = rows // BLOCK

    def kernel(ins, outs, scratch, arrive, leave, reads, writes):
        meta_ref, same_ref, other_ref = ins
        (normed_ref,), (q_ref, att_ref), (w_ref, state_ref) = reads, writes, scratch
        place_slices(meta_ref, same_ref, other_ref, at_slice, w_ref)
        outs[0][...] = w_ref[3 * width : 4 * width, :]
        state_ref[...] = jnp.zeros((width, width), F32)

        @pl.loop(0, steps, unroll=2)
        def _(i):
            at = rows_of(i)
            arrive(i)
            q_ref[at, 0:width], attended, state_ref[...] = attend_rows(
                normed_ref[at, :], w_ref, width, state_ref[...]
            )
            att_ref[at, 0:width] = attended.astype(BF16)
            leave(i)

    first = HEADS + 2 * shard
    return call(
        kernel,
        [((width, model), BF16)],
        [meta, same, other],
        8,
        [pltpu.VMEM((4 * width, model), BF16), pltpu.VMEM((width, width), F32)],
        space=space,
        reads=[(NORMED, model // CELL)],
        writes=[(first, 1), (first + 1, 1)],
        steps=steps,
    )


def slot_rows(chosen, experts, capacity):
    rows = chosen.shape[1]
    hot = chosen == lax.broadcasted_iota(jnp.int32, (experts, rows), 0)
    before = lax.broadcasted_iota(jnp.int32, (rows, rows), 0) < lax.broadcasted_iota(
        jnp.int32, (rows, rows), 1
    )
    preceding = dot_nn(hot.astype(BF16), before.astype(BF16))
    rank = jnp.sum(jnp.where(hot, preceding, 0.0), axis=0, keepdims=True)
    return chosen * capacity + rank.astype(jnp.int32)


def slot_cols(chosen, experts, capacity):
    rows = chosen.shape[0]
    hot = chosen == lax.broadcasted_iota(jnp.int32, (rows, experts), 1)
    before = lax.broadcasted_iota(jnp.int32, (rows, rows), 0) > lax.broadcasted_iota(
        jnp.int32, (rows, rows), 1
    )
    preceding = dot_nn(before.astype(BF16), hot.astype(BF16))
    rank = jnp.sum(jnp.where(hot, preceding, 0.0), axis=1, keepdims=True)
    return chosen * capacity + rank.astype(jnp.int32)


def pick(slots_row, moe_in, seq, ep, local, n_seq, n_ep, capacity):
    wanted = n_seq * capacity
    row = lax.broadcasted_iota(jnp.int32, (wanted, 1), 0)
    pair = ((row // capacity) ^ seq) * (n_ep // 2) + ep // 2
    key = (pair * EXP_DEV + local) * capacity + row % capacity
    hot = (key == slots_row).astype(BF16)
    return dot_nn(hot, moe_in).astype(BF16)


def route(meta, space, same, other, projections, priors, side, early_sum, rows, n_seq, n_ep, capacity, experts):
    width, model = projections[0].shape
    count = len(projections)
    half = rows // BLOCK // 2

    def block(meta_ref, i):
        return half * ((meta_ref[1] // 2) ^ side) + i

    def kernel(ins, outs, scratch, arrive, leave, reads, writes):
        meta_ref, same_ref, other_ref, *refs = ins
        prior_refs, proj_refs, refs = refs[:n_ep], refs[n_ep : n_ep + count], refs[n_ep + count :]
        w_ref, proj_ref, state_ref, key_ref = scratch
        (tok_ref, normed_ref, *kept), fixed = reads[: 2 + 2 * count], reads[2 + 2 * count :]
        place_slices(meta_ref, same_ref, other_ref, n_ep - 3, w_ref)
        for m in range(count):
            proj_ref[m * width : (m + 1) * width, :] = proj_refs[m][...]
        proj_ref[count * width : (count + 1) * width, :] = w_ref[3 * width : 4 * width, :]
        states = [spread_heads(ref[0:HD, :], width) for ref in prior_refs]
        averaging = jnp.where(same_head(width), 1.0 / HD, 0.0).astype(BF16)
        place = meta_ref[1]
        if early_sum is None:
            early, out_refs = jnp.zeros((width, width), F32), outs[1:]
            for i in range(half):
                arrive(i, True)
                n = fixed[0][i * BLOCK : (i + 1) * BLOCK, :]
                k = dot_nt(n, w_ref[width : 2 * width, :]).astype(BF16)
                v = dot_nt(n, w_ref[2 * width : 3 * width, :]).astype(BF16)
                early = early + dot_tn(k, v)
            early = jnp.where(same_head(width), early, 0.0)
            outs[0][...] = early
        else:
            early, out_refs = refs[0][...], outs[1:]
        second = ((place // 2) ^ side) == 1
        state_ref[...] = states[-1].astype(F32) + jnp.where(second, early, 0.0)
        for n in range(2):
            index = prior_refs[2 * side + n][HD : HD + BLOCK // LANES, 0:LANES].astype(F32).astype(jnp.int32)
            index = jnp.concatenate([index[r : r + 1] for r in range(BLOCK // LANES)], axis=1)
            key_ref[n] = slot_rows(index, experts, capacity)

        @pl.loop(0, half)
        def _(i):
            at = rows_of(i)
            relative = (place ^ i) % 2
            arrive(i)
            attended = [
                kept[2 * m + 1][at, 0:width].astype(F32) + dot_nn(kept[2 * m][at, 0:width], states[m])
                for m in range(count)
            ]
            _, last, state_ref[...] = attend_rows(normed_ref[at, :], w_ref, width, state_ref[...])
            heads = []
            for values in (*attended, last):
                mean = dot_nn((values * values).astype(BF16), averaging)
                heads.append((values * lax.rsqrt(mean + EPS)).astype(BF16))
            total = tok_ref[at, :].astype(F32) + dot_nn(jnp.concatenate(heads, axis=1), proj_ref[...])
            stream = total.astype(BF16)
            moe_in = rms(stream.astype(F32)).astype(BF16)
            if side == 0:

                @pl.when(relative == 0)
                def _():
                    outs[0][...] = stream

            for local in range(EXP_DEV):
                picked = pick(key_ref[relative], moe_in, meta_ref[0], place, local, n_seq, n_ep, capacity)
                for k in range(n_seq):
                    out_refs[k // 2][k % 2, relative, local] = picked[k * capacity : (k + 1) * capacity]

    extra = ((width, width), F32) if early_sum is None else ((BLOCK, model), BF16)
    cells = model // CELL
    parts = [(TOKENS, cells), (NORMED, cells)] + [(HEADS + n, 1) for n in range(2 * count)]
    return call(
        kernel,
        [extra] + [((2, 2, EXP_DEV, capacity, model), BF16)] * (n_seq // 2),
        [meta, same, other, *priors, *projections] + ([] if early_sum is None else [early_sum]),
        10,
        [pltpu.VMEM((4 * width, model), BF16), pltpu.VMEM(((count + 1) * width, model), BF16)]
        + [pltpu.VMEM((width, width), F32), pltpu.VMEM((2, 1, BLOCK), jnp.int32)],
        space=space,
        reads=parts + ([(NORMED, cells)] if early_sum is None else []),
        steps=half,
        block=block,
        moving=len(parts),
    )


def expert(got, crossed, expert_in, expert_out, local):
    _, blocks, _, capacity, model = got[0].shape
    count = len(got)
    span = 2 * count * capacity

    def kernel(*refs):
        got_refs, (crossed_ref, w1, w2), out_refs = refs[:count], refs[count : count + 3], refs[count + 3 :]
        pieces = []
        for n in range(blocks):
            for i in range(count):
                pieces += [got_refs[i][0, n, local], crossed_ref[i, n, local]]
        active = jnp.maximum(dot_nn(jnp.concatenate(pieces, axis=0), w1[local]), 0.0).astype(BF16)
        made = dot_nn(active, w2[local]).astype(BF16)
        for n in range(blocks):
            out_refs[n][...] = made[n * span : (n + 1) * span]

    return pl.pallas_call(
        kernel,
        in_specs=[pl.BlockSpec(memory_space=pltpu.VMEM)] * (count + 3),
        out_specs=[pl.BlockSpec(memory_space=pltpu.VMEM)] * blocks,
        out_shape=[jax.ShapeDtypeStruct((span, model), BF16)] * blocks,
        compiler_params=pltpu.CompilerParams(vmem_limit_bytes=EXPERT_VMEM_BYTES),
        cost_estimate=pl.CostEstimate(flops=int(5 * FLOPS), bytes_accessed=1 << 20, transcendentals=0),
    )(*got, crossed, expert_in, expert_out)


def lay_out(meta, own, half, other, n_seq, capacity):
    model = own.shape[1]

    def kernel(ins, outs, scratch, arrive, leave, reads, writes):
        _, own_ref, half_ref, other_ref = ins
        both = (own_ref[...].astype(F32) + half_ref[...].astype(F32)).astype(BF16)
        for side, rows in enumerate((both, other_ref[...])):
            for k in range(n_seq):
                outs[k // 2][k % 2, side * capacity : (side + 1) * capacity, :] = rows[k * capacity : (k + 1) * capacity]

    return call(
        kernel, [((2, 2 * capacity, model), BF16)] * (n_seq // 2), [meta, own, half, other], 0.6
    )


def combine(meta, stream, slots, returned, n_seq, n_ep, capacity):
    rows, model = stream.shape
    count = n_seq // 2 + 1

    def kernel(ins, outs, scratch, arrive, leave, reads, writes):
        meta_ref, stream_ref, slot_ref, *refs = ins
        keys = slot_ref[...]
        total = stream_ref[...].astype(F32)
        span = 2 * capacity
        col = lax.broadcasted_iota(jnp.int32, (1, n_seq * span), 1)
        seq = (col // span) ^ meta_ref[0]
        pair = seq * (n_ep // 2) + ((col // capacity) % 2 ^ (meta_ref[1] // 2))
        for local in range(EXP_DEV):
            key = (pair * EXP_DEV + local) * capacity + col % capacity
            hot = (keys == key).astype(BF16)
            *got_refs, crossed_ref = refs[local * count : (local + 1) * count]
            pieces = []
            for i, got_ref in enumerate(got_refs):
                pieces += [got_ref[0], crossed_ref[i]]
            total = total + dot_nn(hot, jnp.concatenate(pieces, axis=0))
        outs[0][...] = total.astype(BF16)

    flat = [r for got, crossed in returned for r in (*got, crossed)]
    return call(kernel, [((rows, model), BF16)], [meta, stream, slots, *flat], 2.5)[0]


def per_device(tokens, input_proj, output_proj, expert_index, expert_in, expert_out):
    rows, model = tokens.shape
    width = output_proj.shape[0]
    n_seq, n_ep = lax.axis_size("seq"), lax.axis_size("ep")
    seq, ep = lax.axis_index("seq"), lax.axis_index("ep")
    meta = jnp.stack([seq, ep]).astype(jnp.int32)
    own_rows = rows // n_ep
    experts = EXP_DEV * n_seq * n_ep // 2
    capacity = max(2, 2 * own_rows // experts)

    def over_seq(x, bits):
        return lax.ppermute(x, "seq", xor_pairs(n_seq, bits)) if bits else x

    def over_ep(x, bits):
        return lax.ppermute(x, "ep", xor_pairs(n_ep, bits)) if bits else x

    def exchange(outgoing, after=()):
        got = [over_seq(out, 2 * i) for i, out in enumerate(outgoing)]
        got, after = lax.optimization_barrier((got, after))
        return got, over_seq(jnp.stack([g[1] for g in got]), 1)

    stacked = jnp.concatenate(
        [jnp.transpose(input_proj, (1, 2, 0)).reshape(3 * width, model), output_proj], axis=0
    )
    part = stacked.shape[0] // SPLIT
    along = [lax.dynamic_slice_in_dim(stacked, (seq % SPLIT) * part, part, 0)]
    for bit in range(n_ep.bit_length() - 1):
        along.append(over_ep(along[0], 1 << bit))

    own_sum, slots, space = attend_own(
        meta, tokens, stacked, expert_index, width, experts, capacity
    )
    along, own_sum = lax.optimization_barrier((along, own_sum))
    along = {0: along[0], **{1 << bit: a for bit, a in enumerate(along[1:])}}
    for m in range(1, n_ep):
        low = m & (m - 1)
        if low:
            along[m] = over_ep(along[low], m ^ low)

    def gather_layer(pieces):
        first = jnp.concatenate(pieces, axis=0)
        return [over_seq(first, bits) for bits in range(0, SPLIT, 2)]

    early = gather_layer([along[1], own_sum.reshape(-1, model)])
    later = [along[m] for m in range(2, n_ep)]
    later, early = lax.optimization_barrier((later, early))
    late = gather_layer(later)
    early = jnp.stack(early)
    early_other = over_seq(early, 1)

    sum_rows = own_sum.size // model
    sums = jnp.stack([early[:, -sum_rows:], early_other[:, -sum_rows:]], axis=1).reshape(SPLIT, HD, width)
    earlier = (jnp.arange(SPLIT) ^ (seq % SPLIT)) < seq % SPLIT
    prior = jnp.sum(jnp.where(earlier[:, None, None], sums.astype(F32), 0.0), axis=0)
    total, bit = jnp.sum(sums.astype(F32), axis=0), SPLIT
    while bit < n_seq:
        arrived = over_seq(total.astype(BF16), bit).astype(F32)
        prior = prior + jnp.where((seq & bit) != 0, arrived, 0.0)
        total, bit = total + arrived, 2 * bit
    index_rows = jnp.pad(
        expert_index.astype(BF16).reshape(own_rows // LANES, LANES), ((0, 4), (0, width - LANES))
    )
    prior = jnp.concatenate([prior.astype(BF16), index_rows], axis=0)
    priors = [over_ep(prior, m) for m in range(n_ep)]

    early, prior = lax.optimization_barrier((early, prior))
    proj, space = attend_other(meta, space, early, early_other, 0, 1, width, rows, model)
    projections = [output_proj, proj]
    late, projections, priors = lax.optimization_barrier((late, projections, priors))
    late = jnp.stack(late)
    late_other = over_seq(late, 1)
    for m in range(2, n_ep - 1):
        proj, space = attend_other(meta, space, late, late_other, m - 2, m, width, rows, model)
        projections.append(proj)

    def send(side, early_sum):
        return route(
            meta, space, late, late_other, projections, priors, side, early_sum, rows, n_seq, n_ep, capacity, experts
        )

    early_sum, *outgoing = send(1, None)
    stream, *outgoing_own = send(0, early_sum)
    got, crossed = exchange(outgoing, outgoing_own)
    outgoing_own, got = lax.optimization_barrier((outgoing_own, got))
    made, halves = [], []
    for local in range(EXP_DEV):
        if made:
            crossed, made = lax.optimization_barrier((crossed, made))
        made.append(expert(got, crossed, expert_in, expert_out, local))
        halves.append(over_ep(made[-1][1], 1))
    sums = [(pair[0].astype(F32) + half.astype(F32)).astype(BF16) for pair, half in zip(made, halves)]
    got, crossed = exchange(outgoing_own, sums)
    others = [over_ep(both, 2) for both in sums]
    returned = []
    for local in range(EXP_DEV):
        if local > 0:
            crossed, others[0] = lax.optimization_barrier((crossed, others[0]))
        own = expert(got, crossed, expert_in, expert_out, local)
        parts = (own[0], over_ep(own[1], 1), others[local])
        if returned:
            parts, returned[-1] = lax.optimization_barrier((parts, returned[-1]))
        returned.append(exchange(lay_out(meta, *parts, n_seq, capacity)))
    return combine(meta, stream, slots, returned, n_seq, n_ep, capacity)


def solution(mesh):
    return jax.shard_map(
        per_device,
        mesh=mesh,
        in_specs=(
            P("seq", None),
            P(None, None, "ep"),
            P("ep", None),
            P(("seq", "ep"), None),
            P(("seq", "ep"), None, None),
            P(("seq", "ep"), None, None),
        ),
        out_specs=P(("seq", "ep"), None),
        check_vma=False,
    )
```

time: 294 us -> 186 us (0.63)
  blocking collectives: 85.7 us -> 0 us
  Pallas kernels: 0 us -> 62.1 us
  waiting for transfers between devices: 130 us -> 82.7 us
  starting transfers between devices: 4.57 us -> 35.8 us
  matrix products: 28.5 us -> 0 us
  local copies, waits for them, and re-layouts: 15.8 us -> 2.5 us
  between operations: 13.6 us -> 0.54 us
  other arithmetic: 14.5 us -> 2.12 us
    ppermute x0 -> x36, waiting for transfers between devices: none -> 82.7 us  [the longest x12 45 us: over_ep(): return lax.ppermute(x, 'ep', xor_pairs(n_ep, bits)) if bits else x]
    all_to_all x1 -> x0, blocking collectives: 74.5 us -> none  [per_device(): lax.all_to_all(doubled, ('seq', 'ep'), split_axis=0, concat_axis=0, tiled...]
    all_to_all x1 -> x0, waiting for transfers between devices: 70.1 us -> none  [per_device(): lax.all_to_all(expert_part, ('seq', 'ep'), split_axis=0, concat_axis=0, t...]
    pallas_call x0 -> x12, Pallas kernels: none -> 62.1 us  [the longest x8 51.2 us: call(): pl.pallas_call(body, in_specs=[pl.BlockSpec(memory_space=pltpu.SMEM)] + [...]
    reduce_scatter x1 -> x0, waiting for transfers between devices: 59.8 us -> none  [per_device(): lax.psum_scatter(jnp.dot(heads_out, output_proj, preferred_element_type=j...]
    ppermute x0 -> x36, starting transfers between devices: none -> 35.8 us  [the longest x24 21.7 us: over_seq(): return lax.ppermute(x, 'seq', xor_pairs(n_seq, bits)) if bits else x]
    dot_general x7 -> x0, matrix products: 28.5 us -> none  [the longest x1 14.4 us: per_device(): jnp.einsum('sjcf,jfd->sjcd', active, expert_out, preferred_element_type=j...]
    all_gather x1 -> x0, blocking collectives: 11.2 us -> none  [prefix(): everything = lax.all_gather(x.astype(jnp.bfloat16), axis)]
  transfers between devices with their start and end apart: 2 -> 36, of which waited for: 2 -> 20; matrix products, arithmetic and copies ran while one was open for 0% -> 0% of each run, Pallas kernels for 0% -> 17%
where the time goes in v2:
time: 186 us
  waiting for transfers between devices  82.7 us (44%)
  Pallas kernels  62.1 us (33%)
  starting transfers between devices  35.8 us (19%)
  local copies, waits for them, and re-layouts  2.5 us (1%)
  other arithmetic  2.12 us (1%)
    pallas_call x8, Pallas kernels, call(): pl.pallas_call(body, in_specs=[pl.BlockSpec(memory_space=pltpu.SMEM)] + [...  51.2 us
    ppermute x12, waiting for transfers between devices, over_ep(): return lax.ppermute(x, 'ep', xor_pairs(n_ep, bits)) if bits else x  45 us
    ppermute x24, waiting for transfers between devices, over_seq(): return lax.ppermute(x, 'seq', xor_pairs(n_seq, bits)) if bits else x  37.7 us
    ppermute x24, starting transfers between devices, over_seq(): return lax.ppermute(x, 'seq', xor_pairs(n_seq, bits)) if bits else x  21.7 us
    ppermute x12, starting transfers between devices, over_ep(): return lax.ppermute(x, 'ep', xor_pairs(n_ep, bits)) if bits else x  14.1 us
    pallas_call x4, Pallas kernels, expert(): pl.pallas_call(kernel, in_specs=[pl.BlockSpec(memory_space=pltpu.VMEM)] *...  11 us
  transfers between devices with their start and end apart: 36, of which 20 were waited for; matrix products, arithmetic and copies ran while one was open for 0% of the time, Pallas kernels for 17%

profile of v2, /device:TPU:0, one launch (start us, length us, event | category | flops | bytes accessed | tf_op | source)
XLA Modules:
  0.0 185.7 jit_solution(7861038342665691078)
XLA Ops:
  1.1 4.1 %collective-permute-start.1 = (bf16[96,768]{1,0:T(8,128)(2,1)S(1)}, bf16[96,768]{1,0:T(8,128)(2,1)S(1)}, u32[]{:S(2)}, u32[]{:S(2)}) collective-permute-start(bf16[96,768]{1,0:T(8,128)(2,1)S(1)} %fusion), channel_id=1, source_target_pairs={{0,2},{1,3},{2,0},{3,1},{4,6},{5,7},{6,4},{7,5},{8,10},{9,11},{10,... | collective-permute-start | bytes 442376 | tf_op jit(solution)/shard_map/ppermute | solution.py:435
  7.1 1.9 %copy-done.1 = bf16[2048,768]{1,0:T(8,128)(2,1)S(1)} copy-done((bf16[2048,768]{1,0:T(8,128)(2,1)S(1)}, bf16[2048,768]{1,0:T(8,128)(2,1)}, u32[]{:S(2)}) %copy-start.1) | copy-done | bytes 3145752
  9.0 7.1 %shard_map.64 = (bf16[64,192]{1,0:T(8,128)(2,1)S(1)}, s32[512,1]{1,0:T(8,128)S(1)}, bf16[26,2048,256]{2,1,0:T(8,128)(2,1)}) custom-call(s32[2]{0:T(128)S(1)} %pad_add_fusion.refs_0_, bf16[768,768]{1,0:T(8,128)(2,1)S(1)} %pad_maximum_fusion.refs_1_, s32[512,1]{1,0:T(8,128)S(1)} %copy.9.refs_2_, bf16[2048,768]{1,0:T(8,128)(2,1)S(1)} %copy-done.1), custom_call_target="tpu_custom_call" | custom-call | flops 8049999872 | bytes 1048576 | tf_op jit(solution)/shard_map/pallas_call | solution.py:114
  16.2 2.5 %collective-permute-start.5 = (bf16[112,768]{1,0:T(8,128)(2,1)S(1)}, bf16[112,768]{1,0:T(8,128)(2,1)S(1)}, u32[]{:S(2)}, u32[]{:S(2)}) collective-permute-start(bf16[112,768]{1,0:T(8,128)(2,1)S(1)} %constant_dynamic-update-slice_fusion), channel_id=1, source_target_pairs={{0,24},{4,28},{8,16},{12,20},{16,8},{20,12},{24,0},{28,4},{1,25},{... | collective-permute-start | bytes 516104 | tf_op jit(solution)/shard_map/ppermute | solution.py:432
  20.2 4.7 %collective-permute-done.2 = bf16[96,768]{1,0:T(8,128)(2,1)S(1)} collective-permute-done((bf16[96,768]{1,0:T(8,128)(2,1)S(1)}, bf16[96,768]{1,0:T(8,128)(2,1)S(1)}, u32[]{:S(2)}, u32[]{:S(2)}) %collective-permute-start.2) | collective-permute-done | bytes 147488 | tf_op jit(solution)/shard_map/ppermute | solution.py:435
  26.7 1.7 collective-permute-start.8
  32.5 5.0 %collective-permute-done.8 = bf16[192,768]{1,0:T(8,128)(2,1)S(1)} collective-permute-done((bf16[192,768]{1,0:T(8,128)(2,1)S(1)}, bf16[192,768]{1,0:T(8,128)(2,1)S(1)}, u32[]{:S(2)}, u32[]{:S(2)}) %collective-permute-start.8) | collective-permute-done | bytes 294944 | tf_op jit(solution)/shard_map/ppermute | solution.py:432
  38.0 9.0 %shard_map.65 = (bf16[192,768]{1,0:T(8,128)(2,1)S(1)}, bf16[26,2048,256]{2,1,0:T(8,128)(2,1)}) custom-call(s32[2]{0:T(128)S(1)} %pad_add_fusion.refs_0_, bf16[4,112,768]{2,1,0:T(8,128)(2,1)S(1)} %pad_maximum_fusion.4.refs_1_, bf16[4,112,768]{2,1,0:T(8,128)(2,1)S(1)} %collective-permute-done.9.refs_2_, ...), custom_call_target="tpu_custom_call", output_to_operand_aliasing={{1}: (3, {})} | custom-call | flops 9200000000 | bytes 1048576 | tf_op jit(solution)/shard_map/pallas_call | solution.py:114
  47.3 2.8 %collective-permute-done.13.refs_2_ = bf16[4,192,768]{2,1,0:T(8,128)(2,1)S(1)} collective-permute-done((bf16[4,192,768]{2,1,0:T(8,128)(2,1)S(1)}, bf16[4,192,768]{2,1,0:T(8,128)(2,1)S(1)}, u32[]{:S(2)}, u32[]{:S(2)}) %collective-permute-start.13) | collective-permute-done | bytes 1179680 | tf_op jit(solution)/shard_map/ppermute | solution.py:432
  50.1 9.0 %shard_map.66 = (bf16[192,768]{1,0:T(8,128)(2,1)S(1)}, bf16[26,2048,256]{2,1,0:T(8,128)(2,1)}) custom-call(s32[2]{0:T(128)S(1)} %pad_add_fusion.refs_0_, bf16[4,192,768]{2,1,0:T(8,128)(2,1)S(1)} %pad_maximum_fusion.1.refs_1_, bf16[4,192,768]{2,1,0:T(8,128)(2,1)S(1)} %collective-permute-done.13.refs_2_, ...), custom_call_target="tpu_custom_call", output_to_operand_aliasing={{1}: (3, {})} | custom-call | flops 9200000000 | bytes 1048576 | tf_op jit(solution)/shard_map/pallas_call | solution.py:114
  59.1 12.5 %shard_map.67 = (f32[192,192]{1,0:T(8,128)S(1)}, bf16[2,2,2,32,768]{4,3,2,1,0:T(8,128)(2,1)S(1)}, bf16[2,2,2,32,768]{4,3,2,1,0:T(8,128)(2,1)S(1)}, bf16[2,2,2,32...) custom-call(s32[2]{0:T(128)S(1)} %pad_add_fusion.refs_0_, bf16[4,192,768]{2,1,0:T(8,128)(2,1)S(1)} %pad_maximum_fusion.1.refs_1_, ...), custom_call_target="tpu_custom_call" | custom-call | flops 11500000256 | bytes 1048576 | tf_op jit(solution)/shard_map/pallas_call | solution.py:114
  75.1 10.0 %shard_map.68 = (bf16[512,768]{1,0:T(8,128)(2,1)S(1)}, bf16[2,2,2,32,768]{4,3,2,1,0:T(8,128)(2,1)S(1)}, bf16[2,2,2,32,768]{4,3,2,1,0:T(8,128)(2,1)S(1)}, bf16[2,...) custom-call(s32[2]{0:T(128)S(1)} %pad_add_fusion.refs_0_, ...), custom_call_target="tpu_custom_call" | custom-call | flops 11500000256 | bytes 1048576 | tf_op jit(solution)/shard_map/pallas_call | solution.py:114
  85.1 7.3 %collective-permute-done.15.refs_2_ = bf16[2,2,2,32,768]{4,3,2,1,0:T(8,128)(2,1)S(1)} collective-permute-done((bf16[2,2,2,32,768]{4,3,2,1,0:T(8,128)(2,1)S(1)}, bf16[2,2,2,32,768]{4,3,2,1,0:T(8,128)(2,1)S(1)}, u32[]{:S(2)}, u32[]{:S(2)}) %collective-permute-start.15) | collective-permute-done | bytes 393248 | tf_op jit(solution)/shard_map/ppermute | solution.py:432
  92.8 2.3 %collective-permute-done.20.refs_4_ = bf16[4,2,2,32,768]{4,3,2,1,0:T(8,128)(2,1)S(1)} collective-permute-done((bf16[4,2,2,32,768]{4,3,2,1,0:T(8,128)(2,1)S(1)}, bf16[4,2,2,32,768]{4,3,2,1,0:T(8,128)(2,1)S(1)}, u32[]{:S(2)}, u32[]{:S(2)}) %collective-permute-start.20) | collective-permute-done | bytes 786464 | tf_op jit(solution)/shard_map/ppermute | solution.py:432
  95.1 2.7 %shard_map.69 = (bf16[256,768]{1,0:T(8,128)(2,1)S(1)}, bf16[256,768]{1,0:T(8,128)(2,1)S(1)}) custom-call(bf16[2,2,2,32,768]{4,3,2,1,0:T(8,128)(2,1)S(1)} %get-tuple-element.138.refs_0_, bf16[2,2,2,32,768]{4,3,2,1,0:T(8,128)(2,1)S(1)} %collective-permute-done.14.refs_1_, bf16[2,2,2,32,768]{4,3,2,1,0:T(8,128)(2,1)S(1)} %collective-permute-done.15.refs_2_, ...), custom_call_target="tpu_custom_call" | custom-call | flops 5750000128 | bytes 1048576 | tf_op jit(solution)/shard_map/pallas_call | solution.py:370
  97.8 2.7 %shard_map.70 = (bf16[256,768]{1,0:T(8,128)(2,1)S(1)}, bf16[256,768]{1,0:T(8,128)(2,1)S(1)}) custom-call(bf16[2,2,2,32,768]{4,3,2,1,0:T(8,128)(2,1)S(1)} %get-tuple-element.138.refs_0_, bf16[2,2,2,32,768]{4,3,2,1,0:T(8,128)(2,1)S(1)} %collective-permute-done.14.refs_1_, bf16[2,2,2,32,768]{4,3,2,1,0:T(8,128)(2,1)S(1)} %collective-permute-done.15.refs_2_, ...), custom_call_target="tpu_custom_call" | custom-call | flops 5750000128 | bytes 1048576 | tf_op jit(solution)/shard_map/pallas_call | solution.py:370
  100.6 1.6 collective-permute-start.22
  106.1 6.5 %collective-permute-done.22 = bf16[256,768]{1,0:T(8,128)(2,1)S(1)} collective-permute-done((bf16[256,768]{1,0:T(8,128)(2,1)S(1)}, bf16[256,768]{1,0:T(8,128)(2,1)S(1)}, u32[]{:S(2)}, u32[]{:S(2)}) %collective-permute-start.22) | collective-permute-done | bytes 393248 | tf_op jit(solution)/shard_map/ppermute | solution.py:435
  112.7 7.5 %collective-permute-done.21 = bf16[256,768]{1,0:T(8,128)(2,1)S(1)} collective-permute-done((bf16[256,768]{1,0:T(8,128)(2,1)S(1)}, bf16[256,768]{1,0:T(8,128)(2,1)S(1)}, u32[]{:S(2)}, u32[]{:S(2)}) %collective-permute-start.21) | collective-permute-done | bytes 393248 | tf_op jit(solution)/shard_map/ppermute | solution.py:435
  124.4 2.7 %shard_map.72 = (bf16[256,768]{1,0:T(8,128)(2,1)S(1)}, bf16[256,768]{1,0:T(8,128)(2,1)S(1)}) custom-call(bf16[2,2,2,32,768]{4,3,2,1,0:T(8,128)(2,1)S(1)} %get-tuple-element.148.refs_0_, bf16[2,2,2,32,768]{4,3,2,1,0:T(8,128)(2,1)S(1)} %collective-permute-done.17.refs_1_, bf16[2,2,2,32,768]{4,3,2,1,0:T(8,128)(2,1)S(1)} %collective-permute-done.18.refs_2_, ...), custom_call_target="tpu_custom_call" | custom-call | flops 5750000128 | bytes 1048576 | tf_op jit(solution)/shard_map/pallas_call | solution.py:370
  127.2 1.6 collective-permute-start.27
  129.5 14.0 %collective-permute-done.24.refs_3_ = bf16[256,768]{1,0:T(8,128)(2,1)S(1)} collective-permute-done((bf16[256,768]{1,0:T(8,128)(2,1)S(1)}, bf16[256,768]{1,0:T(8,128)(2,1)S(1)}, u32[]{:S(2)}, u32[]{:S(2)}) %collective-permute-start.24) | collective-permute-done | bytes 393248 | tf_op jit(solution)/shard_map/ppermute | solution.py:435
  143.6 3.3 %collective-permute-done.27.refs_2_ = bf16[256,768]{1,0:T(8,128)(2,1)S(1)} collective-permute-done((bf16[256,768]{1,0:T(8,128)(2,1)S(1)}, bf16[256,768]{1,0:T(8,128)(2,1)S(1)}, u32[]{:S(2)}, u32[]{:S(2)}) %collective-permute-start.27) | collective-permute-done | bytes 393248 | tf_op jit(solution)/shard_map/ppermute | solution.py:435
  147.5 1.6 collective-permute-start.28
  151.0 2.7 %shard_map.71 = (bf16[256,768]{1,0:T(8,128)(2,1)S(1)}, bf16[256,768]{1,0:T(8,128)(2,1)S(1)}) custom-call(bf16[2,2,2,32,768]{4,3,2,1,0:T(8,128)(2,1)S(1)} %get-tuple-element.148.refs_0_, bf16[2,2,2,32,768]{4,3,2,1,0:T(8,128)(2,1)S(1)} %collective-permute-done.17.refs_1_, bf16[2,2,2,32,768]{4,3,2,1,0:T(8,128)(2,1)S(1)} %collective-permute-done.18.refs_2_, ...), custom_call_target="tpu_custom_call" | custom-call | flops 5750000128 | bytes 1048576 | tf_op jit(solution)/shard_map/pallas_call | solution.py:370
  155.4 3.7 %collective-permute-done.29.refs_5_ = bf16[2,64,768]{2,1,0:T(8,128)(2,1)S(1)} collective-permute-done((bf16[2,64,768]{2,1,0:T(8,128)(2,1)S(1)}, bf16[2,64,768]{2,1,0:T(8,128)(2,1)S(1)}, u32[]{:S(2)}, u32[]{:S(2)}) %collective-permute-start.29) | collective-permute-done | bytes 196640 | tf_op jit(solution)/shard_map/ppermute | solution.py:432
  160.0 8.3 %collective-permute-done.25.refs_2_ = bf16[256,768]{1,0:T(8,128)(2,1)S(1)} collective-permute-done((bf16[256,768]{1,0:T(8,128)(2,1)S(1)}, bf16[256,768]{1,0:T(8,128)(2,1)S(1)}, u32[]{:S(2)}, u32[]{:S(2)}) %collective-permute-start.25) | collective-permute-done | bytes 393248 | tf_op jit(solution)/shard_map/ppermute | solution.py:435
  169.0 1.6 collective-permute-start.32
  172.6 4.3 %collective-permute-done.32.refs_9_ = bf16[2,64,768]{2,1,0:T(8,128)(2,1)S(1)} collective-permute-done((bf16[2,64,768]{2,1,0:T(8,128)(2,1)S(1)}, bf16[2,64,768]{2,1,0:T(8,128)(2,1)S(1)}, u32[]{:S(2)}, u32[]{:S(2)}) %collective-permute-start.32) | collective-permute-done | bytes 196640 | tf_op jit(solution)/shard_map/ppermute | solution.py:432
  176.8 4.5 %collective-permute-done.33.refs_10_ = bf16[2,64,768]{2,1,0:T(8,128)(2,1)S(1)} collective-permute-done((bf16[2,64,768]{2,1,0:T(8,128)(2,1)S(1)}, bf16[2,64,768]{2,1,0:T(8,128)(2,1)S(1)}, u32[]{:S(2)}, u32[]{:S(2)}) %collective-permute-start.33) | collective-permute-done | bytes 196640 | tf_op jit(solution)/shard_map/ppermute | solution.py:432
  181.6 1.7 collective-permute-done.35.refs_12_
  183.3 2.4 %shard_map.75 = bf16[512,768]{1,0:T(8,128)(2,1)} custom-call(s32[2]{0:T(128)S(1)} %pad_add_fusion.refs_0_, bf16[512,768]{1,0:T(8,128)(2,1)S(1)} %get-tuple-element.120.refs_1_, s32[512,1]{1,0:T(8,128)S(1)} %get-tuple-element.121.refs_2_, bf16[2,64,768]{2,1,0:T(8,128)(2,1)S(1)} %get-tuple-element.165.refs_3_, ...), custom_call_target="tpu_custom_call" | custom-call | flops 2875000064 | bytes 1048576 | tf_op jit(solution)/shard_map/pallas_call | solution.py:114
  (110 shorter events, 31.7 us)
Async XLA Ops:
  1.1 15.0 %collective-permute-start.1 = (bf16[96,768]{1,0:T(8,128)(2,1)S(1)}, bf16[96,768]{1,0:T(8,128)(2,1)S(1)}, u32[]{:S(2)}, u32[]{:S(2)}) collective-permute-start(bf16[96,768]{1,0:T(8,128)(2,1)S(1)} %fusion), channel_id=1, source_target_pairs={{0,2},{1,3},{2,0},{3,1},{4,6},{5,7},{6,4},{7,5},{8,10},{9,11},{10,... | collective-permute-start | bytes 442376 | tf_op jit(solution)/shard_map/ppermute | solution.py:435
  5.2 10.9 %collective-permute-start = (bf16[96,768]{1,0:T(8,128)(2,1)S(1)}, bf16[96,768]{1,0:T(8,128)(2,1)S(1)}, u32[]{:S(2)}, u32[]{:S(2)}) collective-permute-start(bf16[96,768]{1,0:T(8,128)(2,1)S(1)} %fusion), channel_id=1, source_target_pairs={{0,1},{1,0},{2,3},{3,2},{4,5},{5,4},{6,7},{7,6},{8,9},{9,8},{10,11... | collective-permute-start | bytes 442376 | tf_op jit(solution)/shard_map/ppermute | solution.py:435
  16.2 8.7 %collective-permute-start.5 = (bf16[112,768]{1,0:T(8,128)(2,1)S(1)}, bf16[112,768]{1,0:T(8,128)(2,1)S(1)}, u32[]{:S(2)}, u32[]{:S(2)}) collective-permute-start(bf16[112,768]{1,0:T(8,128)(2,1)S(1)} %constant_dynamic-update-slice_fusion), channel_id=1, source_target_pairs={{0,24},{4,28},{8,16},{12,20},{16,8},{20,12},{24,0},{28,4},{1,25},{... | collective-permute-start | bytes 516104 | tf_op jit(solution)/shard_map/ppermute | solution.py:432
  18.7 7.7 %collective-permute-start.4 = (bf16[112,768]{1,0:T(8,128)(2,1)S(1)}, bf16[112,768]{1,0:T(8,128)(2,1)S(1)}, u32[]{:S(2)}, u32[]{:S(2)}) collective-permute-start(bf16[112,768]{1,0:T(8,128)(2,1)S(1)} %constant_dynamic-update-slice_fusion), channel_id=1, source_target_pairs={{0,16},{4,20},{8,24},{12,28},{16,0},{20,4},{24,8},{28,12},{1,17},{... | collective-permute-start | bytes 516104 | tf_op jit(solution)/shard_map/ppermute | solution.py:432
  19.2 7.3 %collective-permute-start.3 = (bf16[112,768]{1,0:T(8,128)(2,1)S(1)}, bf16[112,768]{1,0:T(8,128)(2,1)S(1)}, u32[]{:S(2)}, u32[]{:S(2)}) collective-permute-start(bf16[112,768]{1,0:T(8,128)(2,1)S(1)} %constant_dynamic-update-slice_fusion), channel_id=1, source_target_pairs={{0,8},{4,12},{8,0},{12,4},{16,24},{20,28},{24,16},{28,20},{1,9},{5... | collective-permute-start | bytes 516104 | tf_op jit(solution)/shard_map/ppermute | solution.py:432
  19.8 5.1 %collective-permute-start.2 = (bf16[96,768]{1,0:T(8,128)(2,1)S(1)}, bf16[96,768]{1,0:T(8,128)(2,1)S(1)}, u32[]{:S(2)}, u32[]{:S(2)}) collective-permute-start(bf16[96,768]{1,0:T(8,128)(2,1)S(1)} %collective-permute-done.1), channel_id=1, source_target_pairs={{0,1},{1,0},{2,3},{3,2},{4,5},{5,4},{6,7},{7,6},{8,9},{9,8},{10,11... | collective-permute-start | bytes 442376 | tf_op jit(solution)/shard_map/ppermute | solution.py:435
  26.6 3.7 %collective-permute-start.9 = (bf16[4,112,768]{2,1,0:T(8,128)(2,1)S(1)}, bf16[4,112,768]{2,1,0:T(8,128)(2,1)S(1)}, u32[]{:S(2)}, u32[]{:S(2)}) collective-permute-start(bf16[4,112,768]{2,1,0:T(8,128)(2,1)S(1)} %pad_maximum_fusion.4.refs_1_), channel_id=1, source_target_pairs={{0,4},{4,0},{8,12},{12,8},{16,20},{20,16},{24,28},{28,24},{1,5},{5... | collective-permute-start | bytes 2064392 | tf_op jit(solution)/shard_map/ppermute | solution.py:432
  26.7 10.8 %collective-permute-start.8 = (bf16[192,768]{1,0:T(8,128)(2,1)S(1)}, bf16[192,768]{1,0:T(8,128)(2,1)S(1)}, u32[]{:S(2)}, u32[]{:S(2)}) collective-permute-start(bf16[192,768]{1,0:T(8,128)(2,1)S(1)} %constant_dynamic-update-slice_fusion.2), channel_id=1, source_target_pairs={{0,24},{4,28},{8,16},{12,20},{16,8},{20,12},{24,0},{28,4},{1,25},{... | collective-permute-start | bytes 884744 | tf_op jit(solution)/shard_map/ppermute | solution.py:432
  28.5 18.5 %collective-permute-start.7 = (bf16[192,768]{1,0:T(8,128)(2,1)S(1)}, bf16[192,768]{1,0:T(8,128)(2,1)S(1)}, u32[]{:S(2)}, u32[]{:S(2)}) collective-permute-start(bf16[192,768]{1,0:T(8,128)(2,1)S(1)} %constant_dynamic-update-slice_fusion.2), channel_id=1, source_target_pairs={{0,16},{4,20},{8,24},{12,28},{16,0},{20,4},{24,8},{28,12},{1,17},{... | collective-permute-start | bytes 884744 | tf_op jit(solution)/shard_map/ppermute | solution.py:432
  29.8 17.2 %collective-permute-start.6 = (bf16[192,768]{1,0:T(8,128)(2,1)S(1)}, bf16[192,768]{1,0:T(8,128)(2,1)S(1)}, u32[]{:S(2)}, u32[]{:S(2)}) collective-permute-start(bf16[192,768]{1,0:T(8,128)(2,1)S(1)} %constant_dynamic-update-slice_fusion.2), channel_id=1, source_target_pairs={{0,8},{4,12},{8,0},{12,4},{16,24},{20,28},{24,16},{28,20},{1,9},{5... | collective-permute-start | bytes 884744 | tf_op jit(solution)/shard_map/ppermute | solution.py:432
  30.6 16.4 %collective-permute-start.12 = (bf16[72,192]{1,0:T(8,128)(2,1)S(1)}, bf16[72,192]{1,0:T(8,128)(2,1)S(1)}, u32[]{:S(2)}, u32[]{:S(2)}) collective-permute-start(bf16[72,192]{1,0:T(8,128)(2,1)S(1)} %fusion.2.refs_3_), channel_id=1, source_target_pairs={{0,3},{1,2},{2,1},{3,0},{4,7},{5,6},{6,5},{7,4},{8,11},{9,10},{10,... | collective-permute-start | bytes 82952 | tf_op jit(solution)/shard_map/ppermute | solution.py:435
  31.2 15.8 %collective-permute-start.11 = (bf16[72,192]{1,0:T(8,128)(2,1)S(1)}, bf16[72,192]{1,0:T(8,128)(2,1)S(1)}, u32[]{:S(2)}, u32[]{:S(2)}) collective-permute-start(bf16[72,192]{1,0:T(8,128)(2,1)S(1)} %fusion.2.refs_3_), channel_id=1, source_target_pairs={{0,2},{1,3},{2,0},{3,1},{4,6},{5,7},{6,4},{7,5},{8,10},{9,11},{10,... | collective-permute-start | bytes 82952 | tf_op jit(solution)/shard_map/ppermute | solution.py:435
  37.6 9.5 %collective-permute-start.10 = (bf16[72,192]{1,0:T(8,128)(2,1)S(1)}, bf16[72,192]{1,0:T(8,128)(2,1)S(1)}, u32[]{:S(2)}, u32[]{:S(2)}) collective-permute-start(bf16[72,192]{1,0:T(8,128)(2,1)S(1)} %fusion.2.refs_3_), channel_id=1, source_target_pairs={{0,1},{1,0},{2,3},{3,2},{4,5},{5,4},{6,7},{7,6},{8,9},{9,8},{10,11... | collective-permute-start | bytes 82952 | tf_op jit(solution)/shard_map/ppermute | solution.py:435
  71.6 13.6 %collective-permute-start.14 = (bf16[2,2,2,32,768]{4,3,2,1,0:T(8,128)(2,1)S(1)}, bf16[2,2,2,32,768]{4,3,2,1,0:T(8,128)(2,1)S(1)}, u32[]{:S(2)}, u32[]{:S(2)}) collective-permute-start(bf16[2,2,2,32,768]{4,3,2,1,0:T(8,128)(2,1)S(1)} %get-tuple-element.127), channel_id=1, source_target_pairs={{0,8},{4,12},{8,0},{12,4},{16,24},{20,28},{24,16},{28,20},{1,9},{5... | collective-permute-start | bytes 1179656 | tf_op jit(solution)/shard_map/ppermute | solution.py:432
  73.2 19.3 %collective-permute-start.15 = (bf16[2,2,2,32,768]{4,3,2,1,0:T(8,128)(2,1)S(1)}, bf16[2,2,2,32,768]{4,3,2,1,0:T(8,128)(2,1)S(1)}, u32[]{:S(2)}, u32[]{:S(2)}) collective-permute-start(bf16[2,2,2,32,768]{4,3,2,1,0:T(8,128)(2,1)S(1)} %get-tuple-element.128), channel_id=1, source_target_pairs={{0,16},{4,20},{8,24},{12,28},{16,0},{20,4},{24,8},{28,12},{1,17},{... | collective-permute-start | bytes 1179656 | tf_op jit(solution)/shard_map/ppermute | solution.py:432
  73.9 18.6 %collective-permute-start.16 = (bf16[2,2,2,32,768]{4,3,2,1,0:T(8,128)(2,1)S(1)}, bf16[2,2,2,32,768]{4,3,2,1,0:T(8,128)(2,1)S(1)}, u32[]{:S(2)}, u32[]{:S(2)}) collective-permute-start(bf16[2,2,2,32,768]{4,3,2,1,0:T(8,128)(2,1)S(1)} %get-tuple-element.129), channel_id=1, source_target_pairs={{0,24},{4,28},{8,16},{12,20},{16,8},{20,12},{24,0},{28,4},{1,25},{... | collective-permute-start | bytes 1179656 | tf_op jit(solution)/shard_map/ppermute | solution.py:432
  100.6 12.0 %collective-permute-start.22 = (bf16[256,768]{1,0:T(8,128)(2,1)S(1)}, bf16[256,768]{1,0:T(8,128)(2,1)S(1)}, u32[]{:S(2)}, u32[]{:S(2)}) collective-permute-start(bf16[256,768]{1,0:T(8,128)(2,1)S(1)} %get-tuple-element.147), channel_id=1, source_target_pairs={{0,1},{1,0},{2,3},{3,2},{4,5},{5,4},{6,7},{7,6},{8,9},{9,8},{10,11... | collective-permute-start | bytes 1179656 | tf_op jit(solution)/shard_map/ppermute | solution.py:435
  102.2 18.0 %collective-permute-start.21 = (bf16[256,768]{1,0:T(8,128)(2,1)S(1)}, bf16[256,768]{1,0:T(8,128)(2,1)S(1)}, u32[]{:S(2)}, u32[]{:S(2)}) collective-permute-start(bf16[256,768]{1,0:T(8,128)(2,1)S(1)} %get-tuple-element.143), channel_id=1, source_target_pairs={{0,1},{1,0},{2,3},{3,2},{4,5},{5,4},{6,7},{7,6},{8,9},{9,8},{10,11... | collective-permute-start | bytes 1179656 | tf_op jit(solution)/shard_map/ppermute | solution.py:435
  102.6 17.7 %collective-permute-start.17 = (bf16[2,2,2,32,768]{4,3,2,1,0:T(8,128)(2,1)S(1)}, bf16[2,2,2,32,768]{4,3,2,1,0:T(8,128)(2,1)S(1)}, u32[]{:S(2)}, u32[]{:S(2)}) collective-permute-start(bf16[2,2,2,32,768]{4,3,2,1,0:T(8,128)(2,1)S(1)} %get-tuple-element.135), channel_id=1, source_target_pairs={{0,8},{4,12},{8,0},{12,4},{16,24},{20,28},{24,16},{28,20},{1,9},{5... | collective-permute-start | bytes 1179656 | tf_op jit(solution)/shard_map/ppermute | solution.py:432
  103.2 17.2 %collective-permute-start.18 = (bf16[2,2,2,32,768]{4,3,2,1,0:T(8,128)(2,1)S(1)}, bf16[2,2,2,32,768]{4,3,2,1,0:T(8,128)(2,1)S(1)}, u32[]{:S(2)}, u32[]{:S(2)}) collective-permute-start(bf16[2,2,2,32,768]{4,3,2,1,0:T(8,128)(2,1)S(1)} %get-tuple-element.136), channel_id=1, source_target_pairs={{0,16},{4,20},{8,24},{12,28},{16,0},{20,4},{24,8},{28,12},{1,17},{... | collective-permute-start | bytes 1179656 | tf_op jit(solution)/shard_map/ppermute | solution.py:432
  104.6 17.3 %collective-permute-start.19 = (bf16[2,2,2,32,768]{4,3,2,1,0:T(8,128)(2,1)S(1)}, bf16[2,2,2,32,768]{4,3,2,1,0:T(8,128)(2,1)S(1)}, u32[]{:S(2)}, u32[]{:S(2)}) collective-permute-start(bf16[2,2,2,32,768]{4,3,2,1,0:T(8,128)(2,1)S(1)} %get-tuple-element.137), channel_id=1, source_target_pairs={{0,24},{4,28},{8,16},{12,20},{16,8},{20,12},{24,0},{28,4},{1,25},{... | collective-permute-start | bytes 1179656 | tf_op jit(solution)/shard_map/ppermute | solution.py:432
  122.2 21.4 %collective-permute-start.24 = (bf16[256,768]{1,0:T(8,128)(2,1)S(1)}, bf16[256,768]{1,0:T(8,128)(2,1)S(1)}, u32[]{:S(2)}, u32[]{:S(2)}) collective-permute-start(bf16[256,768]{1,0:T(8,128)(2,1)S(1)} %add_convert_fusion.1), channel_id=1, source_target_pairs={{0,2},{1,3},{2,0},{3,1},{4,6},{5,7},{6,4},{7,5},{8,10},{9,11},{10,... | collective-permute-start | bytes 1179656 | tf_op jit(solution)/shard_map/ppermute | solution.py:435
  127.2 19.6 %collective-permute-start.27 = (bf16[256,768]{1,0:T(8,128)(2,1)S(1)}, bf16[256,768]{1,0:T(8,128)(2,1)S(1)}, u32[]{:S(2)}, u32[]{:S(2)}) collective-permute-start(bf16[256,768]{1,0:T(8,128)(2,1)S(1)} %get-tuple-element.156), channel_id=1, source_target_pairs={{0,1},{1,0},{2,3},{3,2},{4,5},{5,4},{6,7},{7,6},{8,9},{9,8},{10,11... | collective-permute-start | bytes 1179656 | tf_op jit(solution)/shard_map/ppermute | solution.py:435
  128.8 31.2 %collective-permute-start.26 = (bf16[256,768]{1,0:T(8,128)(2,1)S(1)}, bf16[256,768]{1,0:T(8,128)(2,1)S(1)}, u32[]{:S(2)}, u32[]{:S(2)}) collective-permute-start(bf16[256,768]{1,0:T(8,128)(2,1)S(1)} %add_convert_fusion), channel_id=1, source_target_pairs={{0,2},{1,3},{2,0},{3,1},{4,6},{5,7},{6,4},{7,5},{8,10},{9,11},{10,... | collective-permute-start | bytes 1179656 | tf_op jit(solution)/shard_map/ppermute | solution.py:435
  147.5 7.9 %collective-permute-start.28 = (bf16[2,64,768]{2,1,0:T(8,128)(2,1)S(1)}, bf16[2,64,768]{2,1,0:T(8,128)(2,1)S(1)}, u32[]{:S(2)}, u32[]{:S(2)}) collective-permute-start(bf16[2,64,768]{2,1,0:T(8,128)(2,1)S(1)} %get-tuple-element.158), channel_id=1, source_target_pairs={{0,8},{4,12},{8,0},{12,4},{16,24},{20,28},{24,16},{28,20},{1,9},{5... | collective-permute-start | bytes 589832 | tf_op jit(solution)/shard_map/ppermute | solution.py:432
  149.1 10.0 %collective-permute-start.29 = (bf16[2,64,768]{2,1,0:T(8,128)(2,1)S(1)}, bf16[2,64,768]{2,1,0:T(8,128)(2,1)S(1)}, u32[]{:S(2)}, u32[]{:S(2)}) collective-permute-start(bf16[2,64,768]{2,1,0:T(8,128)(2,1)S(1)} %get-tuple-element.159), channel_id=1, source_target_pairs={{0,16},{4,20},{8,24},{12,28},{16,0},{20,4},{24,8},{28,12},{1,17},{... | collective-permute-start | bytes 589832 | tf_op jit(solution)/shard_map/ppermute | solution.py:432
  149.8 9.3 %collective-permute-start.30 = (bf16[2,64,768]{2,1,0:T(8,128)(2,1)S(1)}, bf16[2,64,768]{2,1,0:T(8,128)(2,1)S(1)}, u32[]{:S(2)}, u32[]{:S(2)}) collective-permute-start(bf16[2,64,768]{2,1,0:T(8,128)(2,1)S(1)} %get-tuple-element.160), channel_id=1, source_target_pairs={{0,24},{4,28},{8,16},{12,20},{16,8},{20,12},{24,0},{28,4},{1,25},{... | collective-permute-start | bytes 589832 | tf_op jit(solution)/shard_map/ppermute | solution.py:432
  153.8 14.6 %collective-permute-start.25 = (bf16[256,768]{1,0:T(8,128)(2,1)S(1)}, bf16[256,768]{1,0:T(8,128)(2,1)S(1)}, u32[]{:S(2)}, u32[]{:S(2)}) collective-permute-start(bf16[256,768]{1,0:T(8,128)(2,1)S(1)} %get-tuple-element.154), channel_id=1, source_target_pairs={{0,1},{1,0},{2,3},{3,2},{4,5},{5,4},{6,7},{7,6},{8,9},{9,8},{10,11... | collective-permute-start | bytes 1179656 | tf_op jit(solution)/shard_map/ppermute | solution.py:435
  159.2 9.1 %collective-permute-start.31 = (bf16[4,64,768]{2,1,0:T(8,128)(2,1)S(1)}, bf16[4,64,768]{2,1,0:T(8,128)(2,1)S(1)}, u32[]{:S(2)}, u32[]{:S(2)}) collective-permute-start(bf16[4,64,768]{2,1,0:T(8,128)(2,1)S(1)} %pad_maximum_fusion.5), channel_id=1, source_target_pairs={{0,4},{4,0},{8,12},{12,8},{16,20},{20,16},{24,28},{28,24},{1,5},{5... | collective-permute-start | bytes 1179656 | tf_op jit(solution)/shard_map/ppermute | solution.py:432
  169.0 7.8 %collective-permute-start.32 = (bf16[2,64,768]{2,1,0:T(8,128)(2,1)S(1)}, bf16[2,64,768]{2,1,0:T(8,128)(2,1)S(1)}, u32[]{:S(2)}, u32[]{:S(2)}) collective-permute-start(bf16[2,64,768]{2,1,0:T(8,128)(2,1)S(1)} %get-tuple-element.174), channel_id=1, source_target_pairs={{0,8},{4,12},{8,0},{12,4},{16,24},{20,28},{24,16},{28,20},{1,9},{5... | collective-permute-start | bytes 589832 | tf_op jit(solution)/shard_map/ppermute | solution.py:432
  170.6 10.8 %collective-permute-start.33 = (bf16[2,64,768]{2,1,0:T(8,128)(2,1)S(1)}, bf16[2,64,768]{2,1,0:T(8,128)(2,1)S(1)}, u32[]{:S(2)}, u32[]{:S(2)}) collective-permute-start(bf16[2,64,768]{2,1,0:T(8,128)(2,1)S(1)} %get-tuple-element.175), channel_id=1, source_target_pairs={{0,16},{4,20},{8,24},{12,28},{16,0},{20,4},{24,8},{28,12},{1,17},{... | collective-permute-start | bytes 589832 | tf_op jit(solution)/shard_map/ppermute | solution.py:432
  171.3 10.0 %collective-permute-start.34 = (bf16[2,64,768]{2,1,0:T(8,128)(2,1)S(1)}, bf16[2,64,768]{2,1,0:T(8,128)(2,1)S(1)}, u32[]{:S(2)}, u32[]{:S(2)}) collective-permute-start(bf16[2,64,768]{2,1,0:T(8,128)(2,1)S(1)} %get-tuple-element.176), channel_id=1, source_target_pairs={{0,24},{4,28},{8,16},{12,20},{16,8},{20,12},{24,0},{28,4},{1,25},{... | collective-permute-start | bytes 589832 | tf_op jit(solution)/shard_map/ppermute | solution.py:432
  (12 other events, 142.3 us)

commit v3 on v2

--- a/solution.py
+++ b/solution.py
@@ -83,11 +83,23 @@
                 else:
                     yield pltpu.make_async_copy(near, made_ref[0].at[first + cell, there], sem[0].at[n, i])
 
+        split = len(reads) if moving is None else moving
+
+        def fetch(i, parts):
+            for n in parts:
+                for copy in copies(n, i):
+                    copy.start()
+
         def arrive(i, fixed=False):
-            split = len(reads) if moving is None else moving
-            for n in range(split, len(reads)) if fixed else range(split):
+            parts = range(split, len(reads)) if fixed else range(split)
+            for n in parts:
                 for copy in copies(n, i):
                     copy.wait()
+            if not fixed:
+
+                @pl.when(i + 1 < steps)
+                def _():
+                    fetch(i + 1, parts)
 
         def leave(i):
             for n in range(len(reads), len(buffers)):
@@ -95,13 +107,9 @@
                     copy.start()
 
         if reads:
-
-            @pl.loop(0, steps)
-            def _(i):
-                for n in range(len(reads)):
-                    for copy in copies(n, i):
-                        copy.start()
-
+            for i in range(steps):
+                fetch(i, range(split, len(reads)))
+            fetch(0, range(split))
         kernel(ins, outs, own, arrive, leave, held[: len(reads)], held[len(reads) :])
         if writes:
 
@@ -201,13 +209,13 @@
             w_ref[at, :] = ref[i, shard * part : (shard + 1) * part]
 
 
-def attend_other(meta, space, same, other, at_slice, shard, width, rows, model):
+def attend_other(meta, space, same, other, shard, width, rows, model):
     steps = rows // BLOCK
 
     def kernel(ins, outs, scratch, arrive, leave, reads, writes):
         meta_ref, same_ref, other_ref = ins
         (normed_ref,), (q_ref, att_ref), (w_ref, state_ref) = reads, writes, scratch
-        place_slices(meta_ref, same_ref, other_ref, at_slice, w_ref)
+        place_slices(meta_ref, same_ref, other_ref, 0, w_ref)
         outs[0][...] = w_ref[3 * width : 4 * width, :]
         state_ref[...] = jnp.zeros((width, width), F32)
 
@@ -269,6 +277,7 @@
 def route(meta, space, same, other, projections, priors, side, early_sum, rows, n_seq, n_ep, capacity, experts):
     width, model = projections[0].shape
     count = len(projections)
+    lasts = n_ep - count
     half = rows // BLOCK // 2
 
     def block(meta_ref, i):
@@ -277,33 +286,41 @@
     def kernel(ins, outs, scratch, arrive, leave, reads, writes):
         meta_ref, same_ref, other_ref, *refs = ins
         prior_refs, proj_refs, refs = refs[:n_ep], refs[n_ep : n_ep + count], refs[n_ep + count :]
-        w_ref, proj_ref, state_ref, key_ref = scratch
+        proj_ref, state_ref, key_ref, *w_refs = scratch
         (tok_ref, normed_ref, *kept), fixed = reads[: 2 + 2 * count], reads[2 + 2 * count :]
-        place_slices(meta_ref, same_ref, other_ref, n_ep - 3, w_ref)
         for m in range(count):
             proj_ref[m * width : (m + 1) * width, :] = proj_refs[m][...]
-        proj_ref[count * width : (count + 1) * width, :] = w_ref[3 * width : 4 * width, :]
+        for n, w_ref in enumerate(w_refs):
+            m = count + n
+            place_slices(meta_ref, same_ref, other_ref, n, w_ref)
+            proj_ref[m * width : (m + 1) * width, :] = w_ref[3 * width : 4 * width, :]
+        same_heads = same_head(width)
         states = [spread_heads(ref[0:HD, :], width) for ref in prior_refs]
-        averaging = jnp.where(same_head(width), 1.0 / HD, 0.0).astype(BF16)
+        averaging = jnp.where(same_heads, 1.0 / HD, 0.0).astype(BF16)
         place = meta_ref[1]
-        if early_sum is None:
-            early, out_refs = jnp.zeros((width, width), F32), outs[1:]
-            for i in range(half):
-                arrive(i, True)
-                n = fixed[0][i * BLOCK : (i + 1) * BLOCK, :]
-                k = dot_nt(n, w_ref[width : 2 * width, :]).astype(BF16)
-                v = dot_nt(n, w_ref[2 * width : 3 * width, :]).astype(BF16)
-                early = early + dot_tn(k, v)
-            early = jnp.where(same_head(width), early, 0.0)
-            outs[0][...] = early
-        else:
-            early, out_refs = refs[0][...], outs[1:]
-        second = ((place // 2) ^ side) == 1
-        state_ref[...] = states[-1].astype(F32) + jnp.where(second, early, 0.0)
+        out_refs = outs[1:]
         for n in range(2):
             index = prior_refs[2 * side + n][HD : HD + BLOCK // LANES, 0:LANES].astype(F32).astype(jnp.int32)
             index = jnp.concatenate([index[r : r + 1] for r in range(BLOCK // LANES)], axis=1)
             key_ref[n] = slot_rows(index, experts, capacity)
+        second = ((place // 2) ^ side) == 1
+        if early_sum is None:
+            for n in range(lasts):
+                outs[0][n] = jnp.zeros((width, width), F32)
+            for i in range(half):
+                arrive(i, True)
+
+            @pl.loop(0, half)
+            def _(i):
+                rows_in = fixed[0][rows_of(i), :]
+                for n, w_ref in enumerate(w_refs):
+                    k = dot_nt(rows_in, w_ref[width : 2 * width, :]).astype(BF16)
+                    v = dot_nt(rows_in, w_ref[2 * width : 3 * width, :]).astype(BF16)
+                    outs[0][n] += jnp.where(same_heads, dot_tn(k, v), 0.0)
+
+        early_ref = outs[0] if early_sum is None else refs[0]
+        for n in range(lasts):
+            state_ref[n] = states[count + n].astype(F32) + jnp.where(second, early_ref[n], 0.0)
 
         @pl.loop(0, half)
         def _(i):
@@ -314,9 +331,11 @@
                 kept[2 * m + 1][at, 0:width].astype(F32) + dot_nn(kept[2 * m][at, 0:width], states[m])
                 for m in range(count)
             ]
-            _, last, state_ref[...] = attend_rows(normed_ref[at, :], w_ref, width, state_ref[...])
+            for n, w_ref in enumerate(w_refs):
+                _, last, state_ref[n] = attend_rows(normed_ref[at, :], w_ref, width, state_ref[n])
+                attended.append(last)
             heads = []
-            for values in (*attended, last):
+            for values in attended:
                 mean = dot_nn((values * values).astype(BF16), averaging)
                 heads.append((values * lax.rsqrt(mean + EPS)).astype(BF16))
             total = tok_ref[at, :].astype(F32) + dot_nn(jnp.concatenate(heads, axis=1), proj_ref[...])
@@ -333,16 +352,17 @@
                 for k in range(n_seq):
                     out_refs[k // 2][k % 2, relative, local] = picked[k * capacity : (k + 1) * capacity]
 
-    extra = ((width, width), F32) if early_sum is None else ((BLOCK, model), BF16)
+    extra = ((lasts, width, width), F32) if early_sum is None else ((BLOCK, model), BF16)
     cells = model // CELL
     parts = [(TOKENS, cells), (NORMED, cells)] + [(HEADS + n, 1) for n in range(2 * count)]
     return call(
         kernel,
         [extra] + [((2, 2, EXP_DEV, capacity, model), BF16)] * (n_seq // 2),
         [meta, same, other, *priors, *projections] + ([] if early_sum is None else [early_sum]),
-        10,
-        [pltpu.VMEM((4 * width, model), BF16), pltpu.VMEM(((count + 1) * width, model), BF16)]
-        + [pltpu.VMEM((width, width), F32), pltpu.VMEM((2, 1, BLOCK), jnp.int32)],
+        13,
+        [pltpu.VMEM((n_ep * width, model), BF16), pltpu.VMEM((lasts, width, width), F32)]
+        + [pltpu.VMEM((2, 1, BLOCK), jnp.int32)]
+        + [pltpu.VMEM((4 * width, model), BF16)] * lasts,
         space=space,
         reads=parts + ([(NORMED, cells)] if early_sum is None else []),
         steps=half,
@@ -351,13 +371,17 @@
     )
 
 
-def expert(got, crossed, expert_in, expert_out, local):
+def expert(got, crossed, expert_in, expert_out, local, pairs=()):
     _, blocks, _, capacity, model = got[0].shape
     count = len(got)
     span = 2 * count * capacity
 
     def kernel(*refs):
-        got_refs, (crossed_ref, w1, w2), out_refs = refs[:count], refs[count : count + 3], refs[count + 3 :]
+        got_refs, (crossed_ref, w1, w2) = refs[:count], refs[count : count + 3]
+        pair_refs, out_refs = refs[count + 3 : count + 3 + 2 * len(pairs)], refs[count + 3 + 2 * len(pairs) :]
+        for n in range(len(pairs)):
+            both = pair_refs[2 * n][...].astype(F32) + pair_refs[2 * n + 1][...].astype(F32)
+            out_refs[blocks + n][...] = both.astype(BF16)
         pieces = []
         for n in range(blocks):
             for i in range(count):
@@ -367,14 +391,16 @@
         for n in range(blocks):
             out_refs[n][...] = made[n * span : (n + 1) * span]
 
-    return pl.pallas_call(
+    flat = [a for pair in pairs for a in pair]
+    out = pl.pallas_call(
         kernel,
-        in_specs=[pl.BlockSpec(memory_space=pltpu.VMEM)] * (count + 3),
-        out_specs=[pl.BlockSpec(memory_space=pltpu.VMEM)] * blocks,
-        out_shape=[jax.ShapeDtypeStruct((span, model), BF16)] * blocks,
+        in_specs=[pl.BlockSpec(memory_space=pltpu.VMEM)] * (count + 3 + len(flat)),
+        out_specs=[pl.BlockSpec(memory_space=pltpu.VMEM)] * (blocks + len(pairs)),
+        out_shape=[jax.ShapeDtypeStruct((span, model), BF16)] * (blocks + len(pairs)),
         compiler_params=pltpu.CompilerParams(vmem_limit_bytes=EXPERT_VMEM_BYTES),
-        cost_estimate=pl.CostEstimate(flops=int(5 * FLOPS), bytes_accessed=1 << 20, transcendentals=0),
-    )(*got, crossed, expert_in, expert_out)
+        cost_estimate=pl.CostEstimate(flops=int(3 * FLOPS), bytes_accessed=1 << 20, transcendentals=0),
+    )(*got, crossed, expert_in, expert_out, *flat)
+    return out[:blocks], out[blocks:]
 
 
 def lay_out(meta, own, half, other, n_seq, capacity):
@@ -392,30 +418,25 @@
     )
 
 
-def combine(meta, stream, slots, returned, n_seq, n_ep, capacity):
-    rows, model = stream.shape
-    count = n_seq // 2 + 1
+def combine(meta, total, slots, returned, local, n_seq, n_ep, capacity, dtype):
+    rows, model = total.shape
+    got, crossed = returned
 
     def kernel(ins, outs, scratch, arrive, leave, reads, writes):
-        meta_ref, stream_ref, slot_ref, *refs = ins
-        keys = slot_ref[...]
-        total = stream_ref[...].astype(F32)
+        meta_ref, total_ref, slot_ref, *got_refs, crossed_ref = ins
         span = 2 * capacity
         col = lax.broadcasted_iota(jnp.int32, (1, n_seq * span), 1)
         seq = (col // span) ^ meta_ref[0]
         pair = seq * (n_ep // 2) + ((col // capacity) % 2 ^ (meta_ref[1] // 2))
-        for local in range(EXP_DEV):
-            key = (pair * EXP_DEV + local) * capacity + col % capacity
-            hot = (keys == key).astype(BF16)
-            *got_refs, crossed_ref = refs[local * count : (local + 1) * count]
-            pieces = []
-            for i, got_ref in enumerate(got_refs):
-                pieces += [got_ref[0], crossed_ref[i]]
-            total = total + dot_nn(hot, jnp.concatenate(pieces, axis=0))
-        outs[0][...] = total.astype(BF16)
-
-    flat = [r for got, crossed in returned for r in (*got, crossed)]
-    return call(kernel, [((rows, model), BF16)], [meta, stream, slots, *flat], 2.5)[0]
+        key = (pair * EXP_DEV + local) * capacity + col % capacity
+        hot = (slot_ref[...] == key).astype(BF16)
+        pieces = []
+        for i, got_ref in enumerate(got_refs):
+            pieces += [got_ref[0], crossed_ref[i]]
+        out = total_ref[...].astype(F32) + dot_nn(hot, jnp.concatenate(pieces, axis=0))
+        outs[0][...] = out.astype(dtype)
+
+    return call(kernel, [((rows, model), dtype)], [meta, total, slots, *got, crossed], 1.5)[0]
 
 
 def per_device(tokens, input_proj, output_proj, expert_index, expert_in, expert_out):
@@ -481,18 +502,17 @@
         expert_index.astype(BF16).reshape(own_rows // LANES, LANES), ((0, 4), (0, width - LANES))
     )
     prior = jnp.concatenate([prior.astype(BF16), index_rows], axis=0)
-    priors = [over_ep(prior, m) for m in range(n_ep)]
+    priors = [prior]
+    for m in range(1, n_ep):
+        low = m & (m - 1)
+        priors.append(over_ep(priors[low], m ^ low))
 
     early, prior = lax.optimization_barrier((early, prior))
-    proj, space = attend_other(meta, space, early, early_other, 0, 1, width, rows, model)
+    proj, space = attend_other(meta, space, early, early_other, 1, width, rows, model)
     projections = [output_proj, proj]
     late, projections, priors = lax.optimization_barrier((late, projections, priors))
     late = jnp.stack(late)
     late_other = over_seq(late, 1)
-    for m in range(2, n_ep - 1):
-        proj, space = attend_other(meta, space, late, late_other, m - 2, m, width, rows, model)
-        projections.append(proj)
-
     def send(side, early_sum):
         return route(
             meta, space, late, late_other, projections, priors, side, early_sum, rows, n_seq, n_ep, capacity, experts
@@ -506,21 +526,25 @@
     for local in range(EXP_DEV):
         if made:
             crossed, made = lax.optimization_barrier((crossed, made))
-        made.append(expert(got, crossed, expert_in, expert_out, local))
+        made.append(expert(got, crossed, expert_in, expert_out, local)[0])
         halves.append(over_ep(made[-1][1], 1))
-    sums = [(pair[0].astype(F32) + half.astype(F32)).astype(BF16) for pair, half in zip(made, halves)]
-    got, crossed = exchange(outgoing_own, sums)
-    others = [over_ep(both, 2) for both in sums]
-    returned = []
+    got, crossed = exchange(outgoing_own, halves)
+    owns, sides = [], []
     for local in range(EXP_DEV):
-        if local > 0:
-            crossed, others[0] = lax.optimization_barrier((crossed, others[0]))
-        own = expert(got, crossed, expert_in, expert_out, local)
-        parts = (own[0], over_ep(own[1], 1), others[local])
-        if returned:
-            parts, returned[-1] = lax.optimization_barrier((parts, returned[-1]))
-        returned.append(exchange(lay_out(meta, *parts, n_seq, capacity)))
-    return combine(meta, stream, slots, returned, n_seq, n_ep, capacity)
+        if owns:
+            crossed, owns = lax.optimization_barrier((crossed, owns))
+        pair = (made[local][0], halves[local])
+        own, sums = expert(got, crossed, expert_in, expert_out, local, [pair])
+        owns.append(own)
+        sides.append([own[0], over_ep(own[1], 1), over_ep(sums[0], 2)])
+    sides[0], owns = lax.optimization_barrier((sides[0], owns))
+    total, returned = stream, None
+    for local in range(EXP_DEV):
+        laid = lay_out(meta, *sides[local], n_seq, capacity)
+        returned = exchange(laid, total if returned else sides[1:])
+        last = local == EXP_DEV - 1
+        total = combine(meta, total, slots, returned, local, n_seq, n_ep, capacity, BF16 if last else F32)
+    return total
 
 
 def solution(mesh):

time: 186 us -> 172 us (0.925)
  waiting for transfers between devices: 82.7 us -> 70.8 us
  Pallas kernels: 62.1 us -> 59.4 us
    ppermute x12, waiting for transfers between devices: 45 us -> 37.1 us  [over_ep(): return lax.ppermute(x, 'ep', xor_pairs(n_ep, bits)) if bits else x]
    ppermute x24, waiting for transfers between devices: 37.7 us -> 33.7 us  [over_seq(): return lax.ppermute(x, 'seq', xor_pairs(n_seq, bits)) if bits else x]
    pallas_call x8, Pallas kernels: 51.2 us -> 48.1 us  [call(): pl.pallas_call(body, in_specs=[pl.BlockSpec(memory_space=pltpu.SMEM)] + [...]
  transfers between devices with their start and end apart: 36 -> 36, of which waited for: 20 -> 20; matrix products, arithmetic and copies ran while one was open for 0% -> 0% of each run, Pallas kernels for 17% -> 23%
where the time goes in v3:
time: 172 us
  waiting for transfers between devices  70.8 us (41%)
  Pallas kernels  59.4 us (35%)
  starting transfers between devices  36.9 us (21%)
  local copies, waits for them, and re-layouts  2.5 us (1%)
  other arithmetic  1.93 us (1%)
    pallas_call x8, Pallas kernels, call(): pl.pallas_call(body, in_specs=[pl.BlockSpec(memory_space=pltpu.SMEM)] + [...  48.1 us
    ppermute x12, waiting for transfers between devices, over_ep(): return lax.ppermute(x, 'ep', xor_pairs(n_ep, bits)) if bits else x  37.1 us
    ppermute x24, waiting for transfers between devices, over_seq(): return lax.ppermute(x, 'seq', xor_pairs(n_seq, bits)) if bits else x  33.7 us
    ppermute x24, starting transfers between devices, over_seq(): return lax.ppermute(x, 'seq', xor_pairs(n_seq, bits)) if bits else x  21.7 us
    ppermute x12, starting transfers between devices, over_ep(): return lax.ppermute(x, 'ep', xor_pairs(n_ep, bits)) if bits else x  15.2 us
    pallas_call x4, Pallas kernels, expert(): pl.pallas_call(kernel, in_specs=[pl.BlockSpec(memory_space=pltpu.VMEM)] *...  11.2 us
  transfers between devices with their start and end apart: 36, of which 20 were waited for; matrix products, arithmetic and copies ran while one was open for 0% of the time, Pallas kernels for 23%

profile of v3, /device:TPU:0, one launch (start us, length us, event | category | flops | bytes accessed | tf_op | source)
XLA Modules:
  0.0 172.0 jit_solution(7983376558675006217)
XLA Ops:
  1.1 3.1 %collective-permute-start = (bf16[96,768]{1,0:T(8,128)(2,1)S(1)}, bf16[96,768]{1,0:T(8,128)(2,1)S(1)}, u32[]{:S(2)}, u32[]{:S(2)}) collective-permute-start(bf16[96,768]{1,0:T(8,128)(2,1)S(1)} %fusion), channel_id=1, source_target_pairs={{0,1},{1,0},{2,3},{3,2},{4,5},{5,4},{6,7},{7,6},{8,9},{9,8},{10,11... | collective-permute-start | bytes 442376 | tf_op jit(solution)/shard_map/ppermute | solution.py:456
  4.2 2.6 %collective-permute-start.1 = (bf16[96,768]{1,0:T(8,128)(2,1)S(1)}, bf16[96,768]{1,0:T(8,128)(2,1)S(1)}, u32[]{:S(2)}, u32[]{:S(2)}) collective-permute-start(bf16[96,768]{1,0:T(8,128)(2,1)S(1)} %fusion), channel_id=1, source_target_pairs={{0,2},{1,3},{2,0},{3,1},{4,6},{5,7},{6,4},{7,5},{8,10},{9,11},{10,... | collective-permute-start | bytes 442376 | tf_op jit(solution)/shard_map/ppermute | solution.py:456
  7.1 1.9 %copy-done.1 = bf16[2048,768]{1,0:T(8,128)(2,1)S(1)} copy-done((bf16[2048,768]{1,0:T(8,128)(2,1)S(1)}, bf16[2048,768]{1,0:T(8,128)(2,1)}, u32[]{:S(2)}) %copy-start.1) | copy-done | bytes 3145752
  9.0 7.1 %shard_map.64 = (bf16[64,192]{1,0:T(8,128)(2,1)S(1)}, s32[512,1]{1,0:T(8,128)S(1)}, bf16[26,2048,256]{2,1,0:T(8,128)(2,1)}) custom-call(s32[2]{0:T(128)S(1)} %pad_add_fusion.refs_0_, bf16[768,768]{1,0:T(8,128)(2,1)S(1)} %pad_maximum_fusion.refs_1_, s32[512,1]{1,0:T(8,128)S(1)} %copy.8.refs_2_, bf16[2048,768]{1,0:T(8,128)(2,1)S(1)} %copy-done.1), custom_call_target="tpu_custom_call" | custom-call | flops 8049999872 | bytes 1048576 | tf_op jit(solution)/shard_map/pallas_call | solution.py:122
  16.2 1.6 collective-permute-start.3
  17.8 1.5 collective-permute-start.4
  20.2 4.7 %collective-permute-done.2 = bf16[96,768]{1,0:T(8,128)(2,1)S(1)} collective-permute-done((bf16[96,768]{1,0:T(8,128)(2,1)S(1)}, bf16[96,768]{1,0:T(8,128)(2,1)S(1)}, u32[]{:S(2)}, u32[]{:S(2)}) %collective-permute-start.2) | collective-permute-done | bytes 147488 | tf_op jit(solution)/shard_map/ppermute | solution.py:456
  24.9 1.9 %collective-permute-done.4 = bf16[112,768]{1,0:T(8,128)(2,1)S(1)} collective-permute-done((bf16[112,768]{1,0:T(8,128)(2,1)S(1)}, bf16[112,768]{1,0:T(8,128)(2,1)S(1)}, u32[]{:S(2)}, u32[]{:S(2)}) %collective-permute-start.4) | collective-permute-done | bytes 172064 | tf_op jit(solution)/shard_map/ppermute | solution.py:453
  27.1 2.1 %collective-permute-done.9.refs_2_ = bf16[4,112,768]{2,1,0:T(8,128)(2,1)S(1)} collective-permute-done((bf16[4,112,768]{2,1,0:T(8,128)(2,1)S(1)}, bf16[4,112,768]{2,1,0:T(8,128)(2,1)S(1)}, u32[]{:S(2)}, u32[]{:S(2)}) %collective-permute-start.9) | collective-permute-done | bytes 688160 | tf_op jit(solution)/shard_map/ppermute | solution.py:453
  31.8 1.6 collective-permute-start.8
  35.4 9.0 %shard_map.65 = (bf16[192,768]{1,0:T(8,128)(2,1)S(1)}, bf16[26,2048,256]{2,1,0:T(8,128)(2,1)}) custom-call(s32[2]{0:T(128)S(1)} %pad_add_fusion.refs_0_, bf16[4,112,768]{2,1,0:T(8,128)(2,1)S(1)} %pad_maximum_fusion.4.refs_1_, bf16[4,112,768]{2,1,0:T(8,128)(2,1)S(1)} %collective-permute-done.9.refs_2_, ...), custom_call_target="tpu_custom_call", output_to_operand_aliasing={{1}: (3, {})} | custom-call | flops 9200000000 | bytes 1048576 | tf_op jit(solution)/shard_map/pallas_call | solution.py:122
  46.1 2.8 %collective-permute-done.13.refs_2_ = bf16[4,192,768]{2,1,0:T(8,128)(2,1)S(1)} collective-permute-done((bf16[4,192,768]{2,1,0:T(8,128)(2,1)S(1)}, bf16[4,192,768]{2,1,0:T(8,128)(2,1)S(1)}, u32[]{:S(2)}, u32[]{:S(2)}) %collective-permute-start.13) | collective-permute-done | bytes 1179680 | tf_op jit(solution)/shard_map/ppermute | solution.py:453
  48.9 15.1 %shard_map.66 = (f32[2,192,192]{2,1,0:T(8,128)S(1)}, bf16[2,2,2,32,768]{4,3,2,1,0:T(8,128)(2,1)S(1)}, bf16[2,2,2,32,768]{4,3,2,1,0:T(8,128)(2,1)S(1)}, bf16[2,2,...) custom-call(s32[2]{0:T(128)S(1)} %pad_add_fusion.refs_0_, ...), custom_call_target="tpu_custom_call" | custom-call | flops 14949999616 | bytes 1048576 | tf_op jit(solution)/shard_map/pallas_call | solution.py:122
  67.6 12.5 %shard_map.67 = (bf16[512,768]{1,0:T(8,128)(2,1)S(1)}, bf16[2,2,2,32,768]{4,3,2,1,0:T(8,128)(2,1)S(1)}, bf16[2,2,2,32,768]{4,3,2,1,0:T(8,128)(2,1)S(1)}, bf16[2,...) custom-call(s32[2]{0:T(128)S(1)} %pad_add_fusion.refs_0_, ...), custom_call_target="tpu_custom_call" | custom-call | flops 14949999616 | bytes 1048576 | tf_op jit(solution)/shard_map/pallas_call | solution.py:122
  80.1 4.2 %collective-permute-done.15.refs_2_ = bf16[2,2,2,32,768]{4,3,2,1,0:T(8,128)(2,1)S(1)} collective-permute-done((bf16[2,2,2,32,768]{4,3,2,1,0:T(8,128)(2,1)S(1)}, bf16[2,2,2,32,768]{4,3,2,1,0:T(8,128)(2,1)S(1)}, u32[]{:S(2)}, u32[]{:S(2)}) %collective-permute-start.15) | collective-permute-done | bytes 393248 | tf_op jit(solution)/shard_map/ppermute | solution.py:453
  86.6 1.6 collective-permute-start.19
  88.2 2.7 %shard_map.68 = (bf16[256,768]{1,0:T(8,128)(2,1)S(1)}, bf16[256,768]{1,0:T(8,128)(2,1)S(1)}) custom-call(bf16[2,2,2,32,768]{4,3,2,1,0:T(8,128)(2,1)S(1)} %get-tuple-element.131.refs_0_, bf16[2,2,2,32,768]{4,3,2,1,0:T(8,128)(2,1)S(1)} %collective-permute-done.14.refs_1_, bf16[2,2,2,32,768]{4,3,2,1,0:T(8,128)(2,1)S(1)} %collective-permute-done.15.refs_2_, ...), custom_call_target="tpu_custom_call" | custom-call | flops 3449999872 | bytes 1048576 | tf_op jit(solution)/shard_map/pallas_call | solution.py:395
  91.0 2.7 %shard_map.69 = (bf16[256,768]{1,0:T(8,128)(2,1)S(1)}, bf16[256,768]{1,0:T(8,128)(2,1)S(1)}) custom-call(bf16[2,2,2,32,768]{4,3,2,1,0:T(8,128)(2,1)S(1)} %get-tuple-element.131.refs_0_, bf16[2,2,2,32,768]{4,3,2,1,0:T(8,128)(2,1)S(1)} %collective-permute-done.14.refs_1_, bf16[2,2,2,32,768]{4,3,2,1,0:T(8,128)(2,1)S(1)} %collective-permute-done.15.refs_2_, ...), custom_call_target="tpu_custom_call" | custom-call | flops 3449999872 | bytes 1048576 | tf_op jit(solution)/shard_map/pallas_call | solution.py:395
  97.4 8.0 %collective-permute-done.19.refs_3_ = bf16[2,2,2,32,768]{4,3,2,1,0:T(8,128)(2,1)S(1)} collective-permute-done((bf16[2,2,2,32,768]{4,3,2,1,0:T(8,128)(2,1)S(1)}, bf16[2,2,2,32,768]{4,3,2,1,0:T(8,128)(2,1)S(1)}, u32[]{:S(2)}, u32[]{:S(2)}) %collective-permute-start.19) | collective-permute-done | bytes 393248 | tf_op jit(solution)/shard_map/ppermute | solution.py:453
  105.8 7.0 %collective-permute-done.21.refs_8_ = bf16[256,768]{1,0:T(8,128)(2,1)S(1)} collective-permute-done((bf16[256,768]{1,0:T(8,128)(2,1)S(1)}, bf16[256,768]{1,0:T(8,128)(2,1)S(1)}, u32[]{:S(2)}, u32[]{:S(2)}) %collective-permute-start.21) | collective-permute-done | bytes 393248 | tf_op jit(solution)/shard_map/ppermute | solution.py:456
  113.1 2.3 %collective-permute-done.23.refs_4_ = bf16[4,2,2,32,768]{4,3,2,1,0:T(8,128)(2,1)S(1)} collective-permute-done((bf16[4,2,2,32,768]{4,3,2,1,0:T(8,128)(2,1)S(1)}, bf16[4,2,2,32,768]{4,3,2,1,0:T(8,128)(2,1)S(1)}, u32[]{:S(2)}, u32[]{:S(2)}) %collective-permute-start.23) | collective-permute-done | bytes 786464 | tf_op jit(solution)/shard_map/ppermute | solution.py:453
  115.4 2.9 %shard_map.70 = (bf16[256,768]{1,0:T(8,128)(2,1)S(1)}, bf16[256,768]{1,0:T(8,128)(2,1)S(1)}, bf16[256,768]{1,0:T(8,128)(2,1)S(1)}) custom-call(bf16[2,2,2,32,768]{4,3,2,1,0:T(8,128)(2,1)S(1)} %get-tuple-element.139.refs_0_, bf16[2,2,2,32,768]{4,3,2,1,0:T(8,128)(2,1)S(1)} %collective-permute-done.17.refs_1_, ...), custom_call_target="tpu_custom_call" | custom-call | flops 3449999872 | bytes 1048576 | tf_op jit(solution)/shard_map/pallas_call | solution.py:395
  119.0 2.4 %collective-permute-start.25 = (bf16[256,768]{1,0:T(8,128)(2,1)S(1)}, bf16[256,768]{1,0:T(8,128)(2,1)S(1)}, u32[]{:S(2)}, u32[]{:S(2)}) collective-permute-start(bf16[256,768]{1,0:T(8,128)(2,1)S(1)} %get-tuple-element.146), channel_id=1, source_target_pairs={{0,2},{1,3},{2,0},{3,1},{4,6},{5,7},{6,4},{7,5},{8,10},{9,11},{10,... | collective-permute-start | bytes 1179656 | tf_op jit(solution)/shard_map/ppermute | solution.py:456
  121.3 2.9 %shard_map.71 = (bf16[256,768]{1,0:T(8,128)(2,1)S(1)}, bf16[256,768]{1,0:T(8,128)(2,1)S(1)}, bf16[256,768]{1,0:T(8,128)(2,1)S(1)}) custom-call(bf16[2,2,2,32,768]{4,3,2,1,0:T(8,128)(2,1)S(1)} %get-tuple-element.139.refs_0_, bf16[2,2,2,32,768]{4,3,2,1,0:T(8,128)(2,1)S(1)} %collective-permute-done.17.refs_1_, ...), custom_call_target="tpu_custom_call" | custom-call | flops 3449999872 | bytes 1048576 | tf_op jit(solution)/shard_map/pallas_call | solution.py:395
  124.2 1.6 collective-permute-start.29
  126.2 13.5 %collective-permute-done.24.refs_2_ = bf16[256,768]{1,0:T(8,128)(2,1)S(1)} collective-permute-done((bf16[256,768]{1,0:T(8,128)(2,1)S(1)}, bf16[256,768]{1,0:T(8,128)(2,1)S(1)}, u32[]{:S(2)}, u32[]{:S(2)}) %collective-permute-start.24) | collective-permute-done | bytes 393248 | tf_op jit(solution)/shard_map/ppermute | solution.py:456
  144.0 10.7 %collective-permute-done.29.refs_2_ = bf16[256,768]{1,0:T(8,128)(2,1)S(1)} collective-permute-done((bf16[256,768]{1,0:T(8,128)(2,1)S(1)}, bf16[256,768]{1,0:T(8,128)(2,1)S(1)}, u32[]{:S(2)}, u32[]{:S(2)}) %collective-permute-start.29) | collective-permute-done | bytes 393248 | tf_op jit(solution)/shard_map/ppermute | solution.py:456
  157.6 1.6 collective-permute-start.34
  160.3 3.0 %collective-permute-done.32.refs_4_ = bf16[2,64,768]{2,1,0:T(8,128)(2,1)S(1)} collective-permute-done((bf16[2,64,768]{2,1,0:T(8,128)(2,1)S(1)}, bf16[2,64,768]{2,1,0:T(8,128)(2,1)S(1)}, u32[]{:S(2)}, u32[]{:S(2)}) %collective-permute-start.32) | collective-permute-done | bytes 196640 | tf_op jit(solution)/shard_map/ppermute | solution.py:453
  164.2 3.8 %collective-permute-done.34.refs_6_ = bf16[2,64,768]{2,1,0:T(8,128)(2,1)S(1)} collective-permute-done((bf16[2,64,768]{2,1,0:T(8,128)(2,1)S(1)}, bf16[2,64,768]{2,1,0:T(8,128)(2,1)S(1)}, u32[]{:S(2)}, u32[]{:S(2)}) %collective-permute-start.34) | collective-permute-done | bytes 196640 | tf_op jit(solution)/shard_map/ppermute | solution.py:453
  168.2 1.7 collective-permute-done.35.refs_7_
  169.9 2.0 %shard_map.75 = bf16[512,768]{1,0:T(8,128)(2,1)} custom-call(s32[2]{0:T(128)S(1)} %pad_add_fusion.refs_0_, f32[512,768]{1,0:T(8,128)S(1)} %shard_map.73.refs_1_, s32[512,1]{1,0:T(8,128)S(1)} %get-tuple-element.114.refs_2_, bf16[2,64,768]{2,1,0:T(8,128)(2,1)S(1)} %get-tuple-element.167.refs_3_, bf16[2,64,768]{2,1,0:T(8,128)(2,1)S(1)} %collective-permute-done.32.refs_4_, ...), custom_call_target="tpu_custom_call" | custom-call | flops 1724999936 | bytes 1048576 | tf_op jit(solution)/shard_map/pallas_call | solution.py:122
  (108 shorter events, 29.4 us)
Async XLA Ops:
  1.1 15.0 %collective-permute-start = (bf16[96,768]{1,0:T(8,128)(2,1)S(1)}, bf16[96,768]{1,0:T(8,128)(2,1)S(1)}, u32[]{:S(2)}, u32[]{:S(2)}) collective-permute-start(bf16[96,768]{1,0:T(8,128)(2,1)S(1)} %fusion), channel_id=1, source_target_pairs={{0,1},{1,0},{2,3},{3,2},{4,5},{5,4},{6,7},{7,6},{8,9},{9,8},{10,11... | collective-permute-start | bytes 442376 | tf_op jit(solution)/shard_map/ppermute | solution.py:456
  4.2 11.9 %collective-permute-start.1 = (bf16[96,768]{1,0:T(8,128)(2,1)S(1)}, bf16[96,768]{1,0:T(8,128)(2,1)S(1)}, u32[]{:S(2)}, u32[]{:S(2)}) collective-permute-start(bf16[96,768]{1,0:T(8,128)(2,1)S(1)} %fusion), channel_id=1, source_target_pairs={{0,2},{1,3},{2,0},{3,1},{4,6},{5,7},{6,4},{7,5},{8,10},{9,11},{10,... | collective-permute-start | bytes 442376 | tf_op jit(solution)/shard_map/ppermute | solution.py:456
  16.2 8.7 %collective-permute-start.3 = (bf16[112,768]{1,0:T(8,128)(2,1)S(1)}, bf16[112,768]{1,0:T(8,128)(2,1)S(1)}, u32[]{:S(2)}, u32[]{:S(2)}) collective-permute-start(bf16[112,768]{1,0:T(8,128)(2,1)S(1)} %constant_dynamic-update-slice_fusion), channel_id=1, source_target_pairs={{0,8},{4,12},{8,0},{12,4},{16,24},{20,28},{24,16},{28,20},{1,9},{5... | collective-permute-start | bytes 516104 | tf_op jit(solution)/shard_map/ppermute | solution.py:453
  17.8 9.1 %collective-permute-start.4 = (bf16[112,768]{1,0:T(8,128)(2,1)S(1)}, bf16[112,768]{1,0:T(8,128)(2,1)S(1)}, u32[]{:S(2)}, u32[]{:S(2)}) collective-permute-start(bf16[112,768]{1,0:T(8,128)(2,1)S(1)} %constant_dynamic-update-slice_fusion), channel_id=1, source_target_pairs={{0,16},{4,20},{8,24},{12,28},{16,0},{20,4},{24,8},{28,12},{1,17},{... | collective-permute-start | bytes 516104 | tf_op jit(solution)/shard_map/ppermute | solution.py:453
  19.3 7.6 %collective-permute-start.5 = (bf16[112,768]{1,0:T(8,128)(2,1)S(1)}, bf16[112,768]{1,0:T(8,128)(2,1)S(1)}, u32[]{:S(2)}, u32[]{:S(2)}) collective-permute-start(bf16[112,768]{1,0:T(8,128)(2,1)S(1)} %constant_dynamic-update-slice_fusion), channel_id=1, source_target_pairs={{0,24},{4,28},{8,16},{12,20},{16,8},{20,12},{24,0},{28,4},{1,25},{... | collective-permute-start | bytes 516104 | tf_op jit(solution)/shard_map/ppermute | solution.py:453
  19.8 5.1 %collective-permute-start.2 = (bf16[96,768]{1,0:T(8,128)(2,1)S(1)}, bf16[96,768]{1,0:T(8,128)(2,1)S(1)}, u32[]{:S(2)}, u32[]{:S(2)}) collective-permute-start(bf16[96,768]{1,0:T(8,128)(2,1)S(1)} %collective-permute-done.1), channel_id=1, source_target_pairs={{0,1},{1,0},{2,3},{3,2},{4,5},{5,4},{6,7},{7,6},{8,9},{9,8},{10,11... | collective-permute-start | bytes 442376 | tf_op jit(solution)/shard_map/ppermute | solution.py:456
  29.4 5.2 %collective-permute-start.11 = (bf16[72,192]{1,0:T(8,128)(2,1)S(1)}, bf16[72,192]{1,0:T(8,128)(2,1)S(1)}, u32[]{:S(2)}, u32[]{:S(2)}) collective-permute-start(bf16[72,192]{1,0:T(8,128)(2,1)S(1)} %fusion.2.refs_3_), channel_id=1, source_target_pairs={{0,2},{1,3},{2,0},{3,1},{4,6},{5,7},{6,4},{7,5},{8,10},{9,11},{10,... | collective-permute-start | bytes 82952 | tf_op jit(solution)/shard_map/ppermute | solution.py:456
  29.8 14.6 %collective-permute-start.6 = (bf16[192,768]{1,0:T(8,128)(2,1)S(1)}, bf16[192,768]{1,0:T(8,128)(2,1)S(1)}, u32[]{:S(2)}, u32[]{:S(2)}) collective-permute-start(bf16[192,768]{1,0:T(8,128)(2,1)S(1)} %constant_dynamic-update-slice_fusion.2), channel_id=1, source_target_pairs={{0,8},{4,12},{8,0},{12,4},{16,24},{20,28},{24,16},{28,20},{1,9},{5... | collective-permute-start | bytes 884744 | tf_op jit(solution)/shard_map/ppermute | solution.py:453
  31.0 13.4 %collective-permute-start.7 = (bf16[192,768]{1,0:T(8,128)(2,1)S(1)}, bf16[192,768]{1,0:T(8,128)(2,1)S(1)}, u32[]{:S(2)}, u32[]{:S(2)}) collective-permute-start(bf16[192,768]{1,0:T(8,128)(2,1)S(1)} %constant_dynamic-update-slice_fusion.2), channel_id=1, source_target_pairs={{0,16},{4,20},{8,24},{12,28},{16,0},{20,4},{24,8},{28,12},{1,17},{... | collective-permute-start | bytes 884744 | tf_op jit(solution)/shard_map/ppermute | solution.py:453
  31.8 14.0 %collective-permute-start.8 = (bf16[192,768]{1,0:T(8,128)(2,1)S(1)}, bf16[192,768]{1,0:T(8,128)(2,1)S(1)}, u32[]{:S(2)}, u32[]{:S(2)}) collective-permute-start(bf16[192,768]{1,0:T(8,128)(2,1)S(1)} %constant_dynamic-update-slice_fusion.2), channel_id=1, source_target_pairs={{0,24},{4,28},{8,16},{12,20},{16,8},{20,12},{24,0},{28,4},{1,25},{... | collective-permute-start | bytes 884744 | tf_op jit(solution)/shard_map/ppermute | solution.py:453
  33.4 12.4 %collective-permute-start.10 = (bf16[72,192]{1,0:T(8,128)(2,1)S(1)}, bf16[72,192]{1,0:T(8,128)(2,1)S(1)}, u32[]{:S(2)}, u32[]{:S(2)}) collective-permute-start(bf16[72,192]{1,0:T(8,128)(2,1)S(1)} %fusion.2.refs_3_), channel_id=1, source_target_pairs={{0,1},{1,0},{2,3},{3,2},{4,5},{5,4},{6,7},{7,6},{8,9},{9,8},{10,11... | collective-permute-start | bytes 82952 | tf_op jit(solution)/shard_map/ppermute | solution.py:456
  34.6 11.2 %collective-permute-start.12 = (bf16[72,192]{1,0:T(8,128)(2,1)S(1)}, bf16[72,192]{1,0:T(8,128)(2,1)S(1)}, u32[]{:S(2)}, u32[]{:S(2)}) collective-permute-start(bf16[72,192]{1,0:T(8,128)(2,1)S(1)} %collective-permute-done.11.refs_5_), channel_id=1, source_target_pairs={{0,1},{1,0},{2,3},{3,2},{4,5},{5,4},{6,7},{7,6},{8,9},{9,8},{10,11... | collective-permute-start | bytes 82952 | tf_op jit(solution)/shard_map/ppermute | solution.py:456
  64.0 16.1 %collective-permute-start.14 = (bf16[2,2,2,32,768]{4,3,2,1,0:T(8,128)(2,1)S(1)}, bf16[2,2,2,32,768]{4,3,2,1,0:T(8,128)(2,1)S(1)}, u32[]{:S(2)}, u32[]{:S(2)}) collective-permute-start(bf16[2,2,2,32,768]{4,3,2,1,0:T(8,128)(2,1)S(1)} %get-tuple-element.120), channel_id=1, source_target_pairs={{0,8},{4,12},{8,0},{12,4},{16,24},{20,28},{24,16},{28,20},{1,9},{5... | collective-permute-start | bytes 1179656 | tf_op jit(solution)/shard_map/ppermute | solution.py:453
  65.0 19.3 %collective-permute-start.15 = (bf16[2,2,2,32,768]{4,3,2,1,0:T(8,128)(2,1)S(1)}, bf16[2,2,2,32,768]{4,3,2,1,0:T(8,128)(2,1)S(1)}, u32[]{:S(2)}, u32[]{:S(2)}) collective-permute-start(bf16[2,2,2,32,768]{4,3,2,1,0:T(8,128)(2,1)S(1)} %get-tuple-element.121), channel_id=1, source_target_pairs={{0,16},{4,20},{8,24},{12,28},{16,0},{20,4},{24,8},{28,12},{1,17},{... | collective-permute-start | bytes 1179656 | tf_op jit(solution)/shard_map/ppermute | solution.py:453
  66.4 17.9 %collective-permute-start.16 = (bf16[2,2,2,32,768]{4,3,2,1,0:T(8,128)(2,1)S(1)}, bf16[2,2,2,32,768]{4,3,2,1,0:T(8,128)(2,1)S(1)}, u32[]{:S(2)}, u32[]{:S(2)}) collective-permute-start(bf16[2,2,2,32,768]{4,3,2,1,0:T(8,128)(2,1)S(1)} %get-tuple-element.122), channel_id=1, source_target_pairs={{0,24},{4,28},{8,16},{12,20},{16,8},{20,12},{24,0},{28,4},{1,25},{... | collective-permute-start | bytes 1179656 | tf_op jit(solution)/shard_map/ppermute | solution.py:453
  84.5 3.6 %collective-permute-start.20 = (bf16[4,2,2,32,768]{4,3,2,1,0:T(8,128)(2,1)S(1)}, bf16[4,2,2,32,768]{4,3,2,1,0:T(8,128)(2,1)S(1)}, u32[]{:S(2)}, u32[]{:S(2)}) collective-permute-start(bf16[4,2,2,32,768]{4,3,2,1,0:T(8,128)(2,1)S(1)} %pad_maximum_fusion.2), channel_id=1, source_target_pairs={{0,4},{4,0},{8,12},{12,8},{16,20},{20,16},{24,28},{28,24},{1,5},{5... | collective-permute-start | bytes 2359304 | tf_op jit(solution)/shard_map/ppermute | solution.py:453
  84.6 12.0 %collective-permute-start.17 = (bf16[2,2,2,32,768]{4,3,2,1,0:T(8,128)(2,1)S(1)}, bf16[2,2,2,32,768]{4,3,2,1,0:T(8,128)(2,1)S(1)}, u32[]{:S(2)}, u32[]{:S(2)}) collective-permute-start(bf16[2,2,2,32,768]{4,3,2,1,0:T(8,128)(2,1)S(1)} %get-tuple-element.128), channel_id=1, source_target_pairs={{0,8},{4,12},{8,0},{12,4},{16,24},{20,28},{24,16},{28,20},{1,9},{5... | collective-permute-start | bytes 1179656 | tf_op jit(solution)/shard_map/ppermute | solution.py:453
  85.8 11.6 %collective-permute-start.18 = (bf16[2,2,2,32,768]{4,3,2,1,0:T(8,128)(2,1)S(1)}, bf16[2,2,2,32,768]{4,3,2,1,0:T(8,128)(2,1)S(1)}, u32[]{:S(2)}, u32[]{:S(2)}) collective-permute-start(bf16[2,2,2,32,768]{4,3,2,1,0:T(8,128)(2,1)S(1)} %get-tuple-element.129), channel_id=1, source_target_pairs={{0,16},{4,20},{8,24},{12,28},{16,0},{20,4},{24,8},{28,12},{1,17},{... | collective-permute-start | bytes 1179656 | tf_op jit(solution)/shard_map/ppermute | solution.py:453
  86.6 18.8 %collective-permute-start.19 = (bf16[2,2,2,32,768]{4,3,2,1,0:T(8,128)(2,1)S(1)}, bf16[2,2,2,32,768]{4,3,2,1,0:T(8,128)(2,1)S(1)}, u32[]{:S(2)}, u32[]{:S(2)}) collective-permute-start(bf16[2,2,2,32,768]{4,3,2,1,0:T(8,128)(2,1)S(1)} %get-tuple-element.130), channel_id=1, source_target_pairs={{0,24},{4,28},{8,16},{12,20},{16,8},{20,12},{24,0},{28,4},{1,25},{... | collective-permute-start | bytes 1179656 | tf_op jit(solution)/shard_map/ppermute | solution.py:453
  93.7 12.1 %collective-permute-start.22 = (bf16[256,768]{1,0:T(8,128)(2,1)S(1)}, bf16[256,768]{1,0:T(8,128)(2,1)S(1)}, u32[]{:S(2)}, u32[]{:S(2)}) collective-permute-start(bf16[256,768]{1,0:T(8,128)(2,1)S(1)} %get-tuple-element.138), channel_id=1, source_target_pairs={{0,1},{1,0},{2,3},{3,2},{4,5},{5,4},{6,7},{7,6},{8,9},{9,8},{10,11... | collective-permute-start | bytes 1179656 | tf_op jit(solution)/shard_map/ppermute | solution.py:456
  94.4 18.4 %collective-permute-start.21 = (bf16[256,768]{1,0:T(8,128)(2,1)S(1)}, bf16[256,768]{1,0:T(8,128)(2,1)S(1)}, u32[]{:S(2)}, u32[]{:S(2)}) collective-permute-start(bf16[256,768]{1,0:T(8,128)(2,1)S(1)} %get-tuple-element.135), channel_id=1, source_target_pairs={{0,1},{1,0},{2,3},{3,2},{4,5},{5,4},{6,7},{7,6},{8,9},{9,8},{10,11... | collective-permute-start | bytes 1179656 | tf_op jit(solution)/shard_map/ppermute | solution.py:456
  118.2 21.5 %collective-permute-start.24 = (bf16[256,768]{1,0:T(8,128)(2,1)S(1)}, bf16[256,768]{1,0:T(8,128)(2,1)S(1)}, u32[]{:S(2)}, u32[]{:S(2)}) collective-permute-start(bf16[256,768]{1,0:T(8,128)(2,1)S(1)} %get-tuple-element.145), channel_id=1, source_target_pairs={{0,1},{1,0},{2,3},{3,2},{4,5},{5,4},{6,7},{7,6},{8,9},{9,8},{10,11... | collective-permute-start | bytes 1179656 | tf_op jit(solution)/shard_map/ppermute | solution.py:456
  119.0 20.9 %collective-permute-start.25 = (bf16[256,768]{1,0:T(8,128)(2,1)S(1)}, bf16[256,768]{1,0:T(8,128)(2,1)S(1)}, u32[]{:S(2)}, u32[]{:S(2)}) collective-permute-start(bf16[256,768]{1,0:T(8,128)(2,1)S(1)} %get-tuple-element.146), channel_id=1, source_target_pairs={{0,2},{1,3},{2,0},{3,1},{4,6},{5,7},{6,4},{7,5},{8,10},{9,11},{10,... | collective-permute-start | bytes 1179656 | tf_op jit(solution)/shard_map/ppermute | solution.py:456
  124.2 30.5 %collective-permute-start.29 = (bf16[256,768]{1,0:T(8,128)(2,1)S(1)}, bf16[256,768]{1,0:T(8,128)(2,1)S(1)}, u32[]{:S(2)}, u32[]{:S(2)}) collective-permute-start(bf16[256,768]{1,0:T(8,128)(2,1)S(1)} %get-tuple-element.150), channel_id=1, source_target_pairs={{0,1},{1,0},{2,3},{3,2},{4,5},{5,4},{6,7},{7,6},{8,9},{9,8},{10,11... | collective-permute-start | bytes 1179656 | tf_op jit(solution)/shard_map/ppermute | solution.py:456
  125.8 28.9 %collective-permute-start.30 = (bf16[256,768]{1,0:T(8,128)(2,1)S(1)}, bf16[256,768]{1,0:T(8,128)(2,1)S(1)}, u32[]{:S(2)}, u32[]{:S(2)}) collective-permute-start(bf16[256,768]{1,0:T(8,128)(2,1)S(1)} %get-tuple-element.158), channel_id=1, source_target_pairs={{0,2},{1,3},{2,0},{3,1},{4,6},{5,7},{6,4},{7,5},{8,10},{9,11},{10,... | collective-permute-start | bytes 1179656 | tf_op jit(solution)/shard_map/ppermute | solution.py:456
  140.5 14.3 %collective-permute-start.26 = (bf16[2,64,768]{2,1,0:T(8,128)(2,1)S(1)}, bf16[2,64,768]{2,1,0:T(8,128)(2,1)S(1)}, u32[]{:S(2)}, u32[]{:S(2)}) collective-permute-start(bf16[2,64,768]{2,1,0:T(8,128)(2,1)S(1)} %get-tuple-element.155), channel_id=1, source_target_pairs={{0,8},{4,12},{8,0},{12,4},{16,24},{20,28},{24,16},{28,20},{1,9},{5... | collective-permute-start | bytes 589832 | tf_op jit(solution)/shard_map/ppermute | solution.py:453
  141.9 12.9 %collective-permute-start.27 = (bf16[2,64,768]{2,1,0:T(8,128)(2,1)S(1)}, bf16[2,64,768]{2,1,0:T(8,128)(2,1)S(1)}, u32[]{:S(2)}, u32[]{:S(2)}) collective-permute-start(bf16[2,64,768]{2,1,0:T(8,128)(2,1)S(1)} %get-tuple-element.156), channel_id=1, source_target_pairs={{0,16},{4,20},{8,24},{12,28},{16,0},{20,4},{24,8},{28,12},{1,17},{... | collective-permute-start | bytes 589832 | tf_op jit(solution)/shard_map/ppermute | solution.py:453
  142.7 12.0 %collective-permute-start.28 = (bf16[2,64,768]{2,1,0:T(8,128)(2,1)S(1)}, bf16[2,64,768]{2,1,0:T(8,128)(2,1)S(1)}, u32[]{:S(2)}, u32[]{:S(2)}) collective-permute-start(bf16[2,64,768]{2,1,0:T(8,128)(2,1)S(1)} %get-tuple-element.157), channel_id=1, source_target_pairs={{0,24},{4,28},{8,16},{12,20},{16,8},{20,12},{24,0},{28,4},{1,25},{... | collective-permute-start | bytes 589832 | tf_op jit(solution)/shard_map/ppermute | solution.py:453
  154.9 4.3 %collective-permute-start.31 = (bf16[4,64,768]{2,1,0:T(8,128)(2,1)S(1)}, bf16[4,64,768]{2,1,0:T(8,128)(2,1)S(1)}, u32[]{:S(2)}, u32[]{:S(2)}) collective-permute-start(bf16[4,64,768]{2,1,0:T(8,128)(2,1)S(1)} %pad_maximum_fusion.5), channel_id=1, source_target_pairs={{0,4},{4,0},{8,12},{12,8},{16,20},{20,16},{24,28},{28,24},{1,5},{5... | collective-permute-start | bytes 1179656 | tf_op jit(solution)/shard_map/ppermute | solution.py:453
  155.6 7.8 %collective-permute-start.32 = (bf16[2,64,768]{2,1,0:T(8,128)(2,1)S(1)}, bf16[2,64,768]{2,1,0:T(8,128)(2,1)S(1)}, u32[]{:S(2)}, u32[]{:S(2)}) collective-permute-start(bf16[2,64,768]{2,1,0:T(8,128)(2,1)S(1)} %get-tuple-element.164), channel_id=1, source_target_pairs={{0,8},{4,12},{8,0},{12,4},{16,24},{20,28},{24,16},{28,20},{1,9},{5... | collective-permute-start | bytes 589832 | tf_op jit(solution)/shard_map/ppermute | solution.py:453
  156.8 7.4 %collective-permute-start.33 = (bf16[2,64,768]{2,1,0:T(8,128)(2,1)S(1)}, bf16[2,64,768]{2,1,0:T(8,128)(2,1)S(1)}, u32[]{:S(2)}, u32[]{:S(2)}) collective-permute-start(bf16[2,64,768]{2,1,0:T(8,128)(2,1)S(1)} %get-tuple-element.165), channel_id=1, source_target_pairs={{0,16},{4,20},{8,24},{12,28},{16,0},{20,4},{24,8},{28,12},{1,17},{... | collective-permute-start | bytes 589832 | tf_op jit(solution)/shard_map/ppermute | solution.py:453
  157.6 10.4 %collective-permute-start.34 = (bf16[2,64,768]{2,1,0:T(8,128)(2,1)S(1)}, bf16[2,64,768]{2,1,0:T(8,128)(2,1)S(1)}, u32[]{:S(2)}, u32[]{:S(2)}) collective-permute-start(bf16[2,64,768]{2,1,0:T(8,128)(2,1)S(1)} %get-tuple-element.166), channel_id=1, source_target_pairs={{0,24},{4,28},{8,16},{12,20},{16,8},{20,12},{24,0},{28,4},{1,25},{... | collective-permute-start | bytes 589832 | tf_op jit(solution)/shard_map/ppermute | solution.py:453
  (12 other events, 150.2 us)

commit v4 on v3

--- a/solution.py
+++ b/solution.py
@@ -375,13 +375,18 @@
     _, blocks, _, capacity, model = got[0].shape
     count = len(got)
     span = 2 * count * capacity
+    flat = [a for pair in pairs for a in pair]
 
     def kernel(*refs):
         got_refs, (crossed_ref, w1, w2) = refs[:count], refs[count : count + 3]
-        pair_refs, out_refs = refs[count + 3 : count + 3 + 2 * len(pairs)], refs[count + 3 + 2 * len(pairs) :]
-        for n in range(len(pairs)):
-            both = pair_refs[2 * n][...].astype(F32) + pair_refs[2 * n + 1][...].astype(F32)
-            out_refs[blocks + n][...] = both.astype(BF16)
+        pair_refs, out_refs = list(refs[count + 3 : count + 3 + len(flat)]), refs[count + 3 + len(flat) :]
+        for n, (kept, *pieces) in enumerate(pairs):
+            kept_ref, first = pair_refs.pop(0), 0
+            for piece in pieces:
+                at = slice(first, first + piece.shape[0])
+                both = kept_ref[at, :].astype(F32) + pair_refs.pop(0)[...].astype(F32)
+                out_refs[blocks + n][at, :] = both.astype(BF16)
+                first += piece.shape[0]
         pieces = []
         for n in range(blocks):
             for i in range(count):
@@ -391,7 +396,6 @@
         for n in range(blocks):
             out_refs[n][...] = made[n * span : (n + 1) * span]
 
-    flat = [a for pair in pairs for a in pair]
     out = pl.pallas_call(
         kernel,
         in_specs=[pl.BlockSpec(memory_space=pltpu.VMEM)] * (count + 3 + len(flat)),
@@ -456,7 +460,7 @@
         return lax.ppermute(x, "ep", xor_pairs(n_ep, bits)) if bits else x
 
     def exchange(outgoing, after=()):
-        got = [over_seq(out, 2 * i) for i, out in enumerate(outgoing)]
+        got = [over_seq(out, 2 * i) for i, out in reversed(list(enumerate(outgoing)))][::-1]
         got, after = lax.optimization_barrier((got, after))
         return got, over_seq(jnp.stack([g[1] for g in got]), 1)
 
@@ -480,7 +484,7 @@
 
     def gather_layer(pieces):
         first = jnp.concatenate(pieces, axis=0)
-        return [over_seq(first, bits) for bits in range(0, SPLIT, 2)]
+        return [over_seq(first, bits) for bits in reversed(range(0, SPLIT, 2))][::-1]
 
     early = gather_layer([along[1], own_sum.reshape(-1, model)])
     later = [along[m] for m in range(2, n_ep)]
@@ -527,13 +531,14 @@
         if made:
             crossed, made = lax.optimization_barrier((crossed, made))
         made.append(expert(got, crossed, expert_in, expert_out, local)[0])
-        halves.append(over_ep(made[-1][1], 1))
-    got, crossed = exchange(outgoing_own, halves)
+        cuts = jnp.split(made[-1][1], 1 + (local > 0))
+        halves.append([over_ep(piece, 1) for piece in cuts])
+    got, crossed = exchange(outgoing_own, ([half[0] for half in halves], made))
     owns, sides = [], []
     for local in range(EXP_DEV):
         if owns:
             crossed, owns = lax.optimization_barrier((crossed, owns))
-        pair = (made[local][0], halves[local])
+        pair = (made[local][0], *halves[local])
         own, sums = expert(got, crossed, expert_in, expert_out, local, [pair])
         owns.append(own)
         sides.append([own[0], over_ep(own[1], 1), over_ep(sums[0], 2)])

time: 172 us -> 165 us (0.959)
  waiting for transfers between devices: 70.8 us -> 62.8 us
    ppermute x12 -> x13, waiting for transfers between devices: 37.1 us -> 29.9 us  [over_ep(): return lax.ppermute(x, 'ep', xor_pairs(n_ep, bits)) if bits else x]
    ppermute x12 -> x13, starting transfers between devices: 15.2 us -> 16.1 us  [over_ep(): return lax.ppermute(x, 'ep', xor_pairs(n_ep, bits)) if bits else x]
  transfers between devices with their start and end apart: 36 -> 37, of which waited for: 20 -> 19; matrix products, arithmetic and copies ran while one was open for 0% -> 0% of each run, Pallas kernels for 23% -> 26%
where the time goes in v4:
time: 165 us
  waiting for transfers between devices  62.8 us (38%)
  Pallas kernels  59.4 us (36%)
  starting transfers between devices  37.9 us (23%)
  local copies, waits for them, and re-layouts  2.52 us (2%)
  other arithmetic  1.93 us (1%)
    pallas_call x8, Pallas kernels, call(): pl.pallas_call(body, in_specs=[pl.BlockSpec(memory_space=pltpu.SMEM)] + [...  48.2 us
    ppermute x24, waiting for transfers between devices, over_seq(): return lax.ppermute(x, 'seq', xor_pairs(n_seq, bits)) if bits else x  32.9 us
    ppermute x13, waiting for transfers between devices, over_ep(): return lax.ppermute(x, 'ep', xor_pairs(n_ep, bits)) if bits else x  29.9 us
    ppermute x24, starting transfers between devices, over_seq(): return lax.ppermute(x, 'seq', xor_pairs(n_seq, bits)) if bits else x  21.7 us
    ppermute x13, starting transfers between devices, over_ep(): return lax.ppermute(x, 'ep', xor_pairs(n_ep, bits)) if bits else x  16.1 us
    pallas_call x4, Pallas kernels, expert(): pl.pallas_call(kernel, in_specs=[pl.BlockSpec(memory_space=pltpu.VMEM)] *...  11.2 us
  transfers between devices with their start and end apart: 37, of which 19 were waited for; matrix products, arithmetic and copies ran while one was open for 0% of the time, Pallas kernels for 26%

profile of v4, /device:TPU:0, one launch (start us, length us, event | category | flops | bytes accessed | tf_op | source)
XLA Modules:
  0.0 165.0 jit_solution(5303345860991115818)
XLA Ops:
  1.1 3.1 %collective-permute-start = (bf16[96,768]{1,0:T(8,128)(2,1)S(1)}, bf16[96,768]{1,0:T(8,128)(2,1)S(1)}, u32[]{:S(2)}, u32[]{:S(2)}) collective-permute-start(bf16[96,768]{1,0:T(8,128)(2,1)S(1)} %fusion), channel_id=1, source_target_pairs={{0,1},{1,0},{2,3},{3,2},{4,5},{5,4},{6,7},{7,6},{8,9},{9,8},{10,11... | collective-permute-start | bytes 442376 | tf_op jit(solution)/shard_map/ppermute | solution.py:460
  4.2 2.6 %collective-permute-start.1 = (bf16[96,768]{1,0:T(8,128)(2,1)S(1)}, bf16[96,768]{1,0:T(8,128)(2,1)S(1)}, u32[]{:S(2)}, u32[]{:S(2)}) collective-permute-start(bf16[96,768]{1,0:T(8,128)(2,1)S(1)} %fusion), channel_id=1, source_target_pairs={{0,2},{1,3},{2,0},{3,1},{4,6},{5,7},{6,4},{7,5},{8,10},{9,11},{10,... | collective-permute-start | bytes 442376 | tf_op jit(solution)/shard_map/ppermute | solution.py:460
  7.1 1.9 %copy-done.1 = bf16[2048,768]{1,0:T(8,128)(2,1)S(1)} copy-done((bf16[2048,768]{1,0:T(8,128)(2,1)S(1)}, bf16[2048,768]{1,0:T(8,128)(2,1)}, u32[]{:S(2)}) %copy-start.1) | copy-done | bytes 3145752
  9.0 7.1 %shard_map.64 = (bf16[64,192]{1,0:T(8,128)(2,1)S(1)}, s32[512,1]{1,0:T(8,128)S(1)}, bf16[26,2048,256]{2,1,0:T(8,128)(2,1)}) custom-call(s32[2]{0:T(128)S(1)} %pad_add_fusion.refs_0_, bf16[768,768]{1,0:T(8,128)(2,1)S(1)} %pad_maximum_fusion.refs_1_, s32[512,1]{1,0:T(8,128)S(1)} %copy.8.refs_2_, bf16[2048,768]{1,0:T(8,128)(2,1)S(1)} %copy-done.1), custom_call_target="tpu_custom_call" | custom-call | flops 8049999872 | bytes 1048576 | tf_op jit(solution)/shard_map/pallas_call | solution.py:122
  16.2 1.6 collective-permute-start.3
  17.8 1.5 collective-permute-start.4
  20.2 4.7 %collective-permute-done.2 = bf16[96,768]{1,0:T(8,128)(2,1)S(1)} collective-permute-done((bf16[96,768]{1,0:T(8,128)(2,1)S(1)}, bf16[96,768]{1,0:T(8,128)(2,1)S(1)}, u32[]{:S(2)}, u32[]{:S(2)}) %collective-permute-start.2) | collective-permute-done | bytes 147488 | tf_op jit(solution)/shard_map/ppermute | solution.py:460
  24.9 1.9 %collective-permute-done.4 = bf16[112,768]{1,0:T(8,128)(2,1)S(1)} collective-permute-done((bf16[112,768]{1,0:T(8,128)(2,1)S(1)}, bf16[112,768]{1,0:T(8,128)(2,1)S(1)}, u32[]{:S(2)}, u32[]{:S(2)}) %collective-permute-start.4) | collective-permute-done | bytes 172064 | tf_op jit(solution)/shard_map/ppermute | solution.py:457
  27.1 2.1 %collective-permute-done.9.refs_2_ = bf16[4,112,768]{2,1,0:T(8,128)(2,1)S(1)} collective-permute-done((bf16[4,112,768]{2,1,0:T(8,128)(2,1)S(1)}, bf16[4,112,768]{2,1,0:T(8,128)(2,1)S(1)}, u32[]{:S(2)}, u32[]{:S(2)}) %collective-permute-start.9) | collective-permute-done | bytes 688160 | tf_op jit(solution)/shard_map/ppermute | solution.py:457
  31.8 1.6 collective-permute-start.8
  35.4 9.0 %shard_map.65 = (bf16[192,768]{1,0:T(8,128)(2,1)S(1)}, bf16[26,2048,256]{2,1,0:T(8,128)(2,1)}) custom-call(s32[2]{0:T(128)S(1)} %pad_add_fusion.refs_0_, bf16[4,112,768]{2,1,0:T(8,128)(2,1)S(1)} %pad_maximum_fusion.4.refs_1_, bf16[4,112,768]{2,1,0:T(8,128)(2,1)S(1)} %collective-permute-done.9.refs_2_, ...), custom_call_target="tpu_custom_call", output_to_operand_aliasing={{1}: (3, {})} | custom-call | flops 9200000000 | bytes 1048576 | tf_op jit(solution)/shard_map/pallas_call | solution.py:122
  46.1 2.8 %collective-permute-done.13.refs_2_ = bf16[4,192,768]{2,1,0:T(8,128)(2,1)S(1)} collective-permute-done((bf16[4,192,768]{2,1,0:T(8,128)(2,1)S(1)}, bf16[4,192,768]{2,1,0:T(8,128)(2,1)S(1)}, u32[]{:S(2)}, u32[]{:S(2)}) %collective-permute-start.13) | collective-permute-done | bytes 1179680 | tf_op jit(solution)/shard_map/ppermute | solution.py:457
  48.9 15.1 %shard_map.66 = (f32[2,192,192]{2,1,0:T(8,128)S(1)}, bf16[2,2,2,32,768]{4,3,2,1,0:T(8,128)(2,1)S(1)}, bf16[2,2,2,32,768]{4,3,2,1,0:T(8,128)(2,1)S(1)}, bf16[2,2,...) custom-call(s32[2]{0:T(128)S(1)} %pad_add_fusion.refs_0_, ...), custom_call_target="tpu_custom_call" | custom-call | flops 14949999616 | bytes 1048576 | tf_op jit(solution)/shard_map/pallas_call | solution.py:122
  67.6 12.5 %shard_map.67 = (bf16[512,768]{1,0:T(8,128)(2,1)S(1)}, bf16[2,2,2,32,768]{4,3,2,1,0:T(8,128)(2,1)S(1)}, bf16[2,2,2,32,768]{4,3,2,1,0:T(8,128)(2,1)S(1)}, bf16[2,...) custom-call(s32[2]{0:T(128)S(1)} %pad_add_fusion.refs_0_, ...), custom_call_target="tpu_custom_call" | custom-call | flops 14949999616 | bytes 1048576 | tf_op jit(solution)/shard_map/pallas_call | solution.py:122
  80.1 4.2 %collective-permute-done.15.refs_2_ = bf16[2,2,2,32,768]{4,3,2,1,0:T(8,128)(2,1)S(1)} collective-permute-done((bf16[2,2,2,32,768]{4,3,2,1,0:T(8,128)(2,1)S(1)}, bf16[2,2,2,32,768]{4,3,2,1,0:T(8,128)(2,1)S(1)}, u32[]{:S(2)}, u32[]{:S(2)}) %collective-permute-start.15) | collective-permute-done | bytes 393248 | tf_op jit(solution)/shard_map/ppermute | solution.py:457
  86.6 1.6 collective-permute-start.19
  88.2 2.7 %shard_map.68 = (bf16[256,768]{1,0:T(8,128)(2,1)S(1)}, bf16[256,768]{1,0:T(8,128)(2,1)S(1)}) custom-call(bf16[2,2,2,32,768]{4,3,2,1,0:T(8,128)(2,1)S(1)} %get-tuple-element.131.refs_0_, bf16[2,2,2,32,768]{4,3,2,1,0:T(8,128)(2,1)S(1)} %collective-permute-done.14.refs_1_, bf16[2,2,2,32,768]{4,3,2,1,0:T(8,128)(2,1)S(1)} %collective-permute-done.15.refs_2_, ...), custom_call_target="tpu_custom_call" | custom-call | flops 3449999872 | bytes 1048576 | tf_op jit(solution)/shard_map/pallas_call | solution.py:399
  91.7 2.7 %shard_map.69 = (bf16[256,768]{1,0:T(8,128)(2,1)S(1)}, bf16[256,768]{1,0:T(8,128)(2,1)S(1)}) custom-call(bf16[2,2,2,32,768]{4,3,2,1,0:T(8,128)(2,1)S(1)} %get-tuple-element.131.refs_0_, bf16[2,2,2,32,768]{4,3,2,1,0:T(8,128)(2,1)S(1)} %collective-permute-done.14.refs_1_, bf16[2,2,2,32,768]{4,3,2,1,0:T(8,128)(2,1)S(1)} %collective-permute-done.15.refs_2_, ...), custom_call_target="tpu_custom_call" | custom-call | flops 3449999872 | bytes 1048576 | tf_op jit(solution)/shard_map/pallas_call | solution.py:399
  94.5 1.4 collective-permute-start.22
  97.4 8.0 %collective-permute-done.19.refs_3_ = bf16[2,2,2,32,768]{4,3,2,1,0:T(8,128)(2,1)S(1)} collective-permute-done((bf16[2,2,2,32,768]{4,3,2,1,0:T(8,128)(2,1)S(1)}, bf16[2,2,2,32,768]{4,3,2,1,0:T(8,128)(2,1)S(1)}, u32[]{:S(2)}, u32[]{:S(2)}) %collective-permute-start.19) | collective-permute-done | bytes 393248 | tf_op jit(solution)/shard_map/ppermute | solution.py:457
  106.9 1.6 collective-permute-done.23.refs_4_
  108.4 2.9 %shard_map.70 = (bf16[256,768]{1,0:T(8,128)(2,1)S(1)}, bf16[256,768]{1,0:T(8,128)(2,1)S(1)}, bf16[256,768]{1,0:T(8,128)(2,1)S(1)}) custom-call(bf16[2,2,2,32,768]{4,3,2,1,0:T(8,128)(2,1)S(1)} %get-tuple-element.141.refs_0_, bf16[2,2,2,32,768]{4,3,2,1,0:T(8,128)(2,1)S(1)} %collective-permute-done.17.refs_1_, ...), custom_call_target="tpu_custom_call" | custom-call | flops 3449999872 | bytes 1048576 | tf_op jit(solution)/shard_map/pallas_call | solution.py:399
  112.0 2.4 %collective-permute-start.25 = (bf16[256,768]{1,0:T(8,128)(2,1)S(1)}, bf16[256,768]{1,0:T(8,128)(2,1)S(1)}, u32[]{:S(2)}, u32[]{:S(2)}) collective-permute-start(bf16[256,768]{1,0:T(8,128)(2,1)S(1)} %get-tuple-element.147), channel_id=1, source_target_pairs={{0,2},{1,3},{2,0},{3,1},{4,6},{5,7},{6,4},{7,5},{8,10},{9,11},{10,... | collective-permute-start | bytes 1179656 | tf_op jit(solution)/shard_map/ppermute | solution.py:460
  114.4 2.9 %shard_map.71 = (bf16[256,768]{1,0:T(8,128)(2,1)S(1)}, bf16[256,768]{1,0:T(8,128)(2,1)S(1)}, bf16[256,768]{1,0:T(8,128)(2,1)S(1)}) custom-call(bf16[2,2,2,32,768]{4,3,2,1,0:T(8,128)(2,1)S(1)} %get-tuple-element.141.refs_0_, bf16[2,2,2,32,768]{4,3,2,1,0:T(8,128)(2,1)S(1)} %collective-permute-done.17.refs_1_, ...), custom_call_target="tpu_custom_call" | custom-call | flops 3449999872 | bytes 1048576 | tf_op jit(solution)/shard_map/pallas_call | solution.py:399
  117.3 1.6 collective-permute-start.30
  119.5 13.3 %collective-permute-done.24.refs_2_ = bf16[256,768]{1,0:T(8,128)(2,1)S(1)} collective-permute-done((bf16[256,768]{1,0:T(8,128)(2,1)S(1)}, bf16[256,768]{1,0:T(8,128)(2,1)S(1)}, u32[]{:S(2)}, u32[]{:S(2)}) %collective-permute-start.24) | collective-permute-done | bytes 393248 | tf_op jit(solution)/shard_map/ppermute | solution.py:460
  137.1 10.7 %collective-permute-done.30.refs_2_ = bf16[256,768]{1,0:T(8,128)(2,1)S(1)} collective-permute-done((bf16[256,768]{1,0:T(8,128)(2,1)S(1)}, bf16[256,768]{1,0:T(8,128)(2,1)S(1)}, u32[]{:S(2)}, u32[]{:S(2)}) %collective-permute-start.30) | collective-permute-done | bytes 393248 | tf_op jit(solution)/shard_map/ppermute | solution.py:460
  150.7 1.6 collective-permute-start.35
  153.4 3.0 %collective-permute-done.33.refs_4_ = bf16[2,64,768]{2,1,0:T(8,128)(2,1)S(1)} collective-permute-done((bf16[2,64,768]{2,1,0:T(8,128)(2,1)S(1)}, bf16[2,64,768]{2,1,0:T(8,128)(2,1)S(1)}, u32[]{:S(2)}, u32[]{:S(2)}) %collective-permute-start.33) | collective-permute-done | bytes 196640 | tf_op jit(solution)/shard_map/ppermute | solution.py:457
  157.3 3.8 %collective-permute-done.35.refs_6_ = bf16[2,64,768]{2,1,0:T(8,128)(2,1)S(1)} collective-permute-done((bf16[2,64,768]{2,1,0:T(8,128)(2,1)S(1)}, bf16[2,64,768]{2,1,0:T(8,128)(2,1)S(1)}, u32[]{:S(2)}, u32[]{:S(2)}) %collective-permute-start.35) | collective-permute-done | bytes 196640 | tf_op jit(solution)/shard_map/ppermute | solution.py:457
  161.3 1.7 %collective-permute-done.36.refs_7_ = bf16[4,64,768]{2,1,0:T(8,128)(2,1)S(1)} collective-permute-done((bf16[4,64,768]{2,1,0:T(8,128)(2,1)S(1)}, bf16[4,64,768]{2,1,0:T(8,128)(2,1)S(1)}, u32[]{:S(2)}, u32[]{:S(2)}) %collective-permute-start.36) | collective-permute-done | bytes 393248 | tf_op jit(solution)/shard_map/ppermute | solution.py:457
  163.0 2.0 %shard_map.75 = bf16[512,768]{1,0:T(8,128)(2,1)} custom-call(s32[2]{0:T(128)S(1)} %pad_add_fusion.refs_0_, f32[512,768]{1,0:T(8,128)S(1)} %shard_map.73.refs_1_, s32[512,1]{1,0:T(8,128)S(1)} %get-tuple-element.114.refs_2_, bf16[2,64,768]{2,1,0:T(8,128)(2,1)S(1)} %get-tuple-element.167.refs_3_, bf16[2,64,768]{2,1,0:T(8,128)(2,1)S(1)} %collective-permute-done.33.refs_4_, ...), custom_call_target="tpu_custom_call" | custom-call | flops 1724999936 | bytes 1048576 | tf_op jit(solution)/shard_map/pallas_call | solution.py:122
  (111 shorter events, 28.8 us)
Async XLA Ops:
  1.1 15.0 %collective-permute-start = (bf16[96,768]{1,0:T(8,128)(2,1)S(1)}, bf16[96,768]{1,0:T(8,128)(2,1)S(1)}, u32[]{:S(2)}, u32[]{:S(2)}) collective-permute-start(bf16[96,768]{1,0:T(8,128)(2,1)S(1)} %fusion), channel_id=1, source_target_pairs={{0,1},{1,0},{2,3},{3,2},{4,5},{5,4},{6,7},{7,6},{8,9},{9,8},{10,11... | collective-permute-start | bytes 442376 | tf_op jit(solution)/shard_map/ppermute | solution.py:460
  4.2 11.9 %collective-permute-start.1 = (bf16[96,768]{1,0:T(8,128)(2,1)S(1)}, bf16[96,768]{1,0:T(8,128)(2,1)S(1)}, u32[]{:S(2)}, u32[]{:S(2)}) collective-permute-start(bf16[96,768]{1,0:T(8,128)(2,1)S(1)} %fusion), channel_id=1, source_target_pairs={{0,2},{1,3},{2,0},{3,1},{4,6},{5,7},{6,4},{7,5},{8,10},{9,11},{10,... | collective-permute-start | bytes 442376 | tf_op jit(solution)/shard_map/ppermute | solution.py:460
  16.2 8.7 %collective-permute-start.3 = (bf16[112,768]{1,0:T(8,128)(2,1)S(1)}, bf16[112,768]{1,0:T(8,128)(2,1)S(1)}, u32[]{:S(2)}, u32[]{:S(2)}) collective-permute-start(bf16[112,768]{1,0:T(8,128)(2,1)S(1)} %constant_dynamic-update-slice_fusion), channel_id=1, source_target_pairs={{0,8},{4,12},{8,0},{12,4},{16,24},{20,28},{24,16},{28,20},{1,9},{5... | collective-permute-start | bytes 516104 | tf_op jit(solution)/shard_map/ppermute | solution.py:457
  17.8 9.1 %collective-permute-start.4 = (bf16[112,768]{1,0:T(8,128)(2,1)S(1)}, bf16[112,768]{1,0:T(8,128)(2,1)S(1)}, u32[]{:S(2)}, u32[]{:S(2)}) collective-permute-start(bf16[112,768]{1,0:T(8,128)(2,1)S(1)} %constant_dynamic-update-slice_fusion), channel_id=1, source_target_pairs={{0,16},{4,20},{8,24},{12,28},{16,0},{20,4},{24,8},{28,12},{1,17},{... | collective-permute-start | bytes 516104 | tf_op jit(solution)/shard_map/ppermute | solution.py:457
  19.3 7.6 %collective-permute-start.5 = (bf16[112,768]{1,0:T(8,128)(2,1)S(1)}, bf16[112,768]{1,0:T(8,128)(2,1)S(1)}, u32[]{:S(2)}, u32[]{:S(2)}) collective-permute-start(bf16[112,768]{1,0:T(8,128)(2,1)S(1)} %constant_dynamic-update-slice_fusion), channel_id=1, source_target_pairs={{0,24},{4,28},{8,16},{12,20},{16,8},{20,12},{24,0},{28,4},{1,25},{... | collective-permute-start | bytes 516104 | tf_op jit(solution)/shard_map/ppermute | solution.py:457
  19.8 5.1 %collective-permute-start.2 = (bf16[96,768]{1,0:T(8,128)(2,1)S(1)}, bf16[96,768]{1,0:T(8,128)(2,1)S(1)}, u32[]{:S(2)}, u32[]{:S(2)}) collective-permute-start(bf16[96,768]{1,0:T(8,128)(2,1)S(1)} %collective-permute-done.1), channel_id=1, source_target_pairs={{0,1},{1,0},{2,3},{3,2},{4,5},{5,4},{6,7},{7,6},{8,9},{9,8},{10,11... | collective-permute-start | bytes 442376 | tf_op jit(solution)/shard_map/ppermute | solution.py:460
  29.4 5.2 %collective-permute-start.11 = (bf16[72,192]{1,0:T(8,128)(2,1)S(1)}, bf16[72,192]{1,0:T(8,128)(2,1)S(1)}, u32[]{:S(2)}, u32[]{:S(2)}) collective-permute-start(bf16[72,192]{1,0:T(8,128)(2,1)S(1)} %fusion.2.refs_3_), channel_id=1, source_target_pairs={{0,2},{1,3},{2,0},{3,1},{4,6},{5,7},{6,4},{7,5},{8,10},{9,11},{10,... | collective-permute-start | bytes 82952 | tf_op jit(solution)/shard_map/ppermute | solution.py:460
  29.9 14.6 %collective-permute-start.6 = (bf16[192,768]{1,0:T(8,128)(2,1)S(1)}, bf16[192,768]{1,0:T(8,128)(2,1)S(1)}, u32[]{:S(2)}, u32[]{:S(2)}) collective-permute-start(bf16[192,768]{1,0:T(8,128)(2,1)S(1)} %constant_dynamic-update-slice_fusion.2), channel_id=1, source_target_pairs={{0,8},{4,12},{8,0},{12,4},{16,24},{20,28},{24,16},{28,20},{1,9},{5... | collective-permute-start | bytes 884744 | tf_op jit(solution)/shard_map/ppermute | solution.py:457
  31.0 13.4 %collective-permute-start.7 = (bf16[192,768]{1,0:T(8,128)(2,1)S(1)}, bf16[192,768]{1,0:T(8,128)(2,1)S(1)}, u32[]{:S(2)}, u32[]{:S(2)}) collective-permute-start(bf16[192,768]{1,0:T(8,128)(2,1)S(1)} %constant_dynamic-update-slice_fusion.2), channel_id=1, source_target_pairs={{0,16},{4,20},{8,24},{12,28},{16,0},{20,4},{24,8},{28,12},{1,17},{... | collective-permute-start | bytes 884744 | tf_op jit(solution)/shard_map/ppermute | solution.py:457
  31.8 14.0 %collective-permute-start.8 = (bf16[192,768]{1,0:T(8,128)(2,1)S(1)}, bf16[192,768]{1,0:T(8,128)(2,1)S(1)}, u32[]{:S(2)}, u32[]{:S(2)}) collective-permute-start(bf16[192,768]{1,0:T(8,128)(2,1)S(1)} %constant_dynamic-update-slice_fusion.2), channel_id=1, source_target_pairs={{0,24},{4,28},{8,16},{12,20},{16,8},{20,12},{24,0},{28,4},{1,25},{... | collective-permute-start | bytes 884744 | tf_op jit(solution)/shard_map/ppermute | solution.py:457
  33.4 12.4 %collective-permute-start.10 = (bf16[72,192]{1,0:T(8,128)(2,1)S(1)}, bf16[72,192]{1,0:T(8,128)(2,1)S(1)}, u32[]{:S(2)}, u32[]{:S(2)}) collective-permute-start(bf16[72,192]{1,0:T(8,128)(2,1)S(1)} %fusion.2.refs_3_), channel_id=1, source_target_pairs={{0,1},{1,0},{2,3},{3,2},{4,5},{5,4},{6,7},{7,6},{8,9},{9,8},{10,11... | collective-permute-start | bytes 82952 | tf_op jit(solution)/shard_map/ppermute | solution.py:460
  34.6 11.2 %collective-permute-start.12 = (bf16[72,192]{1,0:T(8,128)(2,1)S(1)}, bf16[72,192]{1,0:T(8,128)(2,1)S(1)}, u32[]{:S(2)}, u32[]{:S(2)}) collective-permute-start(bf16[72,192]{1,0:T(8,128)(2,1)S(1)} %collective-permute-done.11.refs_5_), channel_id=1, source_target_pairs={{0,1},{1,0},{2,3},{3,2},{4,5},{5,4},{6,7},{7,6},{8,9},{9,8},{10,11... | collective-permute-start | bytes 82952 | tf_op jit(solution)/shard_map/ppermute | solution.py:460
  64.1 16.1 %collective-permute-start.14 = (bf16[2,2,2,32,768]{4,3,2,1,0:T(8,128)(2,1)S(1)}, bf16[2,2,2,32,768]{4,3,2,1,0:T(8,128)(2,1)S(1)}, u32[]{:S(2)}, u32[]{:S(2)}) collective-permute-start(bf16[2,2,2,32,768]{4,3,2,1,0:T(8,128)(2,1)S(1)} %get-tuple-element.120), channel_id=1, source_target_pairs={{0,8},{4,12},{8,0},{12,4},{16,24},{20,28},{24,16},{28,20},{1,9},{5... | collective-permute-start | bytes 1179656 | tf_op jit(solution)/shard_map/ppermute | solution.py:457
  65.0 19.3 %collective-permute-start.15 = (bf16[2,2,2,32,768]{4,3,2,1,0:T(8,128)(2,1)S(1)}, bf16[2,2,2,32,768]{4,3,2,1,0:T(8,128)(2,1)S(1)}, u32[]{:S(2)}, u32[]{:S(2)}) collective-permute-start(bf16[2,2,2,32,768]{4,3,2,1,0:T(8,128)(2,1)S(1)} %get-tuple-element.121), channel_id=1, source_target_pairs={{0,16},{4,20},{8,24},{12,28},{16,0},{20,4},{24,8},{28,12},{1,17},{... | collective-permute-start | bytes 1179656 | tf_op jit(solution)/shard_map/ppermute | solution.py:457
  66.4 17.9 %collective-permute-start.16 = (bf16[2,2,2,32,768]{4,3,2,1,0:T(8,128)(2,1)S(1)}, bf16[2,2,2,32,768]{4,3,2,1,0:T(8,128)(2,1)S(1)}, u32[]{:S(2)}, u32[]{:S(2)}) collective-permute-start(bf16[2,2,2,32,768]{4,3,2,1,0:T(8,128)(2,1)S(1)} %get-tuple-element.122), channel_id=1, source_target_pairs={{0,24},{4,28},{8,16},{12,20},{16,8},{20,12},{24,0},{28,4},{1,25},{... | collective-permute-start | bytes 1179656 | tf_op jit(solution)/shard_map/ppermute | solution.py:457
  84.6 12.0 %collective-permute-start.17 = (bf16[2,2,2,32,768]{4,3,2,1,0:T(8,128)(2,1)S(1)}, bf16[2,2,2,32,768]{4,3,2,1,0:T(8,128)(2,1)S(1)}, u32[]{:S(2)}, u32[]{:S(2)}) collective-permute-start(bf16[2,2,2,32,768]{4,3,2,1,0:T(8,128)(2,1)S(1)} %get-tuple-element.128), channel_id=1, source_target_pairs={{0,8},{4,12},{8,0},{12,4},{16,24},{20,28},{24,16},{28,20},{1,9},{5... | collective-permute-start | bytes 1179656 | tf_op jit(solution)/shard_map/ppermute | solution.py:457
  85.8 11.6 %collective-permute-start.18 = (bf16[2,2,2,32,768]{4,3,2,1,0:T(8,128)(2,1)S(1)}, bf16[2,2,2,32,768]{4,3,2,1,0:T(8,128)(2,1)S(1)}, u32[]{:S(2)}, u32[]{:S(2)}) collective-permute-start(bf16[2,2,2,32,768]{4,3,2,1,0:T(8,128)(2,1)S(1)} %get-tuple-element.129), channel_id=1, source_target_pairs={{0,16},{4,20},{8,24},{12,28},{16,0},{20,4},{24,8},{28,12},{1,17},{... | collective-permute-start | bytes 1179656 | tf_op jit(solution)/shard_map/ppermute | solution.py:457
  86.6 18.8 %collective-permute-start.19 = (bf16[2,2,2,32,768]{4,3,2,1,0:T(8,128)(2,1)S(1)}, bf16[2,2,2,32,768]{4,3,2,1,0:T(8,128)(2,1)S(1)}, u32[]{:S(2)}, u32[]{:S(2)}) collective-permute-start(bf16[2,2,2,32,768]{4,3,2,1,0:T(8,128)(2,1)S(1)} %get-tuple-element.130), channel_id=1, source_target_pairs={{0,24},{4,28},{8,16},{12,20},{16,8},{20,12},{24,0},{28,4},{1,25},{... | collective-permute-start | bytes 1179656 | tf_op jit(solution)/shard_map/ppermute | solution.py:457
  91.0 14.9 %collective-permute-start.21 = (bf16[256,768]{1,0:T(8,128)(2,1)S(1)}, bf16[256,768]{1,0:T(8,128)(2,1)S(1)}, u32[]{:S(2)}, u32[]{:S(2)}) collective-permute-start(bf16[256,768]{1,0:T(8,128)(2,1)S(1)} %get-tuple-element.135), channel_id=1, source_target_pairs={{0,1},{1,0},{2,3},{3,2},{4,5},{5,4},{6,7},{7,6},{8,9},{9,8},{10,11... | collective-permute-start | bytes 1179656 | tf_op jit(solution)/shard_map/ppermute | solution.py:460
  94.5 11.4 %collective-permute-start.22 = (bf16[128,768]{1,0:T(8,128)(2,1)S(1)}, bf16[128,768]{1,0:T(8,128)(2,1)S(1)}, u32[]{:S(2)}, u32[]{:S(2)}) collective-permute-start(bf16[128,768]{1,0:T(8,128)(2,1)S(1)} %get-tuple-element.172), channel_id=1, source_target_pairs={{0,1},{1,0},{2,3},{3,2},{4,5},{5,4},{6,7},{7,6},{8,9},{9,8},{10,11... | collective-permute-start | bytes 589832 | tf_op jit(solution)/shard_map/ppermute | solution.py:460
  106.2 8.2 %collective-permute-start.26 = (bf16[128,768]{1,0:T(8,128)(2,1)S(1)}, bf16[128,768]{1,0:T(8,128)(2,1)S(1)}, u32[]{:S(2)}, u32[]{:S(2)}) collective-permute-start(bf16[128,768]{1,0:T(8,128)(2,1)S(1)} %get-tuple-element.171), channel_id=1, source_target_pairs={{0,1},{1,0},{2,3},{3,2},{4,5},{5,4},{6,7},{7,6},{8,9},{9,8},{10,11... | collective-permute-start | bytes 589832 | tf_op jit(solution)/shard_map/ppermute | solution.py:460
  111.3 21.5 %collective-permute-start.24 = (bf16[256,768]{1,0:T(8,128)(2,1)S(1)}, bf16[256,768]{1,0:T(8,128)(2,1)S(1)}, u32[]{:S(2)}, u32[]{:S(2)}) collective-permute-start(bf16[256,768]{1,0:T(8,128)(2,1)S(1)} %get-tuple-element.146), channel_id=1, source_target_pairs={{0,1},{1,0},{2,3},{3,2},{4,5},{5,4},{6,7},{7,6},{8,9},{9,8},{10,11... | collective-permute-start | bytes 1179656 | tf_op jit(solution)/shard_map/ppermute | solution.py:460
  112.0 20.8 %collective-permute-start.25 = (bf16[256,768]{1,0:T(8,128)(2,1)S(1)}, bf16[256,768]{1,0:T(8,128)(2,1)S(1)}, u32[]{:S(2)}, u32[]{:S(2)}) collective-permute-start(bf16[256,768]{1,0:T(8,128)(2,1)S(1)} %get-tuple-element.147), channel_id=1, source_target_pairs={{0,2},{1,3},{2,0},{3,1},{4,6},{5,7},{6,4},{7,5},{8,10},{9,11},{10,... | collective-permute-start | bytes 1179656 | tf_op jit(solution)/shard_map/ppermute | solution.py:460
  117.3 30.5 %collective-permute-start.30 = (bf16[256,768]{1,0:T(8,128)(2,1)S(1)}, bf16[256,768]{1,0:T(8,128)(2,1)S(1)}, u32[]{:S(2)}, u32[]{:S(2)}) collective-permute-start(bf16[256,768]{1,0:T(8,128)(2,1)S(1)} %get-tuple-element.150), channel_id=1, source_target_pairs={{0,1},{1,0},{2,3},{3,2},{4,5},{5,4},{6,7},{7,6},{8,9},{9,8},{10,11... | collective-permute-start | bytes 1179656 | tf_op jit(solution)/shard_map/ppermute | solution.py:460
  118.9 28.9 %collective-permute-start.31 = (bf16[256,768]{1,0:T(8,128)(2,1)S(1)}, bf16[256,768]{1,0:T(8,128)(2,1)S(1)}, u32[]{:S(2)}, u32[]{:S(2)}) collective-permute-start(bf16[256,768]{1,0:T(8,128)(2,1)S(1)} %get-tuple-element.158), channel_id=1, source_target_pairs={{0,2},{1,3},{2,0},{3,1},{4,6},{5,7},{6,4},{7,5},{8,10},{9,11},{10,... | collective-permute-start | bytes 1179656 | tf_op jit(solution)/shard_map/ppermute | solution.py:460
  133.5 14.3 %collective-permute-start.27 = (bf16[2,64,768]{2,1,0:T(8,128)(2,1)S(1)}, bf16[2,64,768]{2,1,0:T(8,128)(2,1)S(1)}, u32[]{:S(2)}, u32[]{:S(2)}) collective-permute-start(bf16[2,64,768]{2,1,0:T(8,128)(2,1)S(1)} %get-tuple-element.155), channel_id=1, source_target_pairs={{0,8},{4,12},{8,0},{12,4},{16,24},{20,28},{24,16},{28,20},{1,9},{5... | collective-permute-start | bytes 589832 | tf_op jit(solution)/shard_map/ppermute | solution.py:457
  135.0 12.9 %collective-permute-start.28 = (bf16[2,64,768]{2,1,0:T(8,128)(2,1)S(1)}, bf16[2,64,768]{2,1,0:T(8,128)(2,1)S(1)}, u32[]{:S(2)}, u32[]{:S(2)}) collective-permute-start(bf16[2,64,768]{2,1,0:T(8,128)(2,1)S(1)} %get-tuple-element.156), channel_id=1, source_target_pairs={{0,16},{4,20},{8,24},{12,28},{16,0},{20,4},{24,8},{28,12},{1,17},{... | collective-permute-start | bytes 589832 | tf_op jit(solution)/shard_map/ppermute | solution.py:457
  135.8 12.0 %collective-permute-start.29 = (bf16[2,64,768]{2,1,0:T(8,128)(2,1)S(1)}, bf16[2,64,768]{2,1,0:T(8,128)(2,1)S(1)}, u32[]{:S(2)}, u32[]{:S(2)}) collective-permute-start(bf16[2,64,768]{2,1,0:T(8,128)(2,1)S(1)} %get-tuple-element.157), channel_id=1, source_target_pairs={{0,24},{4,28},{8,16},{12,20},{16,8},{20,12},{24,0},{28,4},{1,25},{... | collective-permute-start | bytes 589832 | tf_op jit(solution)/shard_map/ppermute | solution.py:457
  148.0 4.3 %collective-permute-start.32 = (bf16[4,64,768]{2,1,0:T(8,128)(2,1)S(1)}, bf16[4,64,768]{2,1,0:T(8,128)(2,1)S(1)}, u32[]{:S(2)}, u32[]{:S(2)}) collective-permute-start(bf16[4,64,768]{2,1,0:T(8,128)(2,1)S(1)} %pad_maximum_fusion.5), channel_id=1, source_target_pairs={{0,4},{4,0},{8,12},{12,8},{16,20},{20,16},{24,28},{28,24},{1,5},{5... | collective-permute-start | bytes 1179656 | tf_op jit(solution)/shard_map/ppermute | solution.py:457
  148.7 7.8 %collective-permute-start.33 = (bf16[2,64,768]{2,1,0:T(8,128)(2,1)S(1)}, bf16[2,64,768]{2,1,0:T(8,128)(2,1)S(1)}, u32[]{:S(2)}, u32[]{:S(2)}) collective-permute-start(bf16[2,64,768]{2,1,0:T(8,128)(2,1)S(1)} %get-tuple-element.164), channel_id=1, source_target_pairs={{0,8},{4,12},{8,0},{12,4},{16,24},{20,28},{24,16},{28,20},{1,9},{5... | collective-permute-start | bytes 589832 | tf_op jit(solution)/shard_map/ppermute | solution.py:457
  149.9 7.4 %collective-permute-start.34 = (bf16[2,64,768]{2,1,0:T(8,128)(2,1)S(1)}, bf16[2,64,768]{2,1,0:T(8,128)(2,1)S(1)}, u32[]{:S(2)}, u32[]{:S(2)}) collective-permute-start(bf16[2,64,768]{2,1,0:T(8,128)(2,1)S(1)} %get-tuple-element.165), channel_id=1, source_target_pairs={{0,16},{4,20},{8,24},{12,28},{16,0},{20,4},{24,8},{28,12},{1,17},{... | collective-permute-start | bytes 589832 | tf_op jit(solution)/shard_map/ppermute | solution.py:457
  150.7 10.4 %collective-permute-start.35 = (bf16[2,64,768]{2,1,0:T(8,128)(2,1)S(1)}, bf16[2,64,768]{2,1,0:T(8,128)(2,1)S(1)}, u32[]{:S(2)}, u32[]{:S(2)}) collective-permute-start(bf16[2,64,768]{2,1,0:T(8,128)(2,1)S(1)} %get-tuple-element.166), channel_id=1, source_target_pairs={{0,24},{4,28},{8,16},{12,20},{16,8},{20,12},{24,0},{28,4},{1,25},{... | collective-permute-start | bytes 589832 | tf_op jit(solution)/shard_map/ppermute | solution.py:457
  (13 other events, 153.9 us)

commit v5 on v4

--- a/solution.py
+++ b/solution.py
@@ -422,25 +422,35 @@
     )
 
 
-def combine(meta, total, slots, returned, local, n_seq, n_ep, capacity, dtype):
+def combine(meta, total, slots, returned, hots, n_seq, n_ep, capacity, dtype):
     rows, model = total.shape
     got, crossed = returned
+    span = 2 * capacity
 
     def kernel(ins, outs, scratch, arrive, leave, reads, writes):
         meta_ref, total_ref, slot_ref, *got_refs, crossed_ref = ins
-        span = 2 * capacity
-        col = lax.broadcasted_iota(jnp.int32, (1, n_seq * span), 1)
-        seq = (col // span) ^ meta_ref[0]
-        pair = seq * (n_ep // 2) + ((col // capacity) % 2 ^ (meta_ref[1] // 2))
-        key = (pair * EXP_DEV + local) * capacity + col % capacity
-        hot = (slot_ref[...] == key).astype(BF16)
+        if hots is None:
+            col = lax.broadcasted_iota(jnp.int32, (1, n_seq * span), 1)
+            seq = (col // span) ^ meta_ref[0]
+            pair = seq * (n_ep // 2) + ((col // capacity) % 2 ^ (meta_ref[1] // 2))
+            found = []
+            for local in range(EXP_DEV):
+                key = (pair * EXP_DEV + local) * capacity + col % capacity
+                found.append((slot_ref[...] == key).astype(BF16))
+            hot = found[0]
+            for out, other in zip(outs[1:], found[1:]):
+                out[...] = other
+        else:
+            hot = slot_ref[...]
         pieces = []
         for i, got_ref in enumerate(got_refs):
             pieces += [got_ref[0], crossed_ref[i]]
         out = total_ref[...].astype(F32) + dot_nn(hot, jnp.concatenate(pieces, axis=0))
         outs[0][...] = out.astype(dtype)
 
-    return call(kernel, [((rows, model), dtype)], [meta, total, slots, *got, crossed], 1.5)[0]
+    others = [((rows, n_seq * span), BF16)] * (EXP_DEV - 1) if hots is None else []
+    where = slots if hots is None else hots
+    return call(kernel, [((rows, model), dtype)] + others, [meta, total, where, *got, crossed], 1.5)
 
 
 def per_device(tokens, input_proj, output_proj, expert_index, expert_in, expert_out):
@@ -543,12 +553,14 @@
         owns.append(own)
         sides.append([own[0], over_ep(own[1], 1), over_ep(sums[0], 2)])
     sides[0], owns = lax.optimization_barrier((sides[0], owns))
-    total, returned = stream, None
+    total, returned, hots = stream, None, []
     for local in range(EXP_DEV):
         laid = lay_out(meta, *sides[local], n_seq, capacity)
         returned = exchange(laid, total if returned else sides[1:])
         last = local == EXP_DEV - 1
-        total = combine(meta, total, slots, returned, local, n_seq, n_ep, capacity, BF16 if last else F32)
+        hot = hots[local - 1] if local else None
+        total, *found = combine(meta, total, slots, returned, hot, n_seq, n_ep, capacity, BF16 if last else F32)
+        hots = hots or found
     return total
 
 

time: 165 us -> 165 us (level)
  no operation moved by 1% of the time
where the time goes in v5:
time: 165 us
  waiting for transfers between devices  62.8 us (38%)
  Pallas kernels  59.4 us (36%)
  starting transfers between devices  37.9 us (23%)
  local copies, waits for them, and re-layouts  2.52 us (2%)
  other arithmetic  1.93 us (1%)
    pallas_call x8, Pallas kernels, call(): pl.pallas_call(body, in_specs=[pl.BlockSpec(memory_space=pltpu.SMEM)] + [...  48.1 us
    ppermute x24, waiting for transfers between devices, over_seq(): return lax.ppermute(x, 'seq', xor_pairs(n_seq, bits)) if bits else x  32.9 us
    ppermute x13, waiting for transfers between devices, over_ep(): return lax.ppermute(x, 'ep', xor_pairs(n_ep, bits)) if bits else x  29.9 us
    ppermute x24, starting transfers between devices, over_seq(): return lax.ppermute(x, 'seq', xor_pairs(n_seq, bits)) if bits else x  21.7 us
    ppermute x13, starting transfers between devices, over_ep(): return lax.ppermute(x, 'ep', xor_pairs(n_ep, bits)) if bits else x  16.2 us
    pallas_call x4, Pallas kernels, expert(): pl.pallas_call(kernel, in_specs=[pl.BlockSpec(memory_space=pltpu.VMEM)] *...  11.2 us
  transfers between devices with their start and end apart: 37, of which 19 were waited for; matrix products, arithmetic and copies ran while one was open for 0% of the time, Pallas kernels for 26%

profile of v5, /device:TPU:0, one launch (start us, length us, event | category | flops | bytes accessed | tf_op | source)
XLA Modules:
  0.0 165.0 jit_solution(14121585496501598166)
XLA Ops:
  1.1 3.1 %collective-permute-start = (bf16[96,768]{1,0:T(8,128)(2,1)S(1)}, bf16[96,768]{1,0:T(8,128)(2,1)S(1)}, u32[]{:S(2)}, u32[]{:S(2)}) collective-permute-start(bf16[96,768]{1,0:T(8,128)(2,1)S(1)} %fusion), channel_id=1, source_target_pairs={{0,1},{1,0},{2,3},{3,2},{4,5},{5,4},{6,7},{7,6},{8,9},{9,8},{10,11... | collective-permute-start | bytes 442376 | tf_op jit(solution)/shard_map/ppermute | solution.py:470
  4.2 2.6 %collective-permute-start.1 = (bf16[96,768]{1,0:T(8,128)(2,1)S(1)}, bf16[96,768]{1,0:T(8,128)(2,1)S(1)}, u32[]{:S(2)}, u32[]{:S(2)}) collective-permute-start(bf16[96,768]{1,0:T(8,128)(2,1)S(1)} %fusion), channel_id=1, source_target_pairs={{0,2},{1,3},{2,0},{3,1},{4,6},{5,7},{6,4},{7,5},{8,10},{9,11},{10,... | collective-permute-start | bytes 442376 | tf_op jit(solution)/shard_map/ppermute | solution.py:470
  7.1 1.9 %copy-done.1 = bf16[2048,768]{1,0:T(8,128)(2,1)S(1)} copy-done((bf16[2048,768]{1,0:T(8,128)(2,1)S(1)}, bf16[2048,768]{1,0:T(8,128)(2,1)}, u32[]{:S(2)}) %copy-start.1) | copy-done | bytes 3145752
  9.0 7.1 %shard_map.64 = (bf16[64,192]{1,0:T(8,128)(2,1)S(1)}, s32[512,1]{1,0:T(8,128)S(1)}, bf16[26,2048,256]{2,1,0:T(8,128)(2,1)}) custom-call(s32[2]{0:T(128)S(1)} %pad_add_fusion.refs_0_, bf16[768,768]{1,0:T(8,128)(2,1)S(1)} %pad_maximum_fusion.refs_1_, s32[512,1]{1,0:T(8,128)S(1)} %copy.8.refs_2_, bf16[2048,768]{1,0:T(8,128)(2,1)S(1)} %copy-done.1), custom_call_target="tpu_custom_call" | custom-call | flops 8049999872 | bytes 1048576 | tf_op jit(solution)/shard_map/pallas_call | solution.py:122
  16.2 1.6 collective-permute-start.3
  17.8 1.5 collective-permute-start.4
  20.2 4.7 %collective-permute-done.2 = bf16[96,768]{1,0:T(8,128)(2,1)S(1)} collective-permute-done((bf16[96,768]{1,0:T(8,128)(2,1)S(1)}, bf16[96,768]{1,0:T(8,128)(2,1)S(1)}, u32[]{:S(2)}, u32[]{:S(2)}) %collective-permute-start.2) | collective-permute-done | bytes 147488 | tf_op jit(solution)/shard_map/ppermute | solution.py:470
  24.9 1.9 %collective-permute-done.4 = bf16[112,768]{1,0:T(8,128)(2,1)S(1)} collective-permute-done((bf16[112,768]{1,0:T(8,128)(2,1)S(1)}, bf16[112,768]{1,0:T(8,128)(2,1)S(1)}, u32[]{:S(2)}, u32[]{:S(2)}) %collective-permute-start.4) | collective-permute-done | bytes 172064 | tf_op jit(solution)/shard_map/ppermute | solution.py:467
  27.1 2.1 %collective-permute-done.9.refs_2_ = bf16[4,112,768]{2,1,0:T(8,128)(2,1)S(1)} collective-permute-done((bf16[4,112,768]{2,1,0:T(8,128)(2,1)S(1)}, bf16[4,112,768]{2,1,0:T(8,128)(2,1)S(1)}, u32[]{:S(2)}, u32[]{:S(2)}) %collective-permute-start.9) | collective-permute-done | bytes 688160 | tf_op jit(solution)/shard_map/ppermute | solution.py:467
  31.8 1.6 collective-permute-start.8
  35.4 9.0 %shard_map.65 = (bf16[192,768]{1,0:T(8,128)(2,1)S(1)}, bf16[26,2048,256]{2,1,0:T(8,128)(2,1)}) custom-call(s32[2]{0:T(128)S(1)} %pad_add_fusion.refs_0_, bf16[4,112,768]{2,1,0:T(8,128)(2,1)S(1)} %pad_maximum_fusion.4.refs_1_, bf16[4,112,768]{2,1,0:T(8,128)(2,1)S(1)} %collective-permute-done.9.refs_2_, ...), custom_call_target="tpu_custom_call", output_to_operand_aliasing={{1}: (3, {})} | custom-call | flops 9200000000 | bytes 1048576 | tf_op jit(solution)/shard_map/pallas_call | solution.py:122
  46.1 2.8 %collective-permute-done.13.refs_2_ = bf16[4,192,768]{2,1,0:T(8,128)(2,1)S(1)} collective-permute-done((bf16[4,192,768]{2,1,0:T(8,128)(2,1)S(1)}, bf16[4,192,768]{2,1,0:T(8,128)(2,1)S(1)}, u32[]{:S(2)}, u32[]{:S(2)}) %collective-permute-start.13) | collective-permute-done | bytes 1179680 | tf_op jit(solution)/shard_map/ppermute | solution.py:467
  48.9 15.1 %shard_map.66 = (f32[2,192,192]{2,1,0:T(8,128)S(1)}, bf16[2,2,2,32,768]{4,3,2,1,0:T(8,128)(2,1)S(1)}, bf16[2,2,2,32,768]{4,3,2,1,0:T(8,128)(2,1)S(1)}, bf16[2,2,...) custom-call(s32[2]{0:T(128)S(1)} %pad_add_fusion.refs_0_, ...), custom_call_target="tpu_custom_call" | custom-call | flops 14949999616 | bytes 1048576 | tf_op jit(solution)/shard_map/pallas_call | solution.py:122
  67.6 12.5 %shard_map.67 = (bf16[512,768]{1,0:T(8,128)(2,1)S(1)}, bf16[2,2,2,32,768]{4,3,2,1,0:T(8,128)(2,1)S(1)}, bf16[2,2,2,32,768]{4,3,2,1,0:T(8,128)(2,1)S(1)}, bf16[2,...) custom-call(s32[2]{0:T(128)S(1)} %pad_add_fusion.refs_0_, ...), custom_call_target="tpu_custom_call" | custom-call | flops 14949999616 | bytes 1048576 | tf_op jit(solution)/shard_map/pallas_call | solution.py:122
  80.1 4.2 %collective-permute-done.15.refs_2_ = bf16[2,2,2,32,768]{4,3,2,1,0:T(8,128)(2,1)S(1)} collective-permute-done((bf16[2,2,2,32,768]{4,3,2,1,0:T(8,128)(2,1)S(1)}, bf16[2,2,2,32,768]{4,3,2,1,0:T(8,128)(2,1)S(1)}, u32[]{:S(2)}, u32[]{:S(2)}) %collective-permute-start.15) | collective-permute-done | bytes 393248 | tf_op jit(solution)/shard_map/ppermute | solution.py:467
  86.6 1.6 collective-permute-start.19
  88.2 2.7 %shard_map.68 = (bf16[256,768]{1,0:T(8,128)(2,1)S(1)}, bf16[256,768]{1,0:T(8,128)(2,1)S(1)}) custom-call(bf16[2,2,2,32,768]{4,3,2,1,0:T(8,128)(2,1)S(1)} %get-tuple-element.133.refs_0_, bf16[2,2,2,32,768]{4,3,2,1,0:T(8,128)(2,1)S(1)} %collective-permute-done.14.refs_1_, bf16[2,2,2,32,768]{4,3,2,1,0:T(8,128)(2,1)S(1)} %collective-permute-done.15.refs_2_, ...), custom_call_target="tpu_custom_call" | custom-call | flops 3449999872 | bytes 1048576 | tf_op jit(solution)/shard_map/pallas_call | solution.py:399
  91.7 2.7 %shard_map.69 = (bf16[256,768]{1,0:T(8,128)(2,1)S(1)}, bf16[256,768]{1,0:T(8,128)(2,1)S(1)}) custom-call(bf16[2,2,2,32,768]{4,3,2,1,0:T(8,128)(2,1)S(1)} %get-tuple-element.133.refs_0_, bf16[2,2,2,32,768]{4,3,2,1,0:T(8,128)(2,1)S(1)} %collective-permute-done.14.refs_1_, bf16[2,2,2,32,768]{4,3,2,1,0:T(8,128)(2,1)S(1)} %collective-permute-done.15.refs_2_, ...), custom_call_target="tpu_custom_call" | custom-call | flops 3449999872 | bytes 1048576 | tf_op jit(solution)/shard_map/pallas_call | solution.py:399
  94.5 1.4 collective-permute-start.22
  97.4 8.0 %collective-permute-done.19.refs_3_ = bf16[2,2,2,32,768]{4,3,2,1,0:T(8,128)(2,1)S(1)} collective-permute-done((bf16[2,2,2,32,768]{4,3,2,1,0:T(8,128)(2,1)S(1)}, bf16[2,2,2,32,768]{4,3,2,1,0:T(8,128)(2,1)S(1)}, u32[]{:S(2)}, u32[]{:S(2)}) %collective-permute-start.19) | collective-permute-done | bytes 393248 | tf_op jit(solution)/shard_map/ppermute | solution.py:467
  106.9 1.5 collective-permute-done.23.refs_4_
  108.4 2.9 %shard_map.70 = (bf16[256,768]{1,0:T(8,128)(2,1)S(1)}, bf16[256,768]{1,0:T(8,128)(2,1)S(1)}, bf16[256,768]{1,0:T(8,128)(2,1)S(1)}) custom-call(bf16[2,2,2,32,768]{4,3,2,1,0:T(8,128)(2,1)S(1)} %get-tuple-element.143.refs_0_, bf16[2,2,2,32,768]{4,3,2,1,0:T(8,128)(2,1)S(1)} %collective-permute-done.17.refs_1_, ...), custom_call_target="tpu_custom_call" | custom-call | flops 3449999872 | bytes 1048576 | tf_op jit(solution)/shard_map/pallas_call | solution.py:399
  112.0 2.4 %collective-permute-start.25 = (bf16[256,768]{1,0:T(8,128)(2,1)S(1)}, bf16[256,768]{1,0:T(8,128)(2,1)S(1)}, u32[]{:S(2)}, u32[]{:S(2)}) collective-permute-start(bf16[256,768]{1,0:T(8,128)(2,1)S(1)} %get-tuple-element.149), channel_id=1, source_target_pairs={{0,2},{1,3},{2,0},{3,1},{4,6},{5,7},{6,4},{7,5},{8,10},{9,11},{10,... | collective-permute-start | bytes 1179656 | tf_op jit(solution)/shard_map/ppermute | solution.py:470
  114.4 2.9 %shard_map.71 = (bf16[256,768]{1,0:T(8,128)(2,1)S(1)}, bf16[256,768]{1,0:T(8,128)(2,1)S(1)}, bf16[256,768]{1,0:T(8,128)(2,1)S(1)}) custom-call(bf16[2,2,2,32,768]{4,3,2,1,0:T(8,128)(2,1)S(1)} %get-tuple-element.143.refs_0_, bf16[2,2,2,32,768]{4,3,2,1,0:T(8,128)(2,1)S(1)} %collective-permute-done.17.refs_1_, ...), custom_call_target="tpu_custom_call" | custom-call | flops 3449999872 | bytes 1048576 | tf_op jit(solution)/shard_map/pallas_call | solution.py:399
  117.3 1.6 collective-permute-start.30
  119.4 13.3 %collective-permute-done.24.refs_2_ = bf16[256,768]{1,0:T(8,128)(2,1)S(1)} collective-permute-done((bf16[256,768]{1,0:T(8,128)(2,1)S(1)}, bf16[256,768]{1,0:T(8,128)(2,1)S(1)}, u32[]{:S(2)}, u32[]{:S(2)}) %collective-permute-start.24) | collective-permute-done | bytes 393248 | tf_op jit(solution)/shard_map/ppermute | solution.py:470
  137.1 10.7 %collective-permute-done.30.refs_2_ = bf16[256,768]{1,0:T(8,128)(2,1)S(1)} collective-permute-done((bf16[256,768]{1,0:T(8,128)(2,1)S(1)}, bf16[256,768]{1,0:T(8,128)(2,1)S(1)}, u32[]{:S(2)}, u32[]{:S(2)}) %collective-permute-start.30) | collective-permute-done | bytes 393248 | tf_op jit(solution)/shard_map/ppermute | solution.py:470
  150.7 1.6 collective-permute-start.35
  153.4 3.0 %collective-permute-done.33.refs_4_ = bf16[2,64,768]{2,1,0:T(8,128)(2,1)S(1)} collective-permute-done((bf16[2,64,768]{2,1,0:T(8,128)(2,1)S(1)}, bf16[2,64,768]{2,1,0:T(8,128)(2,1)S(1)}, u32[]{:S(2)}, u32[]{:S(2)}) %collective-permute-start.33) | collective-permute-done | bytes 196640 | tf_op jit(solution)/shard_map/ppermute | solution.py:467
  157.2 3.8 %collective-permute-done.35.refs_6_ = bf16[2,64,768]{2,1,0:T(8,128)(2,1)S(1)} collective-permute-done((bf16[2,64,768]{2,1,0:T(8,128)(2,1)S(1)}, bf16[2,64,768]{2,1,0:T(8,128)(2,1)S(1)}, u32[]{:S(2)}, u32[]{:S(2)}) %collective-permute-start.35) | collective-permute-done | bytes 196640 | tf_op jit(solution)/shard_map/ppermute | solution.py:467
  161.3 1.7 %collective-permute-done.36.refs_7_ = bf16[4,64,768]{2,1,0:T(8,128)(2,1)S(1)} collective-permute-done((bf16[4,64,768]{2,1,0:T(8,128)(2,1)S(1)}, bf16[4,64,768]{2,1,0:T(8,128)(2,1)S(1)}, u32[]{:S(2)}, u32[]{:S(2)}) %collective-permute-start.36) | collective-permute-done | bytes 393248 | tf_op jit(solution)/shard_map/ppermute | solution.py:467
  163.0 2.0 %shard_map.75 = bf16[512,768]{1,0:T(8,128)(2,1)} custom-call(s32[2]{0:T(128)S(1)} %pad_add_fusion.refs_0_, f32[512,768]{1,0:T(8,128)S(1)} %get-tuple-element.165.refs_1_, bf16[512,512]{1,0:T(8,128)(2,1)S(1)} %get-tuple-element.166.refs_2_, bf16[2,64,768]{2,1,0:T(8,128)(2,1)S(1)} %get-tuple-element.171.refs_3_, ...), custom_call_target="tpu_custom_call" | custom-call | flops 1724999936 | bytes 1048576 | tf_op jit(solution)/shard_map/pallas_call | solution.py:122
  (111 shorter events, 29.0 us)
Async XLA Ops:
  1.1 15.0 %collective-permute-start = (bf16[96,768]{1,0:T(8,128)(2,1)S(1)}, bf16[96,768]{1,0:T(8,128)(2,1)S(1)}, u32[]{:S(2)}, u32[]{:S(2)}) collective-permute-start(bf16[96,768]{1,0:T(8,128)(2,1)S(1)} %fusion), channel_id=1, source_target_pairs={{0,1},{1,0},{2,3},{3,2},{4,5},{5,4},{6,7},{7,6},{8,9},{9,8},{10,11... | collective-permute-start | bytes 442376 | tf_op jit(solution)/shard_map/ppermute | solution.py:470
  4.2 11.9 %collective-permute-start.1 = (bf16[96,768]{1,0:T(8,128)(2,1)S(1)}, bf16[96,768]{1,0:T(8,128)(2,1)S(1)}, u32[]{:S(2)}, u32[]{:S(2)}) collective-permute-start(bf16[96,768]{1,0:T(8,128)(2,1)S(1)} %fusion), channel_id=1, source_target_pairs={{0,2},{1,3},{2,0},{3,1},{4,6},{5,7},{6,4},{7,5},{8,10},{9,11},{10,... | collective-permute-start | bytes 442376 | tf_op jit(solution)/shard_map/ppermute | solution.py:470
  16.2 8.7 %collective-permute-start.3 = (bf16[112,768]{1,0:T(8,128)(2,1)S(1)}, bf16[112,768]{1,0:T(8,128)(2,1)S(1)}, u32[]{:S(2)}, u32[]{:S(2)}) collective-permute-start(bf16[112,768]{1,0:T(8,128)(2,1)S(1)} %constant_dynamic-update-slice_fusion), channel_id=1, source_target_pairs={{0,8},{4,12},{8,0},{12,4},{16,24},{20,28},{24,16},{28,20},{1,9},{5... | collective-permute-start | bytes 516104 | tf_op jit(solution)/shard_map/ppermute | solution.py:467
  17.8 9.1 %collective-permute-start.4 = (bf16[112,768]{1,0:T(8,128)(2,1)S(1)}, bf16[112,768]{1,0:T(8,128)(2,1)S(1)}, u32[]{:S(2)}, u32[]{:S(2)}) collective-permute-start(bf16[112,768]{1,0:T(8,128)(2,1)S(1)} %constant_dynamic-update-slice_fusion), channel_id=1, source_target_pairs={{0,16},{4,20},{8,24},{12,28},{16,0},{20,4},{24,8},{28,12},{1,17},{... | collective-permute-start | bytes 516104 | tf_op jit(solution)/shard_map/ppermute | solution.py:467
  19.3 7.6 %collective-permute-start.5 = (bf16[112,768]{1,0:T(8,128)(2,1)S(1)}, bf16[112,768]{1,0:T(8,128)(2,1)S(1)}, u32[]{:S(2)}, u32[]{:S(2)}) collective-permute-start(bf16[112,768]{1,0:T(8,128)(2,1)S(1)} %constant_dynamic-update-slice_fusion), channel_id=1, source_target_pairs={{0,24},{4,28},{8,16},{12,20},{16,8},{20,12},{24,0},{28,4},{1,25},{... | collective-permute-start | bytes 516104 | tf_op jit(solution)/shard_map/ppermute | solution.py:467
  19.8 5.1 %collective-permute-start.2 = (bf16[96,768]{1,0:T(8,128)(2,1)S(1)}, bf16[96,768]{1,0:T(8,128)(2,1)S(1)}, u32[]{:S(2)}, u32[]{:S(2)}) collective-permute-start(bf16[96,768]{1,0:T(8,128)(2,1)S(1)} %collective-permute-done.1), channel_id=1, source_target_pairs={{0,1},{1,0},{2,3},{3,2},{4,5},{5,4},{6,7},{7,6},{8,9},{9,8},{10,11... | collective-permute-start | bytes 442376 | tf_op jit(solution)/shard_map/ppermute | solution.py:470
  29.4 5.2 %collective-permute-start.11 = (bf16[72,192]{1,0:T(8,128)(2,1)S(1)}, bf16[72,192]{1,0:T(8,128)(2,1)S(1)}, u32[]{:S(2)}, u32[]{:S(2)}) collective-permute-start(bf16[72,192]{1,0:T(8,128)(2,1)S(1)} %fusion.2.refs_3_), channel_id=1, source_target_pairs={{0,2},{1,3},{2,0},{3,1},{4,6},{5,7},{6,4},{7,5},{8,10},{9,11},{10,... | collective-permute-start | bytes 82952 | tf_op jit(solution)/shard_map/ppermute | solution.py:470
  29.8 14.6 %collective-permute-start.6 = (bf16[192,768]{1,0:T(8,128)(2,1)S(1)}, bf16[192,768]{1,0:T(8,128)(2,1)S(1)}, u32[]{:S(2)}, u32[]{:S(2)}) collective-permute-start(bf16[192,768]{1,0:T(8,128)(2,1)S(1)} %constant_dynamic-update-slice_fusion.2), channel_id=1, source_target_pairs={{0,8},{4,12},{8,0},{12,4},{16,24},{20,28},{24,16},{28,20},{1,9},{5... | collective-permute-start | bytes 884744 | tf_op jit(solution)/shard_map/ppermute | solution.py:467
  31.0 13.4 %collective-permute-start.7 = (bf16[192,768]{1,0:T(8,128)(2,1)S(1)}, bf16[192,768]{1,0:T(8,128)(2,1)S(1)}, u32[]{:S(2)}, u32[]{:S(2)}) collective-permute-start(bf16[192,768]{1,0:T(8,128)(2,1)S(1)} %constant_dynamic-update-slice_fusion.2), channel_id=1, source_target_pairs={{0,16},{4,20},{8,24},{12,28},{16,0},{20,4},{24,8},{28,12},{1,17},{... | collective-permute-start | bytes 884744 | tf_op jit(solution)/shard_map/ppermute | solution.py:467
  31.8 14.0 %collective-permute-start.8 = (bf16[192,768]{1,0:T(8,128)(2,1)S(1)}, bf16[192,768]{1,0:T(8,128)(2,1)S(1)}, u32[]{:S(2)}, u32[]{:S(2)}) collective-permute-start(bf16[192,768]{1,0:T(8,128)(2,1)S(1)} %constant_dynamic-update-slice_fusion.2), channel_id=1, source_target_pairs={{0,24},{4,28},{8,16},{12,20},{16,8},{20,12},{24,0},{28,4},{1,25},{... | collective-permute-start | bytes 884744 | tf_op jit(solution)/shard_map/ppermute | solution.py:467
  33.4 12.4 %collective-permute-start.10 = (bf16[72,192]{1,0:T(8,128)(2,1)S(1)}, bf16[72,192]{1,0:T(8,128)(2,1)S(1)}, u32[]{:S(2)}, u32[]{:S(2)}) collective-permute-start(bf16[72,192]{1,0:T(8,128)(2,1)S(1)} %fusion.2.refs_3_), channel_id=1, source_target_pairs={{0,1},{1,0},{2,3},{3,2},{4,5},{5,4},{6,7},{7,6},{8,9},{9,8},{10,11... | collective-permute-start | bytes 82952 | tf_op jit(solution)/shard_map/ppermute | solution.py:470
  34.6 11.2 %collective-permute-start.12 = (bf16[72,192]{1,0:T(8,128)(2,1)S(1)}, bf16[72,192]{1,0:T(8,128)(2,1)S(1)}, u32[]{:S(2)}, u32[]{:S(2)}) collective-permute-start(bf16[72,192]{1,0:T(8,128)(2,1)S(1)} %collective-permute-done.11.refs_5_), channel_id=1, source_target_pairs={{0,1},{1,0},{2,3},{3,2},{4,5},{5,4},{6,7},{7,6},{8,9},{9,8},{10,11... | collective-permute-start | bytes 82952 | tf_op jit(solution)/shard_map/ppermute | solution.py:470
  64.0 16.1 %collective-permute-start.14 = (bf16[2,2,2,32,768]{4,3,2,1,0:T(8,128)(2,1)S(1)}, bf16[2,2,2,32,768]{4,3,2,1,0:T(8,128)(2,1)S(1)}, u32[]{:S(2)}, u32[]{:S(2)}) collective-permute-start(bf16[2,2,2,32,768]{4,3,2,1,0:T(8,128)(2,1)S(1)} %get-tuple-element.122), channel_id=1, source_target_pairs={{0,8},{4,12},{8,0},{12,4},{16,24},{20,28},{24,16},{28,20},{1,9},{5... | collective-permute-start | bytes 1179656 | tf_op jit(solution)/shard_map/ppermute | solution.py:467
  65.0 19.3 %collective-permute-start.15 = (bf16[2,2,2,32,768]{4,3,2,1,0:T(8,128)(2,1)S(1)}, bf16[2,2,2,32,768]{4,3,2,1,0:T(8,128)(2,1)S(1)}, u32[]{:S(2)}, u32[]{:S(2)}) collective-permute-start(bf16[2,2,2,32,768]{4,3,2,1,0:T(8,128)(2,1)S(1)} %get-tuple-element.123), channel_id=1, source_target_pairs={{0,16},{4,20},{8,24},{12,28},{16,0},{20,4},{24,8},{28,12},{1,17},{... | collective-permute-start | bytes 1179656 | tf_op jit(solution)/shard_map/ppermute | solution.py:467
  66.4 17.9 %collective-permute-start.16 = (bf16[2,2,2,32,768]{4,3,2,1,0:T(8,128)(2,1)S(1)}, bf16[2,2,2,32,768]{4,3,2,1,0:T(8,128)(2,1)S(1)}, u32[]{:S(2)}, u32[]{:S(2)}) collective-permute-start(bf16[2,2,2,32,768]{4,3,2,1,0:T(8,128)(2,1)S(1)} %get-tuple-element.124), channel_id=1, source_target_pairs={{0,24},{4,28},{8,16},{12,20},{16,8},{20,12},{24,0},{28,4},{1,25},{... | collective-permute-start | bytes 1179656 | tf_op jit(solution)/shard_map/ppermute | solution.py:467
  84.6 12.0 %collective-permute-start.17 = (bf16[2,2,2,32,768]{4,3,2,1,0:T(8,128)(2,1)S(1)}, bf16[2,2,2,32,768]{4,3,2,1,0:T(8,128)(2,1)S(1)}, u32[]{:S(2)}, u32[]{:S(2)}) collective-permute-start(bf16[2,2,2,32,768]{4,3,2,1,0:T(8,128)(2,1)S(1)} %get-tuple-element.130), channel_id=1, source_target_pairs={{0,8},{4,12},{8,0},{12,4},{16,24},{20,28},{24,16},{28,20},{1,9},{5... | collective-permute-start | bytes 1179656 | tf_op jit(solution)/shard_map/ppermute | solution.py:467
  85.8 11.6 %collective-permute-start.18 = (bf16[2,2,2,32,768]{4,3,2,1,0:T(8,128)(2,1)S(1)}, bf16[2,2,2,32,768]{4,3,2,1,0:T(8,128)(2,1)S(1)}, u32[]{:S(2)}, u32[]{:S(2)}) collective-permute-start(bf16[2,2,2,32,768]{4,3,2,1,0:T(8,128)(2,1)S(1)} %get-tuple-element.131), channel_id=1, source_target_pairs={{0,16},{4,20},{8,24},{12,28},{16,0},{20,4},{24,8},{28,12},{1,17},{... | collective-permute-start | bytes 1179656 | tf_op jit(solution)/shard_map/ppermute | solution.py:467
  86.6 18.8 %collective-permute-start.19 = (bf16[2,2,2,32,768]{4,3,2,1,0:T(8,128)(2,1)S(1)}, bf16[2,2,2,32,768]{4,3,2,1,0:T(8,128)(2,1)S(1)}, u32[]{:S(2)}, u32[]{:S(2)}) collective-permute-start(bf16[2,2,2,32,768]{4,3,2,1,0:T(8,128)(2,1)S(1)} %get-tuple-element.132), channel_id=1, source_target_pairs={{0,24},{4,28},{8,16},{12,20},{16,8},{20,12},{24,0},{28,4},{1,25},{... | collective-permute-start | bytes 1179656 | tf_op jit(solution)/shard_map/ppermute | solution.py:467
  91.0 14.9 %collective-permute-start.21 = (bf16[256,768]{1,0:T(8,128)(2,1)S(1)}, bf16[256,768]{1,0:T(8,128)(2,1)S(1)}, u32[]{:S(2)}, u32[]{:S(2)}) collective-permute-start(bf16[256,768]{1,0:T(8,128)(2,1)S(1)} %get-tuple-element.137), channel_id=1, source_target_pairs={{0,1},{1,0},{2,3},{3,2},{4,5},{5,4},{6,7},{7,6},{8,9},{9,8},{10,11... | collective-permute-start | bytes 1179656 | tf_op jit(solution)/shard_map/ppermute | solution.py:470
  94.5 11.4 %collective-permute-start.22 = (bf16[128,768]{1,0:T(8,128)(2,1)S(1)}, bf16[128,768]{1,0:T(8,128)(2,1)S(1)}, u32[]{:S(2)}, u32[]{:S(2)}) collective-permute-start(bf16[128,768]{1,0:T(8,128)(2,1)S(1)} %get-tuple-element.176), channel_id=1, source_target_pairs={{0,1},{1,0},{2,3},{3,2},{4,5},{5,4},{6,7},{7,6},{8,9},{9,8},{10,11... | collective-permute-start | bytes 589832 | tf_op jit(solution)/shard_map/ppermute | solution.py:470
  106.1 8.2 %collective-permute-start.26 = (bf16[128,768]{1,0:T(8,128)(2,1)S(1)}, bf16[128,768]{1,0:T(8,128)(2,1)S(1)}, u32[]{:S(2)}, u32[]{:S(2)}) collective-permute-start(bf16[128,768]{1,0:T(8,128)(2,1)S(1)} %get-tuple-element.175), channel_id=1, source_target_pairs={{0,1},{1,0},{2,3},{3,2},{4,5},{5,4},{6,7},{7,6},{8,9},{9,8},{10,11... | collective-permute-start | bytes 589832 | tf_op jit(solution)/shard_map/ppermute | solution.py:470
  111.3 21.5 %collective-permute-start.24 = (bf16[256,768]{1,0:T(8,128)(2,1)S(1)}, bf16[256,768]{1,0:T(8,128)(2,1)S(1)}, u32[]{:S(2)}, u32[]{:S(2)}) collective-permute-start(bf16[256,768]{1,0:T(8,128)(2,1)S(1)} %get-tuple-element.148), channel_id=1, source_target_pairs={{0,1},{1,0},{2,3},{3,2},{4,5},{5,4},{6,7},{7,6},{8,9},{9,8},{10,11... | collective-permute-start | bytes 1179656 | tf_op jit(solution)/shard_map/ppermute | solution.py:470
  112.0 20.8 %collective-permute-start.25 = (bf16[256,768]{1,0:T(8,128)(2,1)S(1)}, bf16[256,768]{1,0:T(8,128)(2,1)S(1)}, u32[]{:S(2)}, u32[]{:S(2)}) collective-permute-start(bf16[256,768]{1,0:T(8,128)(2,1)S(1)} %get-tuple-element.149), channel_id=1, source_target_pairs={{0,2},{1,3},{2,0},{3,1},{4,6},{5,7},{6,4},{7,5},{8,10},{9,11},{10,... | collective-permute-start | bytes 1179656 | tf_op jit(solution)/shard_map/ppermute | solution.py:470
  117.3 30.5 %collective-permute-start.30 = (bf16[256,768]{1,0:T(8,128)(2,1)S(1)}, bf16[256,768]{1,0:T(8,128)(2,1)S(1)}, u32[]{:S(2)}, u32[]{:S(2)}) collective-permute-start(bf16[256,768]{1,0:T(8,128)(2,1)S(1)} %get-tuple-element.152), channel_id=1, source_target_pairs={{0,1},{1,0},{2,3},{3,2},{4,5},{5,4},{6,7},{7,6},{8,9},{9,8},{10,11... | collective-permute-start | bytes 1179656 | tf_op jit(solution)/shard_map/ppermute | solution.py:470
  118.9 28.9 %collective-permute-start.31 = (bf16[256,768]{1,0:T(8,128)(2,1)S(1)}, bf16[256,768]{1,0:T(8,128)(2,1)S(1)}, u32[]{:S(2)}, u32[]{:S(2)}) collective-permute-start(bf16[256,768]{1,0:T(8,128)(2,1)S(1)} %get-tuple-element.160), channel_id=1, source_target_pairs={{0,2},{1,3},{2,0},{3,1},{4,6},{5,7},{6,4},{7,5},{8,10},{9,11},{10,... | collective-permute-start | bytes 1179656 | tf_op jit(solution)/shard_map/ppermute | solution.py:470
  133.5 14.3 %collective-permute-start.27 = (bf16[2,64,768]{2,1,0:T(8,128)(2,1)S(1)}, bf16[2,64,768]{2,1,0:T(8,128)(2,1)S(1)}, u32[]{:S(2)}, u32[]{:S(2)}) collective-permute-start(bf16[2,64,768]{2,1,0:T(8,128)(2,1)S(1)} %get-tuple-element.157), channel_id=1, source_target_pairs={{0,8},{4,12},{8,0},{12,4},{16,24},{20,28},{24,16},{28,20},{1,9},{5... | collective-permute-start | bytes 589832 | tf_op jit(solution)/shard_map/ppermute | solution.py:467
  134.9 12.9 %collective-permute-start.28 = (bf16[2,64,768]{2,1,0:T(8,128)(2,1)S(1)}, bf16[2,64,768]{2,1,0:T(8,128)(2,1)S(1)}, u32[]{:S(2)}, u32[]{:S(2)}) collective-permute-start(bf16[2,64,768]{2,1,0:T(8,128)(2,1)S(1)} %get-tuple-element.158), channel_id=1, source_target_pairs={{0,16},{4,20},{8,24},{12,28},{16,0},{20,4},{24,8},{28,12},{1,17},{... | collective-permute-start | bytes 589832 | tf_op jit(solution)/shard_map/ppermute | solution.py:467
  135.8 12.0 %collective-permute-start.29 = (bf16[2,64,768]{2,1,0:T(8,128)(2,1)S(1)}, bf16[2,64,768]{2,1,0:T(8,128)(2,1)S(1)}, u32[]{:S(2)}, u32[]{:S(2)}) collective-permute-start(bf16[2,64,768]{2,1,0:T(8,128)(2,1)S(1)} %get-tuple-element.159), channel_id=1, source_target_pairs={{0,24},{4,28},{8,16},{12,20},{16,8},{20,12},{24,0},{28,4},{1,25},{... | collective-permute-start | bytes 589832 | tf_op jit(solution)/shard_map/ppermute | solution.py:467
  147.9 4.3 %collective-permute-start.32 = (bf16[4,64,768]{2,1,0:T(8,128)(2,1)S(1)}, bf16[4,64,768]{2,1,0:T(8,128)(2,1)S(1)}, u32[]{:S(2)}, u32[]{:S(2)}) collective-permute-start(bf16[4,64,768]{2,1,0:T(8,128)(2,1)S(1)} %pad_maximum_fusion.5), channel_id=1, source_target_pairs={{0,4},{4,0},{8,12},{12,8},{16,20},{20,16},{24,28},{28,24},{1,5},{5... | collective-permute-start | bytes 1179656 | tf_op jit(solution)/shard_map/ppermute | solution.py:467
  148.7 7.8 %collective-permute-start.33 = (bf16[2,64,768]{2,1,0:T(8,128)(2,1)S(1)}, bf16[2,64,768]{2,1,0:T(8,128)(2,1)S(1)}, u32[]{:S(2)}, u32[]{:S(2)}) collective-permute-start(bf16[2,64,768]{2,1,0:T(8,128)(2,1)S(1)} %get-tuple-element.168), channel_id=1, source_target_pairs={{0,8},{4,12},{8,0},{12,4},{16,24},{20,28},{24,16},{28,20},{1,9},{5... | collective-permute-start | bytes 589832 | tf_op jit(solution)/shard_map/ppermute | solution.py:467
  149.8 7.4 %collective-permute-start.34 = (bf16[2,64,768]{2,1,0:T(8,128)(2,1)S(1)}, bf16[2,64,768]{2,1,0:T(8,128)(2,1)S(1)}, u32[]{:S(2)}, u32[]{:S(2)}) collective-permute-start(bf16[2,64,768]{2,1,0:T(8,128)(2,1)S(1)} %get-tuple-element.169), channel_id=1, source_target_pairs={{0,16},{4,20},{8,24},{12,28},{16,0},{20,4},{24,8},{28,12},{1,17},{... | collective-permute-start | bytes 589832 | tf_op jit(solution)/shard_map/ppermute | solution.py:467
  150.7 10.4 %collective-permute-start.35 = (bf16[2,64,768]{2,1,0:T(8,128)(2,1)S(1)}, bf16[2,64,768]{2,1,0:T(8,128)(2,1)S(1)}, u32[]{:S(2)}, u32[]{:S(2)}) collective-permute-start(bf16[2,64,768]{2,1,0:T(8,128)(2,1)S(1)} %get-tuple-element.170), channel_id=1, source_target_pairs={{0,24},{4,28},{8,16},{12,20},{16,8},{20,12},{24,0},{28,4},{1,25},{... | collective-permute-start | bytes 589832 | tf_op jit(solution)/shard_map/ppermute | solution.py:467
  (13 other events, 153.9 us)
